TPU v7x, 256 devices: a whole 4x4x8 slice. The times are simulated.
256 devices in a mesh: dp: 64 (over y, z, core), mp: 4 (over x).
Axes of the slice: x: 4, y: 4, z: 8, core: 2. Of those that a mesh axis runs over, the one named last changes fastest.
Arguments:
- grads: bfloat16 [64, 256, 12288], P('dp', 'mp'), may hold values from -5 to 5
- master: float32 [256, 12288], P('mp', 'dp'), may hold values from -3 to 3
- moment: float32 [256, 12288], P('mp', 'dp'), may hold values from -0.6 to 0.6
- second: float32 [256, 12288], P('mp', 'dp'), may hold values from 0.003 to 0.3
- inputs: bfloat16 [32768, 12288], P(('dp', 'mp')), may hold values from -6 to 6
- out_grads: bfloat16 [32768, 1024], P('dp', 'mp'), may hold values from -0.26367188 to 0.26367188
Outputs:
- weights: bfloat16 [256, 12288], P('mp')
- new_master: float32 [256, 12288], P('mp', 'dp')
- new_moment: float32 [256, 12288], P('mp', 'dp')
- new_second: float32 [256, 12288], P('mp', 'dp')
- next_grads: bfloat16 [64, 1024, 12288], P('dp', 'mp')
All inputs are finite; a program needn't handle non-finite values.
Results may differ from a plain program's by a relative error of at most 0.001.
Values may be sent and summed in bfloat16 or wider, within the bound.
No kernel may reach another device: no remote copies, remote signals or barrier semaphores. Data moves between devices by JAX's collectives and lax.ppermute only.
A program may use at most 128 MiB of HBM per device.

v0:
```python
import jax
import jax.numpy as jnp
from jax import lax
from jax.sharding import PartitionSpec as P

STEP = 10


beta_one = 0.9
beta_two = 0.95
learn_rate = 0.05
decay_rate = 0.1
adam_eps = 1e-08


def per_device(grads, master, moment, second, inputs, out_grads):
    total = lax.psum_scatter(grads[0].astype(jnp.float32), "dp", scatter_dimension=1, tiled=True)
    new_moment = beta_one * moment + (1.0 - beta_one) * total
    new_second = beta_two * second + (1.0 - beta_two) * total * total
    first_hat = new_moment / (1.0 - beta_one**STEP)
    second_hat = new_second / (1.0 - beta_two**STEP)
    new_master = master - learn_rate * (
        first_hat / (jnp.sqrt(second_hat) + adam_eps) + decay_rate * master
    )
    weights = lax.all_gather(new_master.astype(jnp.bfloat16), "dp", axis=1, tiled=True)
    summed = lax.dot_general(
        out_grads,
        lax.all_gather(inputs, "mp", axis=0, tiled=True),
        (((0,), (0,)), ((), ())),
        preferred_element_type=jnp.float32,
    )
    next_grads = summed.astype(jnp.bfloat16)[None]
    return (weights, new_master, new_moment, new_second, next_grads)


def solution(mesh):
    return jax.shard_map(
        per_device,
        mesh=mesh,
        in_specs=(
            P("dp", "mp", None),
            P("mp", "dp"),
            P("mp", "dp"),
            P("mp", "dp"),
            P(("dp", "mp"), None),
            P("dp", "mp"),
        ),
        out_specs=(P("mp", None), P("mp", "dp"), P("mp", "dp"), P("mp", "dp"), P("dp", "mp", None)),
        check_vma=False,
    )
```

profile of v0, /device:TPU:8, one launch (start us, length us, event | category | flops | bytes accessed | tf_op | source)
XLA Modules:
  0.0 380.5 jit_solution(10099056791897781706)
XLA Ops:
  7.2 0.0 copy-start
  7.2 0.0 reduce-scatter.4.cloned.1.call-start
  7.2 1.6 bitcast_convert_fusion
  8.9 0.0 copy-start.1
  8.9 0.0 copy-start.2
  8.9 4.0 %copy.13 = f32[64,12288]{0,1:T(8,128)} copy(f32[64,12288]{1,0:T(8,128)S(1)} %bitcast_convert_fusion) | data formatting | bytes 6291456
  12.9 0.0 copy-start.3
  12.9 0.0 reduce-scatter.4.cloned.1.call-update
  12.9 0.0 all-gather.6.cloned.1.call-start
  13.0 149.9 %reduce-scatter.4.cloned.1.call-done = f32[192,64]{1,0:T(8,128)} async-done(((f32[12288,64]{1,0:T(8,128)}), f32[192,64]{1,0:T(8,128)}) %reduce-scatter.4.cloned.1.call-update) | async-done | bytes 49168
  162.9 1.0 copy.14
  163.9 0.0 copy-done.1
  163.9 0.0 copy-done.2
  163.9 0.0 copy-done.3
  163.9 0.7 convert_bitcast_fusion
  164.6 0.0 all-gather.6.cloned.1.call-update
  164.7 0.0 all-gather.4.cloned.1.call-start
  164.7 0.7 all-gather.4.cloned.1.call-update
  165.4 76.7 %all-gather.6.cloned.1.call-done = bf16[64,192,64]{1,2,0:T(8,128)(2,1)} async-done(((bf16[1,192,64]{1,2,0:T(8,128)(2,1)}), bf16[64,192,64]{1,2,0:T(8,128)(2,1)}) %all-gather.6.cloned.1.call-update) | async-done | bytes 1572880 | tf_op jit(solution)/shard_map/all_gather | solution.py:25
  242.1 2.8 copy.12
  244.9 3.2 reshape.14
  248.1 115.8 %all-gather.4.cloned.1.call-done = bf16[512,12288]{1,0:T(8,128)(2,1)} async-done(((bf16[128,12288]{1,0:T(8,128)(2,1)}), bf16[512,12288]{1,0:T(8,128)(2,1)}) %all-gather.4.cloned.1.call-update) | async-done | bytes 12582928 | tf_op jit(solution)/shard_map/all_gather | solution.py:28
  363.9 0.0 copy-done
  363.9 10.0 %fusion = bf16[1,256,12288]{2,1,0:T(8,128)(2,1)} fusion(bf16[512,256]{1,0:T(8,128)(2,1)S(1)} %copy-done, bf16[512,12288]{1,0:T(8,128)(2,1)} %all-gather.4.cloned.1.call-done), kind=kOutput, calls=%fused_computation.1 | convolution fusion | flops 3224371200 | bytes 19136512 | tf_op jit(solution)/shard_map/dot_general | solution.py:26
Async XLA Ops:
  7.2 356.8 %copy-start = (bf16[512,256]{1,0:T(8,128)(2,1)S(1)}, bf16[512,256]{1,0:T(8,128)(2,1)}, u32[]{:S(2)}) copy-start(bf16[512,256]{1,0:T(8,128)(2,1)} %param.11) | copy-start | bytes 786436
  7.2 155.8 %reduce-scatter.4.cloned.1.call-start = ((), (), s32[]{:S(2)}) async-start(), calls=%async_computation.3 | async-start | bytes 6389760
  8.9 155.0 %copy-start.1 = (f32[64,192]{1,0:T(8,128)S(1)}, f32[64,192]{1,0:T(8,128)}, u32[]{:S(2)}) copy-start(f32[64,192]{1,0:T(8,128)} %param.7) | copy-start | bytes 147460
  8.9 155.0 %copy-start.2 = (f32[64,192]{1,0:T(8,128)S(1)}, f32[64,192]{1,0:T(8,128)}, u32[]{:S(2)}) copy-start(f32[64,192]{1,0:T(8,128)} %param.8) | copy-start | bytes 147460
  12.9 151.0 %copy-start.3 = (f32[64,192]{1,0:T(8,128)S(1)}, f32[64,192]{1,0:T(8,128)}, u32[]{:S(2)}) copy-start(f32[64,192]{1,0:T(8,128)} %param.9) | copy-start | bytes 147460
  12.9 229.2 %all-gather.6.cloned.1.call-start = ((), (), s32[]{:S(2)}) async-start(), calls=%async_computation.2 | async-start | bytes 2129920 | tf_op jit(solution)/shard_map/all_gather | solution.py:25
  164.7 199.3 %all-gather.4.cloned.1.call-start = ((), (), s32[]{:S(2)}) async-start(), calls=%async_computation.1 | async-start | bytes 15728640 | tf_op jit(solution)/shard_map/all_gather | solution.py:28
Sparse Core Ops, SparseCore 0:
  13.1 149.8 reduce-scatter.3
  166.7 75.4 all-gather.5
  244.1 119.7 all-gather.3
where the time goes:
time: 382 us; the launch traced here: 380 us
  waiting for transfers between devices  343 us (90%)
  between operations  13.8 us (4%)
  local copies, waits for them, and re-layouts  11 us (3%)
  matrix products  9.99 us (3%)
    unnamed x4, waiting for transfers between devices  151 us
    all_gather x1, waiting for transfers between devices, per_device(): lax.all_gather(inputs, 'mp', axis=0, tiled=True)  116 us
    all_gather x1, waiting for transfers between devices, per_device(): lax.all_gather(new_master.astype(jnp.bfloat16), 'dp', axis=1, tiled=True)  76.7 us
    dot_general x1, matrix products, per_device(): lax.dot_general(out_grads, lax.all_gather(inputs, 'mp', axis=0, tiled=Tru...  9.99 us
    unnamed x11, local copies, waits for them, and re-layouts  8.19 us
  transfers between devices with their start and end apart: 3, of which 3 were waited for; matrix products, arithmetic and copies ran while one was open for 2% of the time, Pallas kernels for 0%

commit v1 on v0

v1 whole, which is shorter than its diff:
```python
import functools

import jax
import jax.numpy as jnp
from jax import lax
from jax.experimental import pallas as pl
from jax.experimental.pallas import tpu as pltpu
from jax.sharding import PartitionSpec as P

STEP = 10

beta_one = 0.9
beta_two = 0.95
learn_rate = 0.05
decay_rate = 0.1
adam_eps = 1e-08

NY, NZ, NC, NX = 4, 8, 2, 4
D = 12288
BLOCK = 1024
PIECES = ((0, 4096), (6144, 4096), (4096, 2048), (10240, 2048))


def dp_shift(dy, dz, dc):
    pairs = []
    for y in range(NY):
        for z in range(NZ):
            for c in range(NC):
                target = (((y + dy) % NY) * NZ + (z + dz) % NZ) * NC + (c + dc) % NC
                pairs.append(((y * NZ + z) * NC + c, target))
    return pairs


def to_core(array):
    return lax.ppermute(array, "dp", dp_shift(0, 0, 1))


def to_x(array, step):
    return lax.ppermute(array, "mp", [(i, (i + step) % NX) for i in range(NX)])


def columns(array, index, width):
    return lax.dynamic_slice_in_dim(array, index * width, width, axis=1)


def product_kernel(lhs, own, after, opposite, before, *rest):
    out = rest[-1]
    tokens = jnp.concatenate([own[...], after[...], opposite[...], before[...]], axis=0)
    out[0] = jnp.dot(lhs[...], tokens, preferred_element_type=jnp.float32).astype(jnp.bfloat16)


def product(piece, lhs, own, after, opposite, before, carry):
    start, width = PIECES[piece]
    skip = start // BLOCK
    whole = pl.BlockSpec((128, BLOCK), lambda i: (0, skip + i))
    alone = pl.BlockSpec((128, BLOCK), lambda i: (0, i))
    specs = [pl.BlockSpec((256, 512), lambda i: (0, 0)), whole, whole, alone, whole]
    operands = [lhs, own, after, opposite, before]
    aliases = {}
    if carry is not None:
        specs.append(pl.BlockSpec(memory_space=pl.ANY))
        operands.append(carry)
        aliases = {5: 0}
    return pl.pallas_call(
        product_kernel,
        grid=(width // BLOCK,),
        in_specs=specs,
        out_specs=pl.BlockSpec((1, 256, BLOCK), lambda i: (0, 0, skip + i)),
        out_shape=jax.ShapeDtypeStruct((1, 256, D), jnp.bfloat16),
        input_output_aliases=aliases,
        cost_estimate=pl.CostEstimate(flops=2 * 256 * 512 * width, bytes_accessed=1536 * width, transcendentals=0),
        compiler_params=pltpu.CompilerParams(vmem_limit_bytes=24 * 1024 * 1024),
    )(*operands)


def after_that(array, *events):
    return lax.optimization_barrier((array, *events))[0]


def exchange(sends, moves):
    return [lax.ppermute(array, "dp", dp_shift(*move)) for array, move in zip(sends, moves, strict=True)]


def swap_z(array):
    pairs = [(i, i ^ NC) for i in range(NY * NZ * NC)]
    return lax.ppermute(array, "dp", pairs)


VMEM = pl.BlockSpec(memory_space=pltpu.VMEM)
SMEM = pl.BlockSpec(memory_space=pltpu.SMEM)


def local(body, place, operands, shapes):
    return pl.pallas_call(
        body,
        in_specs=[SMEM] + [VMEM] * len(operands),
        out_specs=[VMEM] * len(shapes),
        out_shape=[jax.ShapeDtypeStruct(shape, dtype) for shape, dtype in shapes],
        compiler_params=pltpu.CompilerParams(vmem_limit_bytes=16 * 1024 * 1024),
    )(place, *operands)


def at(block, width):
    return pl.ds(pl.multiple_of(block * width, 128), width)


def half(core):
    return pl.ds(pl.multiple_of(core * 32, 32), 32)


def add_cores(place, grad, theirs, *outs):
    core, y = place[0], place[1]
    for k, out in enumerate(outs):
        piece = at(lax.rem(y + k, NY), 3072)
        out[...] = grad[0, half(core), piece].astype(jnp.float32) + theirs[:, piece].astype(jnp.float32)


def add_y(place, a, b, c, d, kept, sent):
    low = place[4]
    for q in range(4):
        for out, bit in ((kept, low), (sent, 1 - low)):
            piece = at(2 * q + bit, 384)
            out[:, q * 384 : (q + 1) * 384] = (a[:, piece] + b[:, piece]) + (c[:, piece] + d[:, piece])


def add_pair(place, a, b, *outs):
    q = place[3]
    for k, out in enumerate(outs):
        piece = at(lax.rem(q + k, 4), 384)
        out[...] = a[:, piece] + b[:, piece]


def adam(place, a, b, c, d, state, new_state, weights):
    total = (a[...] + b[...]) + (c[...] + d[...])
    new_moment = beta_one * state[1] + (1.0 - beta_one) * total
    new_second = beta_two * state[2] + (1.0 - beta_two) * total * total
    first_hat = new_moment / (1.0 - beta_one**STEP)
    second_hat = new_second / (1.0 - beta_two**STEP)
    new_master = state[0] - learn_rate * (first_hat / (jnp.sqrt(second_hat) + adam_eps) + decay_rate * state[0])
    new_state[0] = new_master
    new_state[1] = new_moment
    new_state[2] = new_second
    weights[...] = new_master.astype(jnp.bfloat16)


def join_ring(place, *refs):
    *parts, out = refs
    width = parts[0].shape[1]
    here = place[3] if width == 384 else place[1]
    for k, part in enumerate(parts):
        out[:, at(lax.rem(here + 4 - k, 4), width)] = part[...]


def join_pair(place, mine, other, out):
    low = place[4]
    for q in range(4):
        piece = slice(q * 384, (q + 1) * 384)
        out[:, at(2 * q + low, 384)] = mine[:, piece]
        out[:, at(2 * q + 1 - low, 384)] = other[:, piece]


def join_cores(place, mine, other, out):
    core = place[0]
    out[half(core), :] = mine[...]
    out[half(1 - core), :] = other[...]


def per_device(grads, master, moment, second, inputs, out_grads):
    index = lax.axis_index("dp")
    x = lax.axis_index("mp")
    core = index % NC
    z = (index // NC) % NZ
    y = index // (NC * NZ)
    first = core == 0
    place = jnp.stack([core, y, z, z // 2, z % 2]).astype(jnp.int32)
    f32, bf16 = jnp.float32, jnp.bfloat16

    before = to_x(inputs, 1)
    after = to_x(inputs, -1)
    lhs = lax.dynamic_slice_in_dim(jnp.concatenate([out_grads, out_grads]), x * 128, 512, axis=0).T

    theirs = to_core(lax.dynamic_slice_in_dim(grads[0], (1 - core) * 32, 32, axis=0))

    state = jnp.stack([master, moment, second])
    kept = lax.dynamic_slice_in_dim(state, core * 32, 32, axis=1)
    got = to_core(after_that(lax.dynamic_slice_in_dim(state, (1 - core) * 32, 32, axis=1), theirs))
    state = jnp.concatenate([jnp.where(first, kept, got), jnp.where(first, got, kept)], axis=2)

    kept, *sent = local(add_cores, place, (grads, theirs), [((32, 3072), f32)] * 4)
    got = exchange(sent, [(k, 0, 0) for k in (1, 2, 3)])
    kept, sent = local(add_y, place, (kept, *got), [((32, 1536), f32)] * 2)
    got = swap_z(sent)
    kept, *sent = local(add_pair, place, (kept, got), [((32, 384), f32)] * 4)
    got = exchange(sent, [(0, 2 * k, 0) for k in (1, 2, 3)])
    state, own = local(adam, place, (kept, *got, state), [((3, 32, 384), f32), ((32, 384), bf16)])

    got = exchange([own] * 3, [(0, 2 * k, 0) for k in (1, 2, 3)])
    (own,) = local(join_ring, place, (own, *got), [((32, 1536), bf16)])
    got = swap_z(own)
    (own,) = local(join_pair, place, (own, got), [((32, 3072), bf16)])
    before, after, own = lax.optimization_barrier((before, after, own))
    opposites = []
    for piece, (start, width) in enumerate(PIECES):
        near, way = ((before, 1), (after, -1))[piece % 2]
        near = near[:, start : start + width]
        if piece >= 2:
            near = after_that(near, opposites[piece - 2])
        opposites.append(to_x(near, way))

    got = exchange([own] * 3, [(k, 0, 0) for k in (1, 2, 3)])
    (own,) = local(join_ring, place, (own, *got), [((32, D), bf16)])

    other = to_core(own)
    (weights,) = local(join_cores, place, (own, other), [((64, D), bf16)])

    left, right = state[:, :, :192], state[:, :, 192:]
    kept = jnp.where(first, left, right)
    got = to_core(after_that(jnp.where(first, right, left), other))
    state = jnp.concatenate([jnp.where(first, kept, got), jnp.where(first, got, kept)], axis=1)

    lhs, weights, state = lax.optimization_barrier((lhs, weights, state))
    carry = None
    for piece in range(4):
        carry = product(piece, lhs, inputs, after, opposites[piece], before, carry)

    return (weights, state[0], state[1], state[2], carry)


def solution(mesh):
    return jax.shard_map(
        per_device,
        mesh=mesh,
        in_specs=(
            P("dp", "mp", None),
            P("mp", "dp"),
            P("mp", "dp"),
            P("mp", "dp"),
            P(("dp", "mp"), None),
            P("dp", "mp"),
        ),
        out_specs=(P("mp", None), P("mp", "dp"), P("mp", "dp"), P("mp", "dp"), P("dp", "mp", None)),
        check_vma=False,
    )
```

time: 382 us -> 127 us (0.33)
  waiting for transfers between devices: 343 us -> 46.9 us
  starting transfers between devices: 0.12 us -> 38 us
  Pallas kernels: 0 us -> 24.4 us
  between operations: 13.8 us -> 0.8 us
  matrix products: 9.99 us -> 0 us
    all_gather x2 -> x0, waiting for transfers between devices: 193 us -> none  [the longest x1 116 us: per_device(): lax.all_gather(inputs, 'mp', axis=0, tiled=True)]
    unnamed x4 -> x0, waiting for transfers between devices: 151 us -> none
    ppermute x0 -> x24, waiting for transfers between devices: none -> 46.9 us  [the longest x12 24.5 us: exchange(): lax.ppermute(array, 'dp', dp_shift(*move))]
    ppermute x0 -> x24, starting transfers between devices: none -> 38 us  [the longest x12 25.9 us: exchange(): lax.ppermute(array, 'dp', dp_shift(*move))]
    pallas_call x0 -> x12, Pallas kernels: none -> 24.4 us  [the longest x4 14.7 us: product(): pl.pallas_call(product_kernel, grid=(width // BLOCK,), in_specs=specs, ou...]
    dot_general x1 -> x0, matrix products: 9.99 us -> none  [per_device(): lax.dot_general(out_grads, lax.all_gather(inputs, 'mp', axis=0, tiled=Tru...]
    slice x0 -> x4, local copies, waits for them, and re-layouts: none -> 4.69 us  [per_device(): near = near[:, start:start + width]]
  transfers between devices with their start and end apart: 3 -> 24, of which waited for: 3 -> 13; matrix products, arithmetic and copies ran while one was open for 2% -> 10% of each run, Pallas kernels for 0% -> 17%
where the time goes in v1:
time: 127 us
  waiting for transfers between devices  46.9 us (37%)
  starting transfers between devices  38 us (30%)
  Pallas kernels  24.4 us (19%)
  local copies, waits for them, and re-layouts  13.2 us (10%)
  other arithmetic  3.21 us (3%)
    ppermute x12, starting transfers between devices, exchange(): lax.ppermute(array, 'dp', dp_shift(*move))  25.9 us
    ppermute x12, waiting for transfers between devices, exchange(): lax.ppermute(array, 'dp', dp_shift(*move))  24.5 us
    pallas_call x4, Pallas kernels, product(): pl.pallas_call(product_kernel, grid=(width // BLOCK,), in_specs=specs, ou...  14.7 us
    ppermute x6, waiting for transfers between devices, to_x(): return lax.ppermute(array, 'mp', [(i, (i + step) % NX) for i in range(NX)])  10.9 us
    pallas_call x8, Pallas kernels, local(): pl.pallas_call(body, in_specs=[SMEM] + [VMEM] * len(operands), out_specs=...  9.72 us
    ppermute x6, starting transfers between devices, to_x(): return lax.ppermute(array, 'mp', [(i, (i + step) % NX) for i in range(NX)])  9.51 us
    ppermute x2, waiting for transfers between devices, swap_z(): return lax.ppermute(array, 'dp', pairs)  8.17 us
    unnamed x11, local copies, waits for them, and re-layouts  4.96 us
  transfers between devices with their start and end apart: 24, of which 13 were waited for; matrix products, arithmetic and copies ran while one was open for 10% of the time, Pallas kernels for 17%

profile of v1, /device:TPU:8, one launch (start us, length us, event | category | flops | bytes accessed | tf_op | source)
XLA Modules:
  0.0 126.5 jit_solution(12209361176222819754)
XLA Ops:
  0.6 2.8 %collective-permute-start.1 = (bf16[128,12288]{1,0:T(8,128)(2,1)}, bf16[128,12288]{1,0:T(8,128)(2,1)S(1)}, u32[]{:S(2)}, u32[]{:S(2)}) collective-permute-start(bf16[128,12288]{1,0:T(8,128)(2,1)} %own.7), channel_id=1, source_target_pairs={{0,3},{1,0},{2,1},{3,2},{4,7},{5,4},{6,5},{7,6},{8,11},{9,8},{10,9... | collective-permute-start | bytes 9437192 | tf_op jit(solution)/shard_map/ppermute | solution.py:39
  3.5 2.1 %dynamic-slice_bitcast_fusion = bf16[32,12288]{1,0:T(8,128)(2,1)} fusion(bf16[1,64,12288]{2,1,0:T(8,128)(2,1)} %grad.1, s32[]{:T(128)S(6)} %select_n.70), kind=kLoop, calls=%fused_computation | loop fusion | bytes 1572868 | tf_op jit(solution)/shard_map/dynamic_slice | solution.py:182
  5.6 2.5 %collective-permute-done.2.theirs = bf16[32,12288]{1,0:T(8,128)(2,1)} collective-permute-done((bf16[32,12288]{1,0:T(8,128)(2,1)}, bf16[32,12288]{1,0:T(8,128)(2,1)}, u32[]{:S(2)}, u32[]{:S(2)}) %collective-permute-start.2) | collective-permute-done | bytes 786464 | tf_op jit(solution)/shard_map/ppermute | solution.py:35
  9.6 2.1 %shard_map.101 = (f32[32,3072]{1,0:T(8,128)S(1)}, f32[32,3072]{1,0:T(8,128)S(1)}, f32[32,3072]{1,0:T(8,128)}, f32[32,3072]{1,0:T(8,128)}) custom-call(s32[5]{0:T(128)S(1)} %stack.35.place, bf16[1,64,12288]{2,1,0:T(8,128)(2,1)S(1)} %copy-done.1, bf16[32,12288]{1,0:T(8,128)(2,1)} %collective-permute-done.2.theirs), custom_call_target="tpu_custom_call" | custom-call | tf_op jit(solution)/shard_map/pallas_call | solution.py:94
  11.7 1.6 %collective-permute-start.3 = (f32[32,3072]{1,0:T(8,128)S(1)}, f32[32,3072]{1,0:T(8,128)S(1)}, u32[]{:S(2)}, u32[]{:S(2)}) collective-permute-start(f32[32,3072]{1,0:T(8,128)S(1)} %get-tuple-element.28), channel_id=1, source_target_pairs={{0,64},{4,68},{8,72},{12,76},{16,80},{20,84},{24,88},{28,92},{32,9... | collective-permute-start | bytes 1179656 | tf_op jit(solution)/shard_map/ppermute | solution.py:81
  13.3 1.9 %collective-permute-start.4 = (f32[32,3072]{1,0:T(8,128)}, f32[32,3072]{1,0:T(8,128)}, u32[]{:S(2)}, u32[]{:S(2)}) collective-permute-start(f32[32,3072]{1,0:T(8,128)} %get-tuple-element.29), channel_id=1, source_target_pairs={{0,128},{4,132},{8,136},{12,140},{16,144},{20,148},{24,152},{28,15... | collective-permute-start | bytes 1179656 | tf_op jit(solution)/shard_map/ppermute | solution.py:81
  15.2 1.4 %collective-permute-start.5 = (f32[32,3072]{1,0:T(8,128)}, f32[32,3072]{1,0:T(8,128)}, u32[]{:S(2)}, u32[]{:S(2)}) collective-permute-start(f32[32,3072]{1,0:T(8,128)} %get-tuple-element.30), channel_id=1, source_target_pairs={{0,192},{4,196},{8,200},{12,204},{16,208},{20,212},{24,216},{28,22... | collective-permute-start | bytes 1179656 | tf_op jit(solution)/shard_map/ppermute | solution.py:81
  18.3 5.4 %collective-permute-done.3.b = f32[32,3072]{1,0:T(8,128)S(1)} collective-permute-done((f32[32,3072]{1,0:T(8,128)S(1)}, f32[32,3072]{1,0:T(8,128)S(1)}, u32[]{:S(2)}, u32[]{:S(2)}) %collective-permute-start.3) | collective-permute-done | bytes 393248 | tf_op jit(solution)/shard_map/ppermute | solution.py:81
  24.4 2.7 %collective-permute-done.4.c = f32[32,3072]{1,0:T(8,128)} collective-permute-done((f32[32,3072]{1,0:T(8,128)}, f32[32,3072]{1,0:T(8,128)}, u32[]{:S(2)}, u32[]{:S(2)}) %collective-permute-start.4) | collective-permute-done | bytes 393248 | tf_op jit(solution)/shard_map/ppermute | solution.py:81
  27.1 7.3 %collective-permute-done.5.d = f32[32,3072]{1,0:T(8,128)} collective-permute-done((f32[32,3072]{1,0:T(8,128)}, f32[32,3072]{1,0:T(8,128)}, u32[]{:S(2)}, u32[]{:S(2)}) %collective-permute-start.5) | collective-permute-done | bytes 393248 | tf_op jit(solution)/shard_map/ppermute | solution.py:81
  38.8 4.7 %collective-permute-done.6.b = f32[32,1536]{1,0:T(8,128)S(1)} collective-permute-done((f32[32,1536]{1,0:T(8,128)S(1)}, f32[32,1536]{1,0:T(8,128)S(1)}, u32[]{:S(2)}, u32[]{:S(2)}) %collective-permute-start.6) | collective-permute-done | bytes 196640 | tf_op jit(solution)/shard_map/ppermute | solution.py:86
  44.1 1.9 %collective-permute-start.7 = (f32[32,384]{1,0:T(8,128)S(1)}, f32[32,384]{1,0:T(8,128)S(1)}, u32[]{:S(2)}, u32[]{:S(2)}) collective-permute-start(f32[32,384]{1,0:T(8,128)S(1)} %get-tuple-element.34), channel_id=1, source_target_pairs={{0,16},{4,20},{8,24},{12,28},{16,32},{20,36},{24,40},{28,44},{32,4... | collective-permute-start | bytes 147464 | tf_op jit(solution)/shard_map/ppermute | solution.py:81
  46.0 5.2 %collective-permute-start.8 = (f32[32,384]{1,0:T(8,128)S(1)}, f32[32,384]{1,0:T(8,128)S(1)}, u32[]{:S(2)}, u32[]{:S(2)}) collective-permute-start(f32[32,384]{1,0:T(8,128)S(1)} %get-tuple-element.35), channel_id=1, source_target_pairs={{0,32},{4,36},{8,40},{12,44},{16,48},{20,52},{24,56},{28,60},{32,0... | collective-permute-start | bytes 147464 | tf_op jit(solution)/shard_map/ppermute | solution.py:81
  51.2 2.7 %collective-permute-start.9 = (f32[32,384]{1,0:T(8,128)S(1)}, f32[32,384]{1,0:T(8,128)S(1)}, u32[]{:S(2)}, u32[]{:S(2)}) collective-permute-start(f32[32,384]{1,0:T(8,128)S(1)} %get-tuple-element.36), channel_id=1, source_target_pairs={{0,48},{4,52},{8,56},{12,60},{16,0},{20,4},{24,8},{28,12},{32,16},... | collective-permute-start | bytes 147464 | tf_op jit(solution)/shard_map/ppermute | solution.py:81
  54.2 2.9 %collective-permute-done.9.d = f32[32,384]{1,0:T(8,128)S(1)} collective-permute-done((f32[32,384]{1,0:T(8,128)S(1)}, f32[32,384]{1,0:T(8,128)S(1)}, u32[]{:S(2)}, u32[]{:S(2)}) %collective-permute-start.9) | collective-permute-done | bytes 49184 | tf_op jit(solution)/shard_map/ppermute | solution.py:81
  57.7 3.0 %collective-permute-start.13 = (bf16[32,384]{1,0:T(8,128)(2,1)S(1)}, bf16[32,384]{1,0:T(8,128)(2,1)S(1)}, u32[]{:S(2)}, u32[]{:S(2)}) collective-permute-start(bf16[32,384]{1,0:T(8,128)(2,1)S(1)} %get-tuple-element.38.refs_0_), channel_id=1, source_target_pairs={{0,48},{4,52},{8,56},{12,60},{16,0},{20,4},{24,8},{28,12},{32,16},... | collective-permute-start | bytes 73736 | tf_op jit(solution)/shard_map/ppermute | solution.py:81
  60.8 1.8 %collective-permute-start.12 = (bf16[32,384]{1,0:T(8,128)(2,1)S(1)}, bf16[32,384]{1,0:T(8,128)(2,1)S(1)}, u32[]{:S(2)}, u32[]{:S(2)}) collective-permute-start(bf16[32,384]{1,0:T(8,128)(2,1)S(1)} %get-tuple-element.38.refs_0_), channel_id=1, source_target_pairs={{0,32},{4,36},{8,40},{12,44},{16,48},{20,52},{24,56},{28,60},{32,0... | collective-permute-start | bytes 73736 | tf_op jit(solution)/shard_map/ppermute | solution.py:81
  63.2 5.5 %collective-permute-done.12.refs_2_ = bf16[32,384]{1,0:T(8,128)(2,1)S(1)} collective-permute-done((bf16[32,384]{1,0:T(8,128)(2,1)S(1)}, bf16[32,384]{1,0:T(8,128)(2,1)S(1)}, u32[]{:S(2)}, u32[]{:S(2)}) %collective-permute-start.12) | collective-permute-done | bytes 24608 | tf_op jit(solution)/shard_map/ppermute | solution.py:81
  71.1 3.4 %collective-permute-done.14.other = bf16[32,1536]{1,0:T(8,128)(2,1)S(1)} collective-permute-done((bf16[32,1536]{1,0:T(8,128)(2,1)S(1)}, bf16[32,1536]{1,0:T(8,128)(2,1)S(1)}, u32[]{:S(2)}, u32[]{:S(2)}) %collective-permute-start.14) | collective-permute-done | bytes 98336 | tf_op jit(solution)/shard_map/ppermute | solution.py:86
  75.9 2.3 %collective-permute-start.16 = (bf16[32,3072]{1,0:T(8,128)(2,1)S(1)}, bf16[32,3072]{1,0:T(8,128)(2,1)S(1)}, u32[]{:S(2)}, u32[]{:S(2)}) collective-permute-start(bf16[32,3072]{1,0:T(8,128)(2,1)S(1)} %shard_map.106.refs_0_), channel_id=1, source_target_pairs={{0,128},{4,132},{8,136},{12,140},{16,144},{20,148},{24,152},{28,15... | collective-permute-start | bytes 589832 | tf_op jit(solution)/shard_map/ppermute | solution.py:81
  78.3 2.5 %collective-permute-start.15 = (bf16[32,3072]{1,0:T(8,128)(2,1)S(1)}, bf16[32,3072]{1,0:T(8,128)(2,1)S(1)}, u32[]{:S(2)}, u32[]{:S(2)}) collective-permute-start(bf16[32,3072]{1,0:T(8,128)(2,1)S(1)} %shard_map.106.refs_0_), channel_id=1, source_target_pairs={{0,64},{4,68},{8,72},{12,76},{16,80},{20,84},{24,88},{28,92},{32,9... | collective-permute-start | bytes 589832 | tf_op jit(solution)/shard_map/ppermute | solution.py:81
  80.8 2.4 %slice.35 = bf16[128,4096]{1,0:T(8,128)(2,1)} slice(bf16[128,12288]{1,0:T(8,128)(2,1)} %collective-permute-done.before), slice={[0:128], [0:4096]} | slice | bytes 2097152 | tf_op jit(solution)/shard_map/slice | solution.py:205
  85.0 2.5 %collective-permute-start.20 = (bf16[128,4096]{1,0:T(8,128)(2,1)}, bf16[128,4096]{1,0:T(8,128)(2,1)}, u32[]{:S(2)}, u32[]{:S(2)}) collective-permute-start(bf16[128,4096]{1,0:T(8,128)(2,1)} %slice.33), channel_id=1, source_target_pairs={{0,3},{1,0},{2,1},{3,2},{4,7},{5,4},{6,5},{7,6},{8,11},{9,8},{10,9... | collective-permute-start | bytes 3145736 | tf_op jit(solution)/shard_map/ppermute | solution.py:39
  87.5 1.5 %shard_map.107.mine = bf16[32,12288]{1,0:T(8,128)(2,1)} custom-call(s32[5]{0:T(128)S(1)} %stack.35.place, bf16[32,3072]{1,0:T(8,128)(2,1)S(1)} %shard_map.106.refs_0_, bf16[32,3072]{1,0:T(8,128)(2,1)S(1)} %collective-permute-done.15.refs_1_, bf16[32,3072]{1,0:T(8,128)(2,1)S(1)} %collective-permute-done.16.refs_2_, ...), custom_call_target="tpu_custom_call" | custom-call | tf_op jit(solution)/shard_map/pallas_call | solution.py:94
  88.9 1.8 %copy.14 = bf16[512,256]{0,1:T(8,128)(2,1)} copy(bf16[512,256]{1,0:T(8,128)(2,1)} %param.11) | data formatting | bytes 524288 | tf_op args[5]
  94.1 2.6 %shard_map.108 = bf16[64,12288]{1,0:T(8,128)(2,1)} custom-call(s32[5]{0:T(128)S(1)} %stack.35.place, bf16[32,12288]{1,0:T(8,128)(2,1)} %shard_map.107.mine, bf16[32,12288]{1,0:T(8,128)(2,1)} %collective-permute-done.18.other), custom_call_target="tpu_custom_call" | custom-call | tf_op jit(solution)/shard_map/pallas_call | solution.py:94
  96.7 10.0 %collective-permute-done.22.opposite = bf16[128,4096]{1,0:T(8,128)(2,1)} collective-permute-done((bf16[128,4096]{1,0:T(8,128)(2,1)}, bf16[128,4096]{1,0:T(8,128)(2,1)}, u32[]{:S(2)}, u32[]{:S(2)}) %collective-permute-start.22) | collective-permute-done | bytes 1048608 | tf_op jit(solution)/shard_map/ppermute | solution.py:39
  107.5 3.4 %collective-permute-start.21 = (bf16[128,2048]{1,0:T(8,128)(2,1)S(1)}, bf16[128,2048]{1,0:T(8,128)(2,1)S(1)}, u32[]{:S(2)}, u32[]{:S(2)}) collective-permute-start(bf16[128,2048]{1,0:T(8,128)(2,1)S(1)} %slice.32), channel_id=1, source_target_pairs={{0,3},{1,0},{2,1},{3,2},{4,7},{5,4},{6,5},{7,6},{8,11},{9,8},{10,9... | collective-permute-start | bytes 1572872 | tf_op jit(solution)/shard_map/ppermute | solution.py:39
  111.1 4.7 %shard_map.109.rest_0_ = bf16[1,256,12288]{2,1,0:T(8,128)(2,1)} custom-call(bf16[256,512]{1,0:T(8,128)(2,1)S(1)} %fusion.1.lhs, bf16[128,12288]{1,0:T(8,128)(2,1)S(1)} %copy-done, bf16[128,12288]{1,0:T(8,128)(2,1)S(1)} %collective-permute-done.1.after, bf16[128,4096]{1,0:T(8,128)(2,1)} %collective-permute-done.22.opposite, ...), custom_call_target="tpu_custom_call" | custom-call | flops 1073741824 | bytes 6291456 | tf_op jit(solution)/shard_map/pallas_call | solution.py:64
  115.8 4.6 %shard_map.110.rest_0_ = bf16[1,256,12288]{2,1,0:T(8,128)(2,1)} custom-call(bf16[256,512]{1,0:T(8,128)(2,1)S(1)} %fusion.1.lhs, bf16[128,12288]{1,0:T(8,128)(2,1)S(1)} %copy-done, bf16[128,12288]{1,0:T(8,128)(2,1)S(1)} %collective-permute-done.1.after, bf16[128,4096]{1,0:T(8,128)(2,1)} %collective-permute-done.20.opposite, ...), custom_call_target="tpu_custom_call", output_to_operand_aliasing={{}: (5, {})} | custom-call | flops 1073741824 | bytes 6291456 | tf_op jit(solution)/shard_map/pallas_call | solution.py:64
  121.1 2.7 %shard_map.111.rest_0_ = bf16[1,256,12288]{2,1,0:T(8,128)(2,1)} custom-call(bf16[256,512]{1,0:T(8,128)(2,1)S(1)} %fusion.1.lhs, bf16[128,12288]{1,0:T(8,128)(2,1)S(1)} %copy-done, bf16[128,12288]{1,0:T(8,128)(2,1)S(1)} %collective-permute-done.1.after, bf16[128,2048]{1,0:T(8,128)(2,1)S(1)} %collective-permute-done.23.opposite, ...), custom_call_target="tpu_custom_call", output_to_operand_aliasing={{}: (5, {})} | custom-call | flops 536870912 | bytes 3145728 | tf_op jit(solution)/shard_map/pallas_call | solution.py:64
  123.8 2.7 %shard_map.112 = bf16[1,256,12288]{2,1,0:T(8,128)(2,1)} custom-call(bf16[256,512]{1,0:T(8,128)(2,1)S(1)} %fusion.1.lhs, bf16[128,12288]{1,0:T(8,128)(2,1)S(1)} %copy-done, bf16[128,12288]{1,0:T(8,128)(2,1)S(1)} %collective-permute-done.1.after, bf16[128,2048]{1,0:T(8,128)(2,1)S(1)} %collective-permute-done.21.opposite, ...), custom_call_target="tpu_custom_call", output_to_operand_aliasing={{}: (5, {})} | custom-call | flops 536870912 | bytes 3145728 | tf_op jit(solution)/shard_map/pallas_call | solution.py:64
  (54 shorter events, 21.0 us)
Async XLA Ops:
  0.6 74.5 %collective-permute-start.1 = (bf16[128,12288]{1,0:T(8,128)(2,1)}, bf16[128,12288]{1,0:T(8,128)(2,1)S(1)}, u32[]{:S(2)}, u32[]{:S(2)}) collective-permute-start(bf16[128,12288]{1,0:T(8,128)(2,1)} %own.7), channel_id=1, source_target_pairs={{0,3},{1,0},{2,1},{3,2},{4,7},{5,4},{6,5},{7,6},{8,11},{9,8},{10,9... | collective-permute-start | bytes 9437192 | tf_op jit(solution)/shard_map/ppermute | solution.py:39
  3.5 71.6 %collective-permute-start = (bf16[128,12288]{1,0:T(8,128)(2,1)}, bf16[128,12288]{1,0:T(8,128)(2,1)}, u32[]{:S(2)}, u32[]{:S(2)}) collective-permute-start(bf16[128,12288]{1,0:T(8,128)(2,1)} %own.7), channel_id=1, source_target_pairs={{0,1},{1,2},{2,3},{3,0},{4,5},{5,6},{6,7},{7,4},{8,9},{9,10},{10,1... | collective-permute-start | bytes 9437192 | tf_op jit(solution)/shard_map/ppermute | solution.py:39
  5.5 2.6 %collective-permute-start.2 = (bf16[32,12288]{1,0:T(8,128)(2,1)}, bf16[32,12288]{1,0:T(8,128)(2,1)}, u32[]{:S(2)}, u32[]{:S(2)}) collective-permute-start(bf16[32,12288]{1,0:T(8,128)(2,1)} %dynamic-slice_bitcast_fusion), channel_id=1, source_target_pairs={{0,4},{4,0},{8,12},{12,8},{16,20},{20,16},{24,28},{28,24},{32,36},... | collective-permute-start | bytes 2359304 | tf_op jit(solution)/shard_map/ppermute | solution.py:35
  8.2 1.4 %copy-start.1 = (bf16[1,64,12288]{2,1,0:T(8,128)(2,1)S(1)}, bf16[1,64,12288]{2,1,0:T(8,128)(2,1)}, u32[]{:S(2)}) copy-start(bf16[1,64,12288]{2,1,0:T(8,128)(2,1)} %grad.1) | copy-start | bytes 4718596
  11.7 12.0 %collective-permute-start.3 = (f32[32,3072]{1,0:T(8,128)S(1)}, f32[32,3072]{1,0:T(8,128)S(1)}, u32[]{:S(2)}, u32[]{:S(2)}) collective-permute-start(f32[32,3072]{1,0:T(8,128)S(1)} %get-tuple-element.28), channel_id=1, source_target_pairs={{0,64},{4,68},{8,72},{12,76},{16,80},{20,84},{24,88},{28,92},{32,9... | collective-permute-start | bytes 1179656 | tf_op jit(solution)/shard_map/ppermute | solution.py:81
  13.3 13.9 %collective-permute-start.4 = (f32[32,3072]{1,0:T(8,128)}, f32[32,3072]{1,0:T(8,128)}, u32[]{:S(2)}, u32[]{:S(2)}) collective-permute-start(f32[32,3072]{1,0:T(8,128)} %get-tuple-element.29), channel_id=1, source_target_pairs={{0,128},{4,132},{8,136},{12,140},{16,144},{20,148},{24,152},{28,15... | collective-permute-start | bytes 1179656 | tf_op jit(solution)/shard_map/ppermute | solution.py:81
  15.2 19.2 %collective-permute-start.5 = (f32[32,3072]{1,0:T(8,128)}, f32[32,3072]{1,0:T(8,128)}, u32[]{:S(2)}, u32[]{:S(2)}) collective-permute-start(f32[32,3072]{1,0:T(8,128)} %get-tuple-element.30), channel_id=1, source_target_pairs={{0,192},{4,196},{8,200},{12,204},{16,208},{20,212},{24,216},{28,22... | collective-permute-start | bytes 1179656 | tf_op jit(solution)/shard_map/ppermute | solution.py:81
  17.5 6.1 %copy-start.4 = (f32[3,64,192]{2,1,0:T(8,128)}, f32[3,64,192]{2,1,0:T(8,128)S(1)}, u32[]{:S(2)}) copy-start(f32[3,64,192]{2,1,0:T(8,128)S(1)} %pad_maximum_fusion) | copy-start | bytes 442372
  23.6 0.8 copy-start.2
  24.4 13.4 %collective-permute-start.10 = (f32[3,32,192]{2,1,0:T(8,128)}, f32[3,32,192]{2,1,0:T(8,128)}, u32[]{:S(2)}, u32[]{:S(2)}) collective-permute-start(f32[3,32,192]{2,1,0:T(8,128)} %constant_dynamic-slice_fusion), channel_id=1, source_target_pairs={{0,4},{4,0},{8,12},{12,8},{16,20},{20,16},{24,28},{28,24},{32,36},... | collective-permute-start | bytes 221192 | tf_op jit(solution)/shard_map/ppermute | solution.py:35
  34.4 1.0 copy-start.3
  36.6 6.9 %collective-permute-start.6 = (f32[32,1536]{1,0:T(8,128)S(1)}, f32[32,1536]{1,0:T(8,128)S(1)}, u32[]{:S(2)}, u32[]{:S(2)}) collective-permute-start(f32[32,1536]{1,0:T(8,128)S(1)} %get-tuple-element.32), channel_id=1, source_target_pairs={{0,8},{4,12},{8,0},{12,4},{16,24},{20,28},{24,16},{28,20},{32,40},... | collective-permute-start | bytes 589832 | tf_op jit(solution)/shard_map/ppermute | solution.py:86
  44.1 9.9 %collective-permute-start.7 = (f32[32,384]{1,0:T(8,128)S(1)}, f32[32,384]{1,0:T(8,128)S(1)}, u32[]{:S(2)}, u32[]{:S(2)}) collective-permute-start(f32[32,384]{1,0:T(8,128)S(1)} %get-tuple-element.34), channel_id=1, source_target_pairs={{0,16},{4,20},{8,24},{12,28},{16,32},{20,36},{24,40},{28,44},{32,4... | collective-permute-start | bytes 147464 | tf_op jit(solution)/shard_map/ppermute | solution.py:81
  46.0 8.2 %collective-permute-start.8 = (f32[32,384]{1,0:T(8,128)S(1)}, f32[32,384]{1,0:T(8,128)S(1)}, u32[]{:S(2)}, u32[]{:S(2)}) collective-permute-start(f32[32,384]{1,0:T(8,128)S(1)} %get-tuple-element.35), channel_id=1, source_target_pairs={{0,32},{4,36},{8,40},{12,44},{16,48},{20,52},{24,56},{28,60},{32,0... | collective-permute-start | bytes 147464 | tf_op jit(solution)/shard_map/ppermute | solution.py:81
  51.2 5.9 %collective-permute-start.9 = (f32[32,384]{1,0:T(8,128)S(1)}, f32[32,384]{1,0:T(8,128)S(1)}, u32[]{:S(2)}, u32[]{:S(2)}) collective-permute-start(f32[32,384]{1,0:T(8,128)S(1)} %get-tuple-element.36), channel_id=1, source_target_pairs={{0,48},{4,52},{8,56},{12,60},{16,0},{20,4},{24,8},{28,12},{32,16},... | collective-permute-start | bytes 147464 | tf_op jit(solution)/shard_map/ppermute | solution.py:81
  57.7 5.5 %collective-permute-start.13 = (bf16[32,384]{1,0:T(8,128)(2,1)S(1)}, bf16[32,384]{1,0:T(8,128)(2,1)S(1)}, u32[]{:S(2)}, u32[]{:S(2)}) collective-permute-start(bf16[32,384]{1,0:T(8,128)(2,1)S(1)} %get-tuple-element.38.refs_0_), channel_id=1, source_target_pairs={{0,48},{4,52},{8,56},{12,60},{16,0},{20,4},{24,8},{28,12},{32,16},... | collective-permute-start | bytes 73736 | tf_op jit(solution)/shard_map/ppermute | solution.py:81
  60.8 8.0 %collective-permute-start.12 = (bf16[32,384]{1,0:T(8,128)(2,1)S(1)}, bf16[32,384]{1,0:T(8,128)(2,1)S(1)}, u32[]{:S(2)}, u32[]{:S(2)}) collective-permute-start(bf16[32,384]{1,0:T(8,128)(2,1)S(1)} %get-tuple-element.38.refs_0_), channel_id=1, source_target_pairs={{0,32},{4,36},{8,40},{12,44},{16,48},{20,52},{24,56},{28,60},{32,0... | collective-permute-start | bytes 73736 | tf_op jit(solution)/shard_map/ppermute | solution.py:81
  62.6 6.7 %collective-permute-start.11 = (bf16[32,384]{1,0:T(8,128)(2,1)S(1)}, bf16[32,384]{1,0:T(8,128)(2,1)S(1)}, u32[]{:S(2)}, u32[]{:S(2)}) collective-permute-start(bf16[32,384]{1,0:T(8,128)(2,1)S(1)} %get-tuple-element.38.refs_0_), channel_id=1, source_target_pairs={{0,16},{4,20},{8,24},{12,28},{16,32},{20,36},{24,40},{28,44},{32,4... | collective-permute-start | bytes 73736 | tf_op jit(solution)/shard_map/ppermute | solution.py:81
  69.8 4.7 %collective-permute-start.14 = (bf16[32,1536]{1,0:T(8,128)(2,1)S(1)}, bf16[32,1536]{1,0:T(8,128)(2,1)S(1)}, u32[]{:S(2)}, u32[]{:S(2)}) collective-permute-start(bf16[32,1536]{1,0:T(8,128)(2,1)S(1)} %shard_map.105.mine), channel_id=1, source_target_pairs={{0,8},{4,12},{8,0},{12,4},{16,24},{20,28},{24,16},{28,20},{32,40},... | collective-permute-start | bytes 294920 | tf_op jit(solution)/shard_map/ppermute | solution.py:86
  75.1 12.3 %collective-permute-start.17 = (bf16[32,3072]{1,0:T(8,128)(2,1)S(1)}, bf16[32,3072]{1,0:T(8,128)(2,1)S(1)}, u32[]{:S(2)}, u32[]{:S(2)}) collective-permute-start(bf16[32,3072]{1,0:T(8,128)(2,1)S(1)} %shard_map.106.refs_0_), channel_id=1, source_target_pairs={{0,192},{4,196},{8,200},{12,204},{16,208},{20,212},{24,216},{28,22... | collective-permute-start | bytes 589832 | tf_op jit(solution)/shard_map/ppermute | solution.py:81
  75.9 11.5 %collective-permute-start.16 = (bf16[32,3072]{1,0:T(8,128)(2,1)S(1)}, bf16[32,3072]{1,0:T(8,128)(2,1)S(1)}, u32[]{:S(2)}, u32[]{:S(2)}) collective-permute-start(bf16[32,3072]{1,0:T(8,128)(2,1)S(1)} %shard_map.106.refs_0_), channel_id=1, source_target_pairs={{0,128},{4,132},{8,136},{12,140},{16,144},{20,148},{24,152},{28,15... | collective-permute-start | bytes 589832 | tf_op jit(solution)/shard_map/ppermute | solution.py:81
  78.3 9.2 %collective-permute-start.15 = (bf16[32,3072]{1,0:T(8,128)(2,1)S(1)}, bf16[32,3072]{1,0:T(8,128)(2,1)S(1)}, u32[]{:S(2)}, u32[]{:S(2)}) collective-permute-start(bf16[32,3072]{1,0:T(8,128)(2,1)S(1)} %shard_map.106.refs_0_), channel_id=1, source_target_pairs={{0,64},{4,68},{8,72},{12,76},{16,80},{20,84},{24,88},{28,92},{32,9... | collective-permute-start | bytes 589832 | tf_op jit(solution)/shard_map/ppermute | solution.py:81
  83.1 23.5 %collective-permute-start.22 = (bf16[128,4096]{1,0:T(8,128)(2,1)}, bf16[128,4096]{1,0:T(8,128)(2,1)}, u32[]{:S(2)}, u32[]{:S(2)}) collective-permute-start(bf16[128,4096]{1,0:T(8,128)(2,1)} %slice.35), channel_id=1, source_target_pairs={{0,1},{1,2},{2,3},{3,0},{4,5},{5,6},{6,7},{7,4},{8,9},{9,10},{10,1... | collective-permute-start | bytes 3145736 | tf_op jit(solution)/shard_map/ppermute | solution.py:39
  85.0 22.6 %collective-permute-start.20 = (bf16[128,4096]{1,0:T(8,128)(2,1)}, bf16[128,4096]{1,0:T(8,128)(2,1)}, u32[]{:S(2)}, u32[]{:S(2)}) collective-permute-start(bf16[128,4096]{1,0:T(8,128)(2,1)} %slice.33), channel_id=1, source_target_pairs={{0,3},{1,0},{2,1},{3,2},{4,7},{5,4},{6,5},{7,6},{8,11},{9,8},{10,9... | collective-permute-start | bytes 3145736 | tf_op jit(solution)/shard_map/ppermute | solution.py:39
  88.9 2.6 %collective-permute-start.18 = (bf16[32,12288]{1,0:T(8,128)(2,1)}, bf16[32,12288]{1,0:T(8,128)(2,1)}, u32[]{:S(2)}, u32[]{:S(2)}) collective-permute-start(bf16[32,12288]{1,0:T(8,128)(2,1)} %shard_map.107.mine), channel_id=1, source_target_pairs={{0,4},{4,0},{8,12},{12,8},{16,20},{20,16},{24,28},{28,24},{32,36},... | collective-permute-start | bytes 2359304 | tf_op jit(solution)/shard_map/ppermute | solution.py:35
  91.6 19.4 %collective-permute-start.19 = (f32[3,32,192]{2,1,0:T(8,128)S(1)}, f32[3,32,192]{2,1,0:T(8,128)S(1)}, u32[]{:S(2)}, u32[]{:S(2)}) collective-permute-start(f32[3,32,192]{2,1,0:T(8,128)S(1)} %slice_select_fusion), channel_id=1, source_target_pairs={{0,4},{4,0},{8,12},{12,8},{16,20},{20,16},{24,28},{28,24},{32,36},... | collective-permute-start | bytes 221192 | tf_op jit(solution)/shard_map/ppermute | solution.py:35
  92.8 18.4 %copy-start = (bf16[128,12288]{1,0:T(8,128)(2,1)S(1)}, bf16[128,12288]{1,0:T(8,128)(2,1)}, u32[]{:S(2)}) copy-start(bf16[128,12288]{1,0:T(8,128)(2,1)} %own.7) | copy-start | bytes 9437188
  106.7 14.4 %collective-permute-start.23 = (bf16[128,2048]{1,0:T(8,128)(2,1)S(1)}, bf16[128,2048]{1,0:T(8,128)(2,1)S(1)}, u32[]{:S(2)}, u32[]{:S(2)}) collective-permute-start(bf16[128,2048]{1,0:T(8,128)(2,1)S(1)} %slice.34), channel_id=1, source_target_pairs={{0,1},{1,2},{2,3},{3,0},{4,5},{5,6},{6,7},{7,4},{8,9},{9,10},{10,1... | collective-permute-start | bytes 1572872 | tf_op jit(solution)/shard_map/ppermute | solution.py:39
  107.5 16.3 %collective-permute-start.21 = (bf16[128,2048]{1,0:T(8,128)(2,1)S(1)}, bf16[128,2048]{1,0:T(8,128)(2,1)S(1)}, u32[]{:S(2)}, u32[]{:S(2)}) collective-permute-start(bf16[128,2048]{1,0:T(8,128)(2,1)S(1)} %slice.32), channel_id=1, source_target_pairs={{0,3},{1,0},{2,1},{3,2},{4,7},{5,4},{6,5},{7,6},{8,11},{9,8},{10,9... | collective-permute-start | bytes 1572872 | tf_op jit(solution)/shard_map/ppermute | solution.py:39

commit v2 on v1

--- a/solution.py
+++ b/solution.py
@@ -17,8 +17,8 @@
 
 NY, NZ, NC, NX = 4, 8, 2, 4
 D = 12288
-BLOCK = 1024
-PIECES = ((0, 4096), (6144, 4096), (4096, 2048), (10240, 2048))
+PIECES = ((0, 5120), (10240, 1024))
+VMEM_LIMIT = 20 * 1024 * 1024
 
 
 def dp_shift(dy, dz, dc):
@@ -43,34 +43,58 @@
     return lax.dynamic_slice_in_dim(array, index * width, width, axis=1)
 
 
-def product_kernel(lhs, own, after, opposite, before, *rest):
+def product_kernel(lhs, own, after, before, first, second, *rest):
     out = rest[-1]
-    tokens = jnp.concatenate([own[...], after[...], opposite[...], before[...]], axis=0)
-    out[0] = jnp.dot(lhs[...], tokens, preferred_element_type=jnp.float32).astype(jnp.bfloat16)
-
-
-def product(piece, lhs, own, after, opposite, before, carry):
-    start, width = PIECES[piece]
-    skip = start // BLOCK
-    whole = pl.BlockSpec((128, BLOCK), lambda i: (0, skip + i))
-    alone = pl.BlockSpec((128, BLOCK), lambda i: (0, i))
-    specs = [pl.BlockSpec((256, 512), lambda i: (0, 0)), whole, whole, alone, whole]
-    operands = [lhs, own, after, opposite, before]
+    step, half_way = pl.program_id(0), pl.num_programs(0) // 2
+
+    def columns_of(opposite):
+        tokens = jnp.concatenate([own[...], after[...], opposite[...], before[...]], axis=0)
+        out[0] = jnp.dot(lhs[...], tokens, preferred_element_type=jnp.float32).astype(jnp.bfloat16)
+
+    @pl.when(step < half_way)
+    def _():
+        columns_of(first)
+
+    @pl.when(step >= half_way)
+    def _():
+        columns_of(second)
+
+
+def product(start, block, lhs, own, after, before, first, second, carry, sign_of_next=None):
+    steps, skip = first.shape[1] // block, start // block
+    whole = pl.BlockSpec((128, block), lambda i: (0, skip + i))
+    specs = [
+        pl.BlockSpec((256, 512), lambda i: (0, 0)),
+        whole,
+        whole,
+        whole,
+        pl.BlockSpec((128, block), lambda i: (0, jnp.minimum(i, steps - 1))),
+        pl.BlockSpec((128, block), lambda i: (0, jnp.maximum(i - steps, 0))),
+    ]
+    operands = [lhs, own, after, before, first, second]
     aliases = {}
     if carry is not None:
         specs.append(pl.BlockSpec(memory_space=pl.ANY))
         operands.append(carry)
-        aliases = {5: 0}
+        aliases = {6: 0}
+    if sign_of_next is not None:
+        specs.append(pl.BlockSpec(memory_space=pl.ANY))
+        operands.append(sign_of_next)
+    width = 2 * first.shape[1]
     return pl.pallas_call(
         product_kernel,
-        grid=(width // BLOCK,),
+        grid=(2 * steps,),
         in_specs=specs,
-        out_specs=pl.BlockSpec((1, 256, BLOCK), lambda i: (0, 0, skip + i)),
+        out_specs=pl.BlockSpec((1, 256, block), lambda i: (0, 0, skip + i)),
         out_shape=jax.ShapeDtypeStruct((1, 256, D), jnp.bfloat16),
         input_output_aliases=aliases,
         cost_estimate=pl.CostEstimate(flops=2 * 256 * 512 * width, bytes_accessed=1536 * width, transcendentals=0),
-        compiler_params=pltpu.CompilerParams(vmem_limit_bytes=24 * 1024 * 1024),
+        compiler_params=pltpu.CompilerParams(vmem_limit_bytes=VMEM_LIMIT),
     )(*operands)
+
+
+def sign(*arrays):
+    return jnp.concatenate([array[:16, :128] for array in arrays])
 
 
 def after_that(array, *events):
@@ -96,6 +120,7 @@
         in_specs=[SMEM] + [VMEM] * len(operands),
         out_specs=[VMEM] * len(shapes),
         out_shape=[jax.ShapeDtypeStruct(shape, dtype) for shape, dtype in shapes],
+        cost_estimate=pl.CostEstimate(flops=1024, bytes_accessed=1024, transcendentals=0),
         compiler_params=pltpu.CompilerParams(vmem_limit_bytes=16 * 1024 * 1024),
     )(place, *operands)
 
@@ -106,6 +131,40 @@
 
 def half(core):
     return pl.ds(pl.multiple_of(core * 32, 32), 32)
+
+
+def cut_kernel(places, before, after, *refs):
+    outs, sems = refs[:-1], refs[-1]
+    copies = []
+    for k, (out, start) in enumerate(zip(outs, places)):
+        source = (before, after)[k % 2].at[:, start : start + out.shape[1]]
+        copies.append(pltpu.make_async_copy(source, out, sems.at[k]))
+    for copy in copies:
+        copy.start()
+    for copy in copies:
+        copy.wait()
+
+
+def cut(pieces, before, after):
+    anywhere = pl.BlockSpec(memory_space=pl.ANY)
+    places = [start + way * width for start, width in pieces for way in (0, 1)]
+    shapes = [jax.ShapeDtypeStruct((128, width), jnp.bfloat16) for _, width in pieces for _ in (0, 1)]
+    return pl.pallas_call(
+        functools.partial(cut_kernel, places),
+        in_specs=[anywhere, anywhere],
+        out_specs=[VMEM] * len(shapes),
+        out_shape=shapes,
+        scratch_shapes=[pltpu.SemaphoreType.DMA((len(shapes),))],
+        cost_estimate=pl.CostEstimate(flops=1024, bytes_accessed=1024, transcendentals=0),
+        compiler_params=pltpu.CompilerParams(vmem_limit_bytes=16 * 1024 * 1024),
+    )(before, after)
+
+
+def turn(place, out_grads, out):
+    for step in range(NX):
+        owner = lax.rem(place[5] + step, NX)
+        rows = pl.ds(pl.multiple_of(owner * 128, 128), 128)
+        out[:, step * 128 : (step + 1) * 128] = out_grads[rows, :].T
 
 
 def add_cores(place, grad, theirs, *outs):
@@ -159,10 +218,13 @@
         out[:, at(2 * q + 1 - low, 384)] = other[:, piece]
 
 
-def join_cores(place, mine, other, out):
-    core = place[0]
-    out[half(core), :] = mine[...]
-    out[half(1 - core), :] = other[...]
+def join_rows(place, *refs):
+    *parts, out = refs
+    core, y = place[0], place[1]
+    for k in range(NY):
+        piece = at(lax.rem(y + NY - k, NY), 3072)
+        out[half(core), piece] = parts[k][...]
+        out[half(1 - core), piece] = parts[NY + k][...]
 
 
 def per_device(grads, master, moment, second, inputs, out_grads):
@@ -172,12 +234,12 @@
     z = (index // NC) % NZ
     y = index // (NC * NZ)
     first = core == 0
-    place = jnp.stack([core, y, z, z // 2, z % 2]).astype(jnp.int32)
+    place = jnp.stack([core, y, z, z // 2, z % 2, x]).astype(jnp.int32)
     f32, bf16 = jnp.float32, jnp.bfloat16
 
     before = to_x(inputs, 1)
     after = to_x(inputs, -1)
-    lhs = lax.dynamic_slice_in_dim(jnp.concatenate([out_grads, out_grads]), x * 128, 512, axis=0).T
+    (lhs,) = local(turn, place, (out_grads,), [((256, 512), bf16)])
 
     theirs = to_core(lax.dynamic_slice_in_dim(grads[0], (1 - core) * 32, 32, axis=0))
 
@@ -197,31 +259,33 @@
     got = exchange([own] * 3, [(0, 2 * k, 0) for k in (1, 2, 3)])
     (own,) = local(join_ring, place, (own, *got), [((32, 1536), bf16)])
     got = swap_z(own)
+
+    before, after, own, got = lax.optimization_barrier((before, after, own, got))
+    near = cut(PIECES[:1], before, after)
+    *near, own, got = lax.optimization_barrier((*near, own, got))
+    opposites = [to_x(near[0], 1), to_x(near[1], -1)]
+
     (own,) = local(join_pair, place, (own, got), [((32, 3072), bf16)])
-    before, after, own = lax.optimization_barrier((before, after, own))
-    opposites = []
-    for piece, (start, width) in enumerate(PIECES):
-        near, way = ((before, 1), (after, -1))[piece % 2]
-        near = near[:, start : start + width]
-        if piece >= 2:
-            near = after_that(near, opposites[piece - 2])
-        opposites.append(to_x(near, way))
-
     got = exchange([own] * 3, [(k, 0, 0) for k in (1, 2, 3)])
-    (own,) = local(join_ring, place, (own, *got), [((32, D), bf16)])
-
-    other = to_core(own)
-    (weights,) = local(join_cores, place, (own, other), [((64, D), bf16)])
+
+    parts = [own, *got]
+    others = [to_core(part) for part in parts]
+    (weights,) = local(join_rows, place, (*parts, *others), [((64, D), bf16)])
 
     left, right = state[:, :, :192], state[:, :, 192:]
     kept = jnp.where(first, left, right)
-    got = to_core(after_that(jnp.where(first, right, left), other))
+    got = to_core(after_that(jnp.where(first, right, left), others[0]))
     state = jnp.concatenate([jnp.where(first, kept, got), jnp.where(first, got, kept)], axis=1)
-
-    lhs, weights, state = lax.optimization_barrier((lhs, weights, state))
-    carry = None
-    for piece in range(4):
-        carry = product(piece, lhs, inputs, after, opposites[piece], before, carry)
+    state = [state[0], state[1], state[2]]
+
+    near = cut(PIECES[1:], before, after)
+    *near, weights, state[0], state[1], state[2], there = lax.optimization_barrier(
+        (*near, weights, *state, sign(*opposites))
+    )
+    opposites += [to_x(near[0], 1), to_x(near[1], -1)]
+
+    carry = product(PIECES[0][0], 2560, lhs, inputs, after, before, *opposites[:2], None, there)
+    carry = product(PIECES[1][0], 1024, lhs, inputs, after, before, *opposites[2:], carry)
 
     return (weights, state[0], state[1], state[2], carry)
 

time: 127 us -> 120 us (0.945)
  local copies, waits for them, and re-layouts: 13.2 us -> 6.05 us
  waiting for transfers between devices: 46.9 us -> 51.8 us
  Pallas kernels: 24.4 us -> 19.9 us
    ppermute x12, waiting for transfers between devices: 24.5 us -> 31.4 us  [exchange(): lax.ppermute(array, 'dp', dp_shift(*move))]
    slice x4 -> x2, local copies, waits for them, and re-layouts: 4.69 us -> 0.01 us  [sign(): return jnp.concatenate([array[:16, :128] for array in arrays])]
    pallas_call x4, Pallas kernels: 14.7 us -> 11.8 us  [the longest x2 9.45 us: product(): pl.pallas_call(product_kernel, grid=(2 * steps,), in_specs=specs, out_spe...]
    unnamed x11 -> x14, local copies, waits for them, and re-layouts: 4.96 us -> 3.17 us
    ppermute x6, waiting for transfers between devices: 10.9 us -> 9.16 us  [to_x(): return lax.ppermute(array, 'mp', [(i, (i + step) % NX) for i in range(NX)])]
    pallas_call x8, Pallas kernels: 9.72 us -> 8.11 us  [local(): pl.pallas_call(body, in_specs=[SMEM] + [VMEM] * len(operands), out_specs=...]
    ppermute x4 -> x7, waiting for transfers between devices: 3.28 us -> 2.96 us  [to_core(): return lax.ppermute(array, 'dp', dp_shift(0, 0, 1))]
  transfers between devices with their start and end apart: 24 -> 27, of which waited for: 13 -> 16; matrix products, arithmetic and copies ran while one was open for 10% -> 5% of each run, Pallas kernels for 17% -> 13%
where the time goes in v2:
time: 120 us
  waiting for transfers between devices  51.8 us (43%)
  starting transfers between devices  38.7 us (32%)
  Pallas kernels  19.9 us (17%)
  local copies, waits for them, and re-layouts  6.05 us (5%)
  other arithmetic  2.78 us (2%)
    ppermute x12, waiting for transfers between devices, exchange(): lax.ppermute(array, 'dp', dp_shift(*move))  31.4 us
    ppermute x12, starting transfers between devices, exchange(): lax.ppermute(array, 'dp', dp_shift(*move))  25.8 us
    ppermute x6, starting transfers between devices, to_x(): return lax.ppermute(array, 'mp', [(i, (i + step) % NX) for i in range(NX)])  9.77 us
    pallas_call x2, Pallas kernels, product(): pl.pallas_call(product_kernel, grid=(2 * steps,), in_specs=specs, out_spe...  9.45 us
    ppermute x6, waiting for transfers between devices, to_x(): return lax.ppermute(array, 'mp', [(i, (i + step) % NX) for i in range(NX)])  9.16 us
    ppermute x2, waiting for transfers between devices, swap_z(): return lax.ppermute(array, 'dp', pairs)  8.22 us
    pallas_call x8, Pallas kernels, local(): pl.pallas_call(body, in_specs=[SMEM] + [VMEM] * len(operands), out_specs=...  8.11 us
    unnamed x14, local copies, waits for them, and re-layouts  3.17 us
  transfers between devices with their start and end apart: 27, of which 16 were waited for; matrix products, arithmetic and copies ran while one was open for 5% of the time, Pallas kernels for 13%

profile of v2, /device:TPU:8, one launch (start us, length us, event | category | flops | bytes accessed | tf_op | source)
XLA Modules:
  0.0 120.0 jit_solution(15586358263939420302)
XLA Ops:
  0.6 2.8 %collective-permute-start.1 = (bf16[128,12288]{1,0:T(8,128)(2,1)}, bf16[128,12288]{1,0:T(8,128)(2,1)S(1)}, u32[]{:S(2)}, u32[]{:S(2)}) collective-permute-start(bf16[128,12288]{1,0:T(8,128)(2,1)} %own.3), channel_id=1, source_target_pairs={{0,3},{1,0},{2,1},{3,2},{4,7},{5,4},{6,5},{7,6},{8,11},{9,8},{10,9... | collective-permute-start | bytes 9437192 | tf_op jit(solution)/shard_map/ppermute | solution.py:39
  3.5 2.1 %dynamic-slice_bitcast_fusion = bf16[32,12288]{1,0:T(8,128)(2,1)} fusion(bf16[1,64,12288]{2,1,0:T(8,128)(2,1)} %grad.1, s32[]{:T(128)S(6)} %select_n.66), kind=kLoop, calls=%fused_computation | loop fusion | bytes 1572868 | tf_op jit(solution)/shard_map/dynamic_slice | solution.py:244
  5.6 2.5 %collective-permute-done.2.theirs = bf16[32,12288]{1,0:T(8,128)(2,1)} collective-permute-done((bf16[32,12288]{1,0:T(8,128)(2,1)}, bf16[32,12288]{1,0:T(8,128)(2,1)}, u32[]{:S(2)}, u32[]{:S(2)}) %collective-permute-start.2) | collective-permute-done | bytes 786464 | tf_op jit(solution)/shard_map/ppermute | solution.py:35
  8.2 1.4 %copy-done.1 = bf16[1,64,12288]{2,1,0:T(8,128)(2,1)S(1)} copy-done((bf16[1,64,12288]{2,1,0:T(8,128)(2,1)S(1)}, bf16[1,64,12288]{2,1,0:T(8,128)(2,1)}, u32[]{:S(2)}) %copy-start.1) | copy-done | bytes 1572888
  9.6 2.1 %shard_map.101 = (f32[32,3072]{1,0:T(8,128)S(1)}, f32[32,3072]{1,0:T(8,128)S(1)}, f32[32,3072]{1,0:T(8,128)}, f32[32,3072]{1,0:T(8,128)}) custom-call(s32[6]{0:T(128)S(1)} %stack.39.place, bf16[1,64,12288]{2,1,0:T(8,128)(2,1)S(1)} %copy-done.1, bf16[32,12288]{1,0:T(8,128)(2,1)} %collective-permute-done.2.theirs), custom_call_target="tpu_custom_call" | custom-call | flops 1024 | bytes 1024 | tf_op jit(solution)/shard_map/pallas_call | solution.py:118
  11.7 1.6 %collective-permute-start.3 = (f32[32,3072]{1,0:T(8,128)S(1)}, f32[32,3072]{1,0:T(8,128)S(1)}, u32[]{:S(2)}, u32[]{:S(2)}) collective-permute-start(f32[32,3072]{1,0:T(8,128)S(1)} %get-tuple-element.39), channel_id=1, source_target_pairs={{0,64},{4,68},{8,72},{12,76},{16,80},{20,84},{24,88},{28,92},{32,9... | collective-permute-start | bytes 1179656 | tf_op jit(solution)/shard_map/ppermute | solution.py:105
  13.3 1.9 %collective-permute-start.4 = (f32[32,3072]{1,0:T(8,128)}, f32[32,3072]{1,0:T(8,128)}, u32[]{:S(2)}, u32[]{:S(2)}) collective-permute-start(f32[32,3072]{1,0:T(8,128)} %get-tuple-element.40), channel_id=1, source_target_pairs={{0,128},{4,132},{8,136},{12,140},{16,144},{20,148},{24,152},{28,15... | collective-permute-start | bytes 1179656 | tf_op jit(solution)/shard_map/ppermute | solution.py:105
  15.2 1.4 %collective-permute-start.5 = (f32[32,3072]{1,0:T(8,128)}, f32[32,3072]{1,0:T(8,128)}, u32[]{:S(2)}, u32[]{:S(2)}) collective-permute-start(f32[32,3072]{1,0:T(8,128)} %get-tuple-element.41), channel_id=1, source_target_pairs={{0,192},{4,196},{8,200},{12,204},{16,208},{20,212},{24,216},{28,22... | collective-permute-start | bytes 1179656 | tf_op jit(solution)/shard_map/ppermute | solution.py:105
  18.3 5.4 %collective-permute-done.3.b = f32[32,3072]{1,0:T(8,128)S(1)} collective-permute-done((f32[32,3072]{1,0:T(8,128)S(1)}, f32[32,3072]{1,0:T(8,128)S(1)}, u32[]{:S(2)}, u32[]{:S(2)}) %collective-permute-start.3) | collective-permute-done | bytes 393248 | tf_op jit(solution)/shard_map/ppermute | solution.py:105
  24.4 2.7 %collective-permute-done.4.c = f32[32,3072]{1,0:T(8,128)} collective-permute-done((f32[32,3072]{1,0:T(8,128)}, f32[32,3072]{1,0:T(8,128)}, u32[]{:S(2)}, u32[]{:S(2)}) %collective-permute-start.4) | collective-permute-done | bytes 393248 | tf_op jit(solution)/shard_map/ppermute | solution.py:105
  27.1 7.3 %collective-permute-done.5.d = f32[32,3072]{1,0:T(8,128)} collective-permute-done((f32[32,3072]{1,0:T(8,128)}, f32[32,3072]{1,0:T(8,128)}, u32[]{:S(2)}, u32[]{:S(2)}) %collective-permute-start.5) | collective-permute-done | bytes 393248 | tf_op jit(solution)/shard_map/ppermute | solution.py:105
  38.8 4.8 %collective-permute-done.6.b = f32[32,1536]{1,0:T(8,128)S(1)} collective-permute-done((f32[32,1536]{1,0:T(8,128)S(1)}, f32[32,1536]{1,0:T(8,128)S(1)}, u32[]{:S(2)}, u32[]{:S(2)}) %collective-permute-start.6) | collective-permute-done | bytes 196640 | tf_op jit(solution)/shard_map/ppermute | solution.py:110
  44.1 1.9 %collective-permute-start.7 = (f32[32,384]{1,0:T(8,128)S(1)}, f32[32,384]{1,0:T(8,128)S(1)}, u32[]{:S(2)}, u32[]{:S(2)}) collective-permute-start(f32[32,384]{1,0:T(8,128)S(1)} %get-tuple-element.45), channel_id=1, source_target_pairs={{0,16},{4,20},{8,24},{12,28},{16,32},{20,36},{24,40},{28,44},{32,4... | collective-permute-start | bytes 147464 | tf_op jit(solution)/shard_map/ppermute | solution.py:105
  46.0 5.2 %collective-permute-start.8 = (f32[32,384]{1,0:T(8,128)S(1)}, f32[32,384]{1,0:T(8,128)S(1)}, u32[]{:S(2)}, u32[]{:S(2)}) collective-permute-start(f32[32,384]{1,0:T(8,128)S(1)} %get-tuple-element.46), channel_id=1, source_target_pairs={{0,32},{4,36},{8,40},{12,44},{16,48},{20,52},{24,56},{28,60},{32,0... | collective-permute-start | bytes 147464 | tf_op jit(solution)/shard_map/ppermute | solution.py:105
  51.2 2.7 %collective-permute-start.9 = (f32[32,384]{1,0:T(8,128)S(1)}, f32[32,384]{1,0:T(8,128)S(1)}, u32[]{:S(2)}, u32[]{:S(2)}) collective-permute-start(f32[32,384]{1,0:T(8,128)S(1)} %get-tuple-element.47), channel_id=1, source_target_pairs={{0,48},{4,52},{8,56},{12,60},{16,0},{20,4},{24,8},{28,12},{32,16},... | collective-permute-start | bytes 147464 | tf_op jit(solution)/shard_map/ppermute | solution.py:105
  54.3 2.9 %collective-permute-done.9.d = f32[32,384]{1,0:T(8,128)S(1)} collective-permute-done((f32[32,384]{1,0:T(8,128)S(1)}, f32[32,384]{1,0:T(8,128)S(1)}, u32[]{:S(2)}, u32[]{:S(2)}) %collective-permute-start.9) | collective-permute-done | bytes 49184 | tf_op jit(solution)/shard_map/ppermute | solution.py:105
  57.8 3.0 %collective-permute-start.13 = (bf16[32,384]{1,0:T(8,128)(2,1)S(1)}, bf16[32,384]{1,0:T(8,128)(2,1)S(1)}, u32[]{:S(2)}, u32[]{:S(2)}) collective-permute-start(bf16[32,384]{1,0:T(8,128)(2,1)S(1)} %get-tuple-element.49.refs_0_), channel_id=1, source_target_pairs={{0,48},{4,52},{8,56},{12,60},{16,0},{20,4},{24,8},{28,12},{32,16},... | collective-permute-start | bytes 73736 | tf_op jit(solution)/shard_map/ppermute | solution.py:105
  60.8 1.8 %collective-permute-start.12 = (bf16[32,384]{1,0:T(8,128)(2,1)S(1)}, bf16[32,384]{1,0:T(8,128)(2,1)S(1)}, u32[]{:S(2)}, u32[]{:S(2)}) collective-permute-start(bf16[32,384]{1,0:T(8,128)(2,1)S(1)} %get-tuple-element.49.refs_0_), channel_id=1, source_target_pairs={{0,32},{4,36},{8,40},{12,44},{16,48},{20,52},{24,56},{28,60},{32,0... | collective-permute-start | bytes 73736 | tf_op jit(solution)/shard_map/ppermute | solution.py:105
  63.3 5.5 %collective-permute-done.12.refs_2_ = bf16[32,384]{1,0:T(8,128)(2,1)S(1)} collective-permute-done((bf16[32,384]{1,0:T(8,128)(2,1)S(1)}, bf16[32,384]{1,0:T(8,128)(2,1)S(1)}, u32[]{:S(2)}, u32[]{:S(2)}) %collective-permute-start.12) | collective-permute-done | bytes 24608 | tf_op jit(solution)/shard_map/ppermute | solution.py:105
  69.8 1.3 %collective-permute-start.14 = (bf16[32,1536]{1,0:T(8,128)(2,1)S(1)}, bf16[32,1536]{1,0:T(8,128)(2,1)S(1)}, u32[]{:S(2)}, u32[]{:S(2)}) collective-permute-start(bf16[32,1536]{1,0:T(8,128)(2,1)S(1)} %shard_map.105.mine), channel_id=1, source_target_pairs={{0,8},{4,12},{8,0},{12,4},{16,24},{20,28},{24,16},{28,20},{32,40},... | collective-permute-start | bytes 294920 | tf_op jit(solution)/shard_map/ppermute | solution.py:110
  71.1 3.4 %collective-permute-done.14.other = bf16[32,1536]{1,0:T(8,128)(2,1)S(1)} collective-permute-done((bf16[32,1536]{1,0:T(8,128)(2,1)S(1)}, bf16[32,1536]{1,0:T(8,128)(2,1)S(1)}, u32[]{:S(2)}, u32[]{:S(2)}) %collective-permute-start.14) | collective-permute-done | bytes 98336 | tf_op jit(solution)/shard_map/ppermute | solution.py:110
  74.6 1.3 %shard_map.107 = (bf16[128,5120]{1,0:T(8,128)(2,1)S(1)}, bf16[128,5120]{1,0:T(8,128)(2,1)S(1)}) custom-call(bf16[128,12288]{1,0:T(8,128)(2,1)} %collective-permute-done.before, bf16[128,12288]{1,0:T(8,128)(2,1)S(1)} %collective-permute-done.1.after), custom_call_target="tpu_custom_call" | custom-call | flops 1024 | bytes 1024 | tf_op jit(solution)/shard_map/pallas_call | solution.py:152
  76.7 2.8 %collective-permute-start.24 = (bf16[128,5120]{1,0:T(8,128)(2,1)S(1)}, bf16[128,5120]{1,0:T(8,128)(2,1)S(1)}, u32[]{:S(2)}, u32[]{:S(2)}) collective-permute-start(bf16[128,5120]{1,0:T(8,128)(2,1)S(1)} %get-tuple-element.63), channel_id=1, source_target_pairs={{0,3},{1,0},{2,1},{3,2},{4,7},{5,4},{6,5},{7,6},{8,11},{9,8},{10,9... | collective-permute-start | bytes 3932168 | tf_op jit(solution)/shard_map/ppermute | solution.py:39
  81.0 2.3 %collective-permute-start.16 = (bf16[32,3072]{1,0:T(8,128)(2,1)S(1)}, bf16[32,3072]{1,0:T(8,128)(2,1)S(1)}, u32[]{:S(2)}, u32[]{:S(2)}) collective-permute-start(bf16[32,3072]{1,0:T(8,128)(2,1)S(1)} %shard_map.108.refs_0_), channel_id=1, source_target_pairs={{0,128},{4,132},{8,136},{12,140},{16,144},{20,148},{24,152},{28,15... | collective-permute-start | bytes 589832 | tf_op jit(solution)/shard_map/ppermute | solution.py:105
  83.3 2.5 %collective-permute-start.15 = (bf16[32,3072]{1,0:T(8,128)(2,1)S(1)}, bf16[32,3072]{1,0:T(8,128)(2,1)S(1)}, u32[]{:S(2)}, u32[]{:S(2)}) collective-permute-start(bf16[32,3072]{1,0:T(8,128)(2,1)S(1)} %shard_map.108.refs_0_), channel_id=1, source_target_pairs={{0,64},{4,68},{8,72},{12,76},{16,80},{20,84},{24,88},{28,92},{32,9... | collective-permute-start | bytes 589832 | tf_op jit(solution)/shard_map/ppermute | solution.py:105
  85.9 1.6 %collective-permute-done.17.refs_3_ = bf16[32,3072]{1,0:T(8,128)(2,1)S(1)} collective-permute-done((bf16[32,3072]{1,0:T(8,128)(2,1)S(1)}, bf16[32,3072]{1,0:T(8,128)(2,1)S(1)}, u32[]{:S(2)}, u32[]{:S(2)}) %collective-permute-start.17) | collective-permute-done | bytes 196640 | tf_op jit(solution)/shard_map/ppermute | solution.py:105
  88.5 4.4 %collective-permute-done.16.refs_2_ = bf16[32,3072]{1,0:T(8,128)(2,1)S(1)} collective-permute-done((bf16[32,3072]{1,0:T(8,128)(2,1)S(1)}, bf16[32,3072]{1,0:T(8,128)(2,1)S(1)}, u32[]{:S(2)}, u32[]{:S(2)}) %collective-permute-start.16) | collective-permute-done | bytes 196640 | tf_op jit(solution)/shard_map/ppermute | solution.py:105
  95.6 1.8 %shard_map.109 = bf16[64,12288]{1,0:T(8,128)(2,1)} custom-call(s32[6]{0:T(128)S(1)} %stack.39.place, bf16[32,3072]{1,0:T(8,128)(2,1)S(1)} %shard_map.108.refs_0_, bf16[32,3072]{1,0:T(8,128)(2,1)S(1)} %collective-permute-done.15.refs_1_, bf16[32,3072]{1,0:T(8,128)(2,1)S(1)} %collective-permute-done.16.refs_2_, ...), custom_call_target="tpu_custom_call" | custom-call | flops 1024 | bytes 1024 | tf_op jit(solution)/shard_map/pallas_call | solution.py:118
  97.4 9.1 %collective-permute-done.23.first = bf16[128,5120]{1,0:T(8,128)(2,1)S(1)} collective-permute-done((bf16[128,5120]{1,0:T(8,128)(2,1)S(1)}, bf16[128,5120]{1,0:T(8,128)(2,1)S(1)}, u32[]{:S(2)}, u32[]{:S(2)}) %collective-permute-start.23) | collective-permute-done | bytes 1310752 | tf_op jit(solution)/shard_map/ppermute | solution.py:39
  106.6 3.2 %collective-permute-start.26 = (bf16[128,1024]{1,0:T(8,128)(2,1)S(1)}, bf16[128,1024]{1,0:T(8,128)(2,1)S(1)}, u32[]{:S(2)}, u32[]{:S(2)}) collective-permute-start(bf16[128,1024]{1,0:T(8,128)(2,1)S(1)} %get-tuple-element.69), channel_id=1, source_target_pairs={{0,3},{1,0},{2,1},{3,2},{4,7},{5,4},{6,5},{7,6},{8,11},{9,8},{10,9... | collective-permute-start | bytes 786440 | tf_op jit(solution)/shard_map/ppermute | solution.py:39
  110.5 6.7 %shard_map.111.rest_0_ = bf16[1,256,12288]{2,1,0:T(8,128)(2,1)} custom-call(bf16[256,512]{1,0:T(8,128)(2,1)S(1)} %shard_map.110.lhs, bf16[128,12288]{1,0:T(8,128)(2,1)S(1)} %copy-done, bf16[128,12288]{1,0:T(8,128)(2,1)S(1)} %collective-permute-done.1.after, bf16[128,12288]{1,0:T(8,128)(2,1)} %collective-permute-done.before, ...), custom_call_target="tpu_custom_call" | custom-call | flops 2684354560 | bytes 15728640 | tf_op jit(solution)/shard_map/pallas_call | solution.py:84
  117.3 2.7 %shard_map.112 = bf16[1,256,12288]{2,1,0:T(8,128)(2,1)} custom-call(bf16[256,512]{1,0:T(8,128)(2,1)S(1)} %shard_map.110.lhs, bf16[128,12288]{1,0:T(8,128)(2,1)S(1)} %copy-done, bf16[128,12288]{1,0:T(8,128)(2,1)S(1)} %collective-permute-done.1.after, bf16[128,12288]{1,0:T(8,128)(2,1)} %collective-permute-done.before, ...), custom_call_target="tpu_custom_call", output_to_operand_aliasing={{}: (6, {})} | custom-call | flops 536870912 | bytes 3145728 | tf_op jit(solution)/shard_map/pallas_call | solution.py:84
  (60 shorter events, 16.8 us)
Async XLA Ops:
  0.6 73.9 %collective-permute-start.1 = (bf16[128,12288]{1,0:T(8,128)(2,1)}, bf16[128,12288]{1,0:T(8,128)(2,1)S(1)}, u32[]{:S(2)}, u32[]{:S(2)}) collective-permute-start(bf16[128,12288]{1,0:T(8,128)(2,1)} %own.3), channel_id=1, source_target_pairs={{0,3},{1,0},{2,1},{3,2},{4,7},{5,4},{6,5},{7,6},{8,11},{9,8},{10,9... | collective-permute-start | bytes 9437192 | tf_op jit(solution)/shard_map/ppermute | solution.py:39
  3.5 71.1 %collective-permute-start = (bf16[128,12288]{1,0:T(8,128)(2,1)}, bf16[128,12288]{1,0:T(8,128)(2,1)}, u32[]{:S(2)}, u32[]{:S(2)}) collective-permute-start(bf16[128,12288]{1,0:T(8,128)(2,1)} %own.3), channel_id=1, source_target_pairs={{0,1},{1,2},{2,3},{3,0},{4,5},{5,6},{6,7},{7,4},{8,9},{9,10},{10,1... | collective-permute-start | bytes 9437192 | tf_op jit(solution)/shard_map/ppermute | solution.py:39
  5.5 2.6 %collective-permute-start.2 = (bf16[32,12288]{1,0:T(8,128)(2,1)}, bf16[32,12288]{1,0:T(8,128)(2,1)}, u32[]{:S(2)}, u32[]{:S(2)}) collective-permute-start(bf16[32,12288]{1,0:T(8,128)(2,1)} %dynamic-slice_bitcast_fusion), channel_id=1, source_target_pairs={{0,4},{4,0},{8,12},{12,8},{16,20},{20,16},{24,28},{28,24},{32,36},... | collective-permute-start | bytes 2359304 | tf_op jit(solution)/shard_map/ppermute | solution.py:35
  8.2 1.4 %copy-start.1 = (bf16[1,64,12288]{2,1,0:T(8,128)(2,1)S(1)}, bf16[1,64,12288]{2,1,0:T(8,128)(2,1)}, u32[]{:S(2)}) copy-start(bf16[1,64,12288]{2,1,0:T(8,128)(2,1)} %grad.1) | copy-start | bytes 4718596
  11.7 12.0 %collective-permute-start.3 = (f32[32,3072]{1,0:T(8,128)S(1)}, f32[32,3072]{1,0:T(8,128)S(1)}, u32[]{:S(2)}, u32[]{:S(2)}) collective-permute-start(f32[32,3072]{1,0:T(8,128)S(1)} %get-tuple-element.39), channel_id=1, source_target_pairs={{0,64},{4,68},{8,72},{12,76},{16,80},{20,84},{24,88},{28,92},{32,9... | collective-permute-start | bytes 1179656 | tf_op jit(solution)/shard_map/ppermute | solution.py:105
  13.3 13.9 %collective-permute-start.4 = (f32[32,3072]{1,0:T(8,128)}, f32[32,3072]{1,0:T(8,128)}, u32[]{:S(2)}, u32[]{:S(2)}) collective-permute-start(f32[32,3072]{1,0:T(8,128)} %get-tuple-element.40), channel_id=1, source_target_pairs={{0,128},{4,132},{8,136},{12,140},{16,144},{20,148},{24,152},{28,15... | collective-permute-start | bytes 1179656 | tf_op jit(solution)/shard_map/ppermute | solution.py:105
  15.2 19.2 %collective-permute-start.5 = (f32[32,3072]{1,0:T(8,128)}, f32[32,3072]{1,0:T(8,128)}, u32[]{:S(2)}, u32[]{:S(2)}) collective-permute-start(f32[32,3072]{1,0:T(8,128)} %get-tuple-element.41), channel_id=1, source_target_pairs={{0,192},{4,196},{8,200},{12,204},{16,208},{20,212},{24,216},{28,22... | collective-permute-start | bytes 1179656 | tf_op jit(solution)/shard_map/ppermute | solution.py:105
  17.5 6.1 %copy-start.5 = (f32[3,64,192]{2,1,0:T(8,128)}, f32[3,64,192]{2,1,0:T(8,128)S(1)}, u32[]{:S(2)}) copy-start(f32[3,64,192]{2,1,0:T(8,128)S(1)} %pad_maximum_fusion) | copy-start | bytes 442372
  24.4 13.5 %collective-permute-start.10 = (f32[3,32,192]{2,1,0:T(8,128)}, f32[3,32,192]{2,1,0:T(8,128)}, u32[]{:S(2)}, u32[]{:S(2)}) collective-permute-start(f32[3,32,192]{2,1,0:T(8,128)} %constant_dynamic-slice_fusion), channel_id=1, source_target_pairs={{0,4},{4,0},{8,12},{12,8},{16,20},{20,16},{24,28},{28,24},{32,36},... | collective-permute-start | bytes 221192 | tf_op jit(solution)/shard_map/ppermute | solution.py:35
  35.4 2.5 %copy-start.6 = (f32[3,64,192]{2,1,0:T(8,128)S(1)}, f32[3,64,192]{2,1,0:T(8,128)}, u32[]{:S(2)}) copy-start(f32[3,64,192]{2,1,0:T(8,128)} %copy-done.5) | copy-start | bytes 442372
  36.6 6.9 %collective-permute-start.6 = (f32[32,1536]{1,0:T(8,128)S(1)}, f32[32,1536]{1,0:T(8,128)S(1)}, u32[]{:S(2)}, u32[]{:S(2)}) collective-permute-start(f32[32,1536]{1,0:T(8,128)S(1)} %get-tuple-element.43), channel_id=1, source_target_pairs={{0,8},{4,12},{8,0},{12,4},{16,24},{20,28},{24,16},{28,20},{32,40},... | collective-permute-start | bytes 589832 | tf_op jit(solution)/shard_map/ppermute | solution.py:110
  44.1 9.9 %collective-permute-start.7 = (f32[32,384]{1,0:T(8,128)S(1)}, f32[32,384]{1,0:T(8,128)S(1)}, u32[]{:S(2)}, u32[]{:S(2)}) collective-permute-start(f32[32,384]{1,0:T(8,128)S(1)} %get-tuple-element.45), channel_id=1, source_target_pairs={{0,16},{4,20},{8,24},{12,28},{16,32},{20,36},{24,40},{28,44},{32,4... | collective-permute-start | bytes 147464 | tf_op jit(solution)/shard_map/ppermute | solution.py:105
  46.0 8.2 %collective-permute-start.8 = (f32[32,384]{1,0:T(8,128)S(1)}, f32[32,384]{1,0:T(8,128)S(1)}, u32[]{:S(2)}, u32[]{:S(2)}) collective-permute-start(f32[32,384]{1,0:T(8,128)S(1)} %get-tuple-element.46), channel_id=1, source_target_pairs={{0,32},{4,36},{8,40},{12,44},{16,48},{20,52},{24,56},{28,60},{32,0... | collective-permute-start | bytes 147464 | tf_op jit(solution)/shard_map/ppermute | solution.py:105
  51.2 5.9 %collective-permute-start.9 = (f32[32,384]{1,0:T(8,128)S(1)}, f32[32,384]{1,0:T(8,128)S(1)}, u32[]{:S(2)}, u32[]{:S(2)}) collective-permute-start(f32[32,384]{1,0:T(8,128)S(1)} %get-tuple-element.47), channel_id=1, source_target_pairs={{0,48},{4,52},{8,56},{12,60},{16,0},{20,4},{24,8},{28,12},{32,16},... | collective-permute-start | bytes 147464 | tf_op jit(solution)/shard_map/ppermute | solution.py:105
  57.8 5.5 %collective-permute-start.13 = (bf16[32,384]{1,0:T(8,128)(2,1)S(1)}, bf16[32,384]{1,0:T(8,128)(2,1)S(1)}, u32[]{:S(2)}, u32[]{:S(2)}) collective-permute-start(bf16[32,384]{1,0:T(8,128)(2,1)S(1)} %get-tuple-element.49.refs_0_), channel_id=1, source_target_pairs={{0,48},{4,52},{8,56},{12,60},{16,0},{20,4},{24,8},{28,12},{32,16},... | collective-permute-start | bytes 73736 | tf_op jit(solution)/shard_map/ppermute | solution.py:105
  60.8 8.0 %collective-permute-start.12 = (bf16[32,384]{1,0:T(8,128)(2,1)S(1)}, bf16[32,384]{1,0:T(8,128)(2,1)S(1)}, u32[]{:S(2)}, u32[]{:S(2)}) collective-permute-start(bf16[32,384]{1,0:T(8,128)(2,1)S(1)} %get-tuple-element.49.refs_0_), channel_id=1, source_target_pairs={{0,32},{4,36},{8,40},{12,44},{16,48},{20,52},{24,56},{28,60},{32,0... | collective-permute-start | bytes 73736 | tf_op jit(solution)/shard_map/ppermute | solution.py:105
  62.6 6.7 %collective-permute-start.11 = (bf16[32,384]{1,0:T(8,128)(2,1)S(1)}, bf16[32,384]{1,0:T(8,128)(2,1)S(1)}, u32[]{:S(2)}, u32[]{:S(2)}) collective-permute-start(bf16[32,384]{1,0:T(8,128)(2,1)S(1)} %get-tuple-element.49.refs_0_), channel_id=1, source_target_pairs={{0,16},{4,20},{8,24},{12,28},{16,32},{20,36},{24,40},{28,44},{32,4... | collective-permute-start | bytes 73736 | tf_op jit(solution)/shard_map/ppermute | solution.py:105
  69.8 4.7 %collective-permute-start.14 = (bf16[32,1536]{1,0:T(8,128)(2,1)S(1)}, bf16[32,1536]{1,0:T(8,128)(2,1)S(1)}, u32[]{:S(2)}, u32[]{:S(2)}) collective-permute-start(bf16[32,1536]{1,0:T(8,128)(2,1)S(1)} %shard_map.105.mine), channel_id=1, source_target_pairs={{0,8},{4,12},{8,0},{12,4},{16,24},{20,28},{24,16},{28,20},{32,40},... | collective-permute-start | bytes 294920 | tf_op jit(solution)/shard_map/ppermute | solution.py:110
  75.9 30.6 %collective-permute-start.23 = (bf16[128,5120]{1,0:T(8,128)(2,1)S(1)}, bf16[128,5120]{1,0:T(8,128)(2,1)S(1)}, u32[]{:S(2)}, u32[]{:S(2)}) collective-permute-start(bf16[128,5120]{1,0:T(8,128)(2,1)S(1)} %get-tuple-element.62), channel_id=1, source_target_pairs={{0,1},{1,2},{2,3},{3,0},{4,5},{5,6},{6,7},{7,4},{8,9},{9,10},{10,1... | collective-permute-start | bytes 3932168 | tf_op jit(solution)/shard_map/ppermute | solution.py:39
  76.7 29.8 %collective-permute-start.24 = (bf16[128,5120]{1,0:T(8,128)(2,1)S(1)}, bf16[128,5120]{1,0:T(8,128)(2,1)S(1)}, u32[]{:S(2)}, u32[]{:S(2)}) collective-permute-start(bf16[128,5120]{1,0:T(8,128)(2,1)S(1)} %get-tuple-element.63), channel_id=1, source_target_pairs={{0,3},{1,0},{2,1},{3,2},{4,7},{5,4},{6,5},{7,6},{8,11},{9,8},{10,9... | collective-permute-start | bytes 3932168 | tf_op jit(solution)/shard_map/ppermute | solution.py:39
  80.1 3.2 %collective-permute-start.18 = (bf16[32,3072]{1,0:T(8,128)(2,1)S(1)}, bf16[32,3072]{1,0:T(8,128)(2,1)S(1)}, u32[]{:S(2)}, u32[]{:S(2)}) collective-permute-start(bf16[32,3072]{1,0:T(8,128)(2,1)S(1)} %shard_map.108.refs_0_), channel_id=1, source_target_pairs={{0,4},{4,0},{8,12},{12,8},{16,20},{20,16},{24,28},{28,24},{32,36},... | collective-permute-start | bytes 589832 | tf_op jit(solution)/shard_map/ppermute | solution.py:35
  80.2 7.3 %collective-permute-start.17 = (bf16[32,3072]{1,0:T(8,128)(2,1)S(1)}, bf16[32,3072]{1,0:T(8,128)(2,1)S(1)}, u32[]{:S(2)}, u32[]{:S(2)}) collective-permute-start(bf16[32,3072]{1,0:T(8,128)(2,1)S(1)} %shard_map.108.refs_0_), channel_id=1, source_target_pairs={{0,192},{4,196},{8,200},{12,204},{16,208},{20,212},{24,216},{28,22... | collective-permute-start | bytes 589832 | tf_op jit(solution)/shard_map/ppermute | solution.py:105
  81.0 11.9 %collective-permute-start.16 = (bf16[32,3072]{1,0:T(8,128)(2,1)S(1)}, bf16[32,3072]{1,0:T(8,128)(2,1)S(1)}, u32[]{:S(2)}, u32[]{:S(2)}) collective-permute-start(bf16[32,3072]{1,0:T(8,128)(2,1)S(1)} %shard_map.108.refs_0_), channel_id=1, source_target_pairs={{0,128},{4,132},{8,136},{12,140},{16,144},{20,148},{24,152},{28,15... | collective-permute-start | bytes 589832 | tf_op jit(solution)/shard_map/ppermute | solution.py:105
  83.3 10.5 %collective-permute-start.15 = (bf16[32,3072]{1,0:T(8,128)(2,1)S(1)}, bf16[32,3072]{1,0:T(8,128)(2,1)S(1)}, u32[]{:S(2)}, u32[]{:S(2)}) collective-permute-start(bf16[32,3072]{1,0:T(8,128)(2,1)S(1)} %shard_map.108.refs_0_), channel_id=1, source_target_pairs={{0,64},{4,68},{8,72},{12,76},{16,80},{20,84},{24,88},{28,92},{32,9... | collective-permute-start | bytes 589832 | tf_op jit(solution)/shard_map/ppermute | solution.py:105
  87.5 6.3 %collective-permute-start.22 = (f32[3,32,192]{2,1,0:T(8,128)S(1)}, f32[3,32,192]{2,1,0:T(8,128)S(1)}, u32[]{:S(2)}, u32[]{:S(2)}) collective-permute-start(f32[3,32,192]{2,1,0:T(8,128)S(1)} %slice_select_fusion), channel_id=1, source_target_pairs={{0,4},{4,0},{8,12},{12,8},{16,20},{20,16},{24,28},{28,24},{32,36},... | collective-permute-start | bytes 221192 | tf_op jit(solution)/shard_map/ppermute | solution.py:35
  92.9 2.3 %collective-permute-start.21 = (bf16[32,3072]{1,0:T(8,128)(2,1)S(1)}, bf16[32,3072]{1,0:T(8,128)(2,1)S(1)}, u32[]{:S(2)}, u32[]{:S(2)}) collective-permute-start(bf16[32,3072]{1,0:T(8,128)(2,1)S(1)} %collective-permute-done.17.refs_3_), channel_id=1, source_target_pairs={{0,4},{4,0},{8,12},{12,8},{16,20},{20,16},{24,28},{28,24},{32,36},... | collective-permute-start | bytes 589832 | tf_op jit(solution)/shard_map/ppermute | solution.py:35
  93.8 1.4 %collective-permute-start.20 = (bf16[32,3072]{1,0:T(8,128)(2,1)S(1)}, bf16[32,3072]{1,0:T(8,128)(2,1)S(1)}, u32[]{:S(2)}, u32[]{:S(2)}) collective-permute-start(bf16[32,3072]{1,0:T(8,128)(2,1)S(1)} %collective-permute-done.16.refs_2_), channel_id=1, source_target_pairs={{0,4},{4,0},{8,12},{12,8},{16,20},{20,16},{24,28},{28,24},{32,36},... | collective-permute-start | bytes 589832 | tf_op jit(solution)/shard_map/ppermute | solution.py:35
  93.9 1.7 %collective-permute-start.19 = (bf16[32,3072]{1,0:T(8,128)(2,1)S(1)}, bf16[32,3072]{1,0:T(8,128)(2,1)S(1)}, u32[]{:S(2)}, u32[]{:S(2)}) collective-permute-start(bf16[32,3072]{1,0:T(8,128)(2,1)S(1)} %collective-permute-done.15.refs_1_), channel_id=1, source_target_pairs={{0,4},{4,0},{8,12},{12,8},{16,20},{20,16},{24,28},{28,24},{32,36},... | collective-permute-start | bytes 589832 | tf_op jit(solution)/shard_map/ppermute | solution.py:35
  94.5 15.4 %copy-start.4 = (bf16[512,256]{1,0:T(8,128)(2,1)S(1)}, bf16[512,256]{1,0:T(8,128)(2,1)}, u32[]{:S(2)}) copy-start(bf16[512,256]{1,0:T(8,128)(2,1)} %out_grads.1) | copy-start | bytes 786436
  95.2 15.4 %copy-start = (bf16[128,12288]{1,0:T(8,128)(2,1)S(1)}, bf16[128,12288]{1,0:T(8,128)(2,1)}, u32[]{:S(2)}) copy-start(bf16[128,12288]{1,0:T(8,128)(2,1)} %own.3) | copy-start | bytes 9437188
  106.5 10.7 %collective-permute-start.25 = (bf16[128,1024]{1,0:T(8,128)(2,1)S(1)}, bf16[128,1024]{1,0:T(8,128)(2,1)S(1)}, u32[]{:S(2)}, u32[]{:S(2)}) collective-permute-start(bf16[128,1024]{1,0:T(8,128)(2,1)S(1)} %get-tuple-element.68), channel_id=1, source_target_pairs={{0,1},{1,2},{2,3},{3,0},{4,5},{5,6},{6,7},{7,4},{8,9},{9,10},{10,1... | collective-permute-start | bytes 786440 | tf_op jit(solution)/shard_map/ppermute | solution.py:39
  106.6 10.6 %collective-permute-start.26 = (bf16[128,1024]{1,0:T(8,128)(2,1)S(1)}, bf16[128,1024]{1,0:T(8,128)(2,1)S(1)}, u32[]{:S(2)}, u32[]{:S(2)}) collective-permute-start(bf16[128,1024]{1,0:T(8,128)(2,1)S(1)} %get-tuple-element.69), channel_id=1, source_target_pairs={{0,3},{1,0},{2,1},{3,2},{4,7},{5,4},{6,5},{7,6},{8,11},{9,8},{10,9... | collective-permute-start | bytes 786440 | tf_op jit(solution)/shard_map/ppermute | solution.py:39
  (2 other events, 1.8 us)

commit v3 on v2

--- a/solution.py
+++ b/solution.py
@@ -17,26 +17,20 @@
 
 NY, NZ, NC, NX = 4, 8, 2, 4
 D = 12288
-PIECES = ((0, 5120), (10240, 1024))
+PIECES = ((0, 4608), (9216, 1536))
 VMEM_LIMIT = 20 * 1024 * 1024
 
 
-def dp_shift(dy, dz, dc):
-    pairs = []
-    for y in range(NY):
-        for z in range(NZ):
-            for c in range(NC):
-                target = (((y + dy) % NY) * NZ + (z + dz) % NZ) * NC + (c + dc) % NC
-                pairs.append(((y * NZ + z) * NC + c, target))
-    return pairs
+def dp_swap(dy, dz, dc):
+    return [(i, i ^ ((dy * NZ + dz) * NC + dc)) for i in range(NY * NZ * NC)]
 
 
 def to_core(array):
-    return lax.ppermute(array, "dp", dp_shift(0, 0, 1))
-
-
-def to_x(array, step):
-    return lax.ppermute(array, "mp", [(i, (i + step) % NX) for i in range(NX)])
+    return lax.ppermute(array, "dp", dp_swap(0, 0, 1))
+
+
+def swap_x(array, bits):
+    return lax.ppermute(array, "mp", [(i, i ^ bits) for i in range(NX)])
 
 
 def columns(array, index, width):
@@ -48,7 +42,7 @@
     step, half_way = pl.program_id(0), pl.num_programs(0) // 2
 
     def columns_of(opposite):
-        tokens = jnp.concatenate([own[...], after[...], opposite[...], before[...]], axis=0)
+        tokens = jnp.concatenate([own[...], before[...], opposite[...], after[...]], axis=0)
         out[0] = jnp.dot(lhs[...], tokens, preferred_element_type=jnp.float32).astype(jnp.bfloat16)
 
     @pl.when(step < half_way)
@@ -102,12 +96,11 @@
 
 
 def exchange(sends, moves):
-    return [lax.ppermute(array, "dp", dp_shift(*move)) for array, move in zip(sends, moves, strict=True)]
+    return [lax.ppermute(array, "dp", dp_swap(*move)) for array, move in zip(sends, moves, strict=True)]
 
 
 def swap_z(array):
-    pairs = [(i, i ^ NC) for i in range(NY * NZ * NC)]
-    return lax.ppermute(array, "dp", pairs)
+    return lax.ppermute(array, "dp", dp_swap(0, 1, 0))
 
 
 VMEM = pl.BlockSpec(memory_space=pltpu.VMEM)
@@ -162,16 +155,40 @@
 
 def turn(place, out_grads, out):
     for step in range(NX):
-        owner = lax.rem(place[5] + step, NX)
+        owner = place[5] ^ step
         rows = pl.ds(pl.multiple_of(owner * 128, 128), 128)
         out[:, step * 128 : (step + 1) * 128] = out_grads[rows, :].T
 
 
-def add_cores(place, grad, theirs, *outs):
-    core, y = place[0], place[1]
+def halves_kernel(place, grads, mine, sent, sems):
+    core = place[0]
+    copies = [
+        pltpu.make_async_copy(grads.at[0, half(1 - core), :], sent, sems.at[0]),
+        pltpu.make_async_copy(grads.at[0, half(core), :], mine, sems.at[1]),
+    ]
+    for copy in copies:
+        copy.start()
+    for copy in copies:
+        copy.wait()
+
+
+def halves(place, grads):
+    shape = jax.ShapeDtypeStruct((32, D), jnp.bfloat16)
+    return pl.pallas_call(
+        halves_kernel,
+        in_specs=[SMEM, pl.BlockSpec(memory_space=pltpu.HBM)],
+        out_specs=[VMEM, VMEM],
+        out_shape=[shape, shape],
+        scratch_shapes=[pltpu.SemaphoreType.DMA((2,))],
+        cost_estimate=pl.CostEstimate(flops=1024, bytes_accessed=1024, transcendentals=0),
+        compiler_params=pltpu.CompilerParams(vmem_limit_bytes=8 * 1024 * 1024),
+    )(place, grads)
+
+
+def add_cores(place, mine, theirs, *outs):
     for k, out in enumerate(outs):
-        piece = at(lax.rem(y + k, NY), 3072)
-        out[...] = grad[0, half(core), piece].astype(jnp.float32) + theirs[:, piece].astype(jnp.float32)
+        piece = at(place[1] ^ k, 3072)
+        out[...] = mine[:, piece].astype(jnp.float32) + theirs[:, piece].astype(jnp.float32)
 
 
 def add_y(place, a, b, c, d, kept, sent):
@@ -185,7 +202,7 @@
 def add_pair(place, a, b, *outs):
     q = place[3]
     for k, out in enumerate(outs):
-        piece = at(lax.rem(q + k, 4), 384)
+        piece = at(q ^ k, 384)
         out[...] = a[:, piece] + b[:, piece]
 
 
@@ -207,7 +224,7 @@
     width = parts[0].shape[1]
     here = place[3] if width == 384 else place[1]
     for k, part in enumerate(parts):
-        out[:, at(lax.rem(here + 4 - k, 4), width)] = part[...]
+        out[:, at(here ^ k, width)] = part[...]
 
 
 def join_pair(place, mine, other, out):
@@ -222,7 +239,7 @@
     *parts, out = refs
     core, y = place[0], place[1]
     for k in range(NY):
-        piece = at(lax.rem(y + NY - k, NY), 3072)
+        piece = at(y ^ k, 3072)
         out[half(core), piece] = parts[k][...]
         out[half(1 - core), piece] = parts[NY + k][...]
 
@@ -237,18 +254,19 @@
     place = jnp.stack([core, y, z, z // 2, z % 2, x]).astype(jnp.int32)
     f32, bf16 = jnp.float32, jnp.bfloat16
 
-    before = to_x(inputs, 1)
-    after = to_x(inputs, -1)
+    before = swap_x(inputs, 1)
+    after = swap_x(inputs, 3)
     (lhs,) = local(turn, place, (out_grads,), [((256, 512), bf16)])
 
-    theirs = to_core(lax.dynamic_slice_in_dim(grads[0], (1 - core) * 32, 32, axis=0))
+    mine, sent = halves(place, grads)
+    theirs = to_core(sent)
 
     state = jnp.stack([master, moment, second])
     kept = lax.dynamic_slice_in_dim(state, core * 32, 32, axis=1)
     got = to_core(after_that(lax.dynamic_slice_in_dim(state, (1 - core) * 32, 32, axis=1), theirs))
     state = jnp.concatenate([jnp.where(first, kept, got), jnp.where(first, got, kept)], axis=2)
 
-    kept, *sent = local(add_cores, place, (grads, theirs), [((32, 3072), f32)] * 4)
+    kept, *sent = local(add_cores, place, (mine, theirs), [((32, 3072), f32)] * 4)
     got = exchange(sent, [(k, 0, 0) for k in (1, 2, 3)])
     kept, sent = local(add_y, place, (kept, *got), [((32, 1536), f32)] * 2)
     got = swap_z(sent)
@@ -258,17 +276,20 @@
 
     got = exchange([own] * 3, [(0, 2 * k, 0) for k in (1, 2, 3)])
     (own,) = local(join_ring, place, (own, *got), [((32, 1536), bf16)])
+
+    before, after, own = lax.optimization_barrier((before, after, own))
+    near = cut(PIECES[:1], before, after)
+    *near, own = lax.optimization_barrier((*near, own))
+    opposites = [swap_x(near[0], 3), swap_x(near[1], 1)]
+
     got = swap_z(own)
-
-    before, after, own, got = lax.optimization_barrier((before, after, own, got))
-    near = cut(PIECES[:1], before, after)
-    *near, own, got = lax.optimization_barrier((*near, own, got))
-    opposites = [to_x(near[0], 1), to_x(near[1], -1)]
-
     (own,) = local(join_pair, place, (own, got), [((32, 3072), bf16)])
     got = exchange([own] * 3, [(k, 0, 0) for k in (1, 2, 3)])
 
-    parts = [own, *got]
+    near = cut(PIECES[1:], before, after)
+    *near, got0, got1, got2 = lax.optimization_barrier((*near, *got))
+    opposites += [swap_x(near[0], 3), swap_x(near[1], 1)]
+    parts = [own, got0, got1, got2]
     others = [to_core(part) for part in parts]
     (weights,) = local(join_rows, place, (*parts, *others), [((64, D), bf16)])
 
@@ -278,14 +299,9 @@
     state = jnp.concatenate([jnp.where(first, kept, got), jnp.where(first, got, kept)], axis=1)
     state = [state[0], state[1], state[2]]
 
-    near = cut(PIECES[1:], before, after)
-    *near, weights, state[0], state[1], state[2], there = lax.optimization_barrier(
-        (*near, weights, *state, sign(*opposites))
-    )
-    opposites += [to_x(near[0], 1), to_x(near[1], -1)]
-
-    carry = product(PIECES[0][0], 2560, lhs, inputs, after, before, *opposites[:2], None, there)
-    carry = product(PIECES[1][0], 1024, lhs, inputs, after, before, *opposites[2:], carry)
+    weights, state[0], state[1], state[2], lhs = lax.optimization_barrier((weights, *state, lhs))
+    carry = product(PIECES[0][0], 2304, lhs, inputs, after, before, *opposites[:2], None)
+    carry = product(PIECES[1][0], 1536, lhs, inputs, after, before, *opposites[2:], carry)
 
     return (weights, state[0], state[1], state[2], carry)
 

time: 120 us -> 115 us (0.958)
  starting transfers between devices: 38.7 us -> 35.3 us
  local copies, waits for them, and re-layouts: 6.05 us -> 2.81 us
    ppermute x27, starting transfers between devices: 38.7 us -> 35.3 us  [the longest x12 23 us: exchange(): lax.ppermute(array, 'dp', dp_swap(*move))]
    dynamic_slice x1 -> x0, local copies, waits for them, and re-layouts: 2.06 us -> none  [per_device(): lax.dynamic_slice_in_dim(grads[0], (1 - core) * 32, 32, axis=0)]
    unnamed x14 -> x10, local copies, waits for them, and re-layouts: 3.17 us -> 2.09 us
  transfers between devices with their start and end apart: 27 -> 27, of which waited for: 16 -> 18; matrix products, arithmetic and copies ran while one was open for 5% -> 3% of each run, Pallas kernels for 13% -> 14%
where the time goes in v3:
time: 115 us
  waiting for transfers between devices  52.7 us (46%)
  starting transfers between devices  35.3 us (31%)
  Pallas kernels  20.1 us (17%)
  local copies, waits for them, and re-layouts  2.81 us (2%)
  other arithmetic  2.78 us (2%)
    ppermute x12, waiting for transfers between devices, exchange(): lax.ppermute(array, 'dp', dp_swap(*move))  31.6 us
    ppermute x12, starting transfers between devices, exchange(): lax.ppermute(array, 'dp', dp_swap(*move))  23 us
    ppermute x6, waiting for transfers between devices, swap_x(): return lax.ppermute(array, 'mp', [(i, i ^ bits) for i in range(NX)])  12.7 us
    pallas_call x2, Pallas kernels, product(): pl.pallas_call(product_kernel, grid=(2 * steps,), in_specs=specs, out_spe...  9.48 us
    pallas_call x8, Pallas kernels, local(): pl.pallas_call(body, in_specs=[SMEM] + [VMEM] * len(operands), out_specs=...  7.67 us
    ppermute x6, starting transfers between devices, swap_x(): return lax.ppermute(array, 'mp', [(i, i ^ bits) for i in range(NX)])  7.52 us
    ppermute x2, waiting for transfers between devices, swap_z(): return lax.ppermute(array, 'dp', dp_swap(0, 1, 0))  5.53 us
    ppermute x2, starting transfers between devices, swap_z(): return lax.ppermute(array, 'dp', dp_swap(0, 1, 0))  3.92 us
  transfers between devices with their start and end apart: 27, of which 18 were waited for; matrix products, arithmetic and copies ran while one was open for 3% of the time, Pallas kernels for 14%

profile of v3, /device:TPU:8, one launch (start us, length us, event | category | flops | bytes accessed | tf_op | source)
XLA Modules:
  0.0 114.5 jit_solution(11074309987428968655)
XLA Ops:
  0.6 2.8 %collective-permute-start.1 = (bf16[128,12288]{1,0:T(8,128)(2,1)}, bf16[128,12288]{1,0:T(8,128)(2,1)S(1)}, u32[]{:S(2)}, u32[]{:S(2)}) collective-permute-start(bf16[128,12288]{1,0:T(8,128)(2,1)} %own.3), channel_id=1, source_target_pairs={{0,3},{1,2},{2,1},{3,0},{4,7},{5,6},{6,5},{7,4},{8,11},{9,10},{10,... | collective-permute-start | bytes 9437192 | tf_op jit(solution)/shard_map/ppermute | solution.py:33
  3.8 1.4 %copy-done.1 = bf16[1,64,12288]{2,1,0:T(8,128)(2,1)S(1)} copy-done((bf16[1,64,12288]{2,1,0:T(8,128)(2,1)S(1)}, bf16[1,64,12288]{2,1,0:T(8,128)(2,1)}, u32[]{:S(2)}) %copy-start.1) | copy-done | bytes 1572888
  6.0 2.3 %collective-permute-done.2.theirs = bf16[32,12288]{1,0:T(8,128)(2,1)S(1)} collective-permute-done((bf16[32,12288]{1,0:T(8,128)(2,1)S(1)}, bf16[32,12288]{1,0:T(8,128)(2,1)S(1)}, u32[]{:S(2)}, u32[]{:S(2)}) %collective-permute-start.2) | collective-permute-done | bytes 786464 | tf_op jit(solution)/shard_map/ppermute | solution.py:29
  8.2 1.6 %shard_map.102 = (f32[32,3072]{1,0:T(8,128)S(1)}, f32[32,3072]{1,0:T(8,128)}, f32[32,3072]{1,0:T(8,128)}, f32[32,3072]{1,0:T(8,128)}) custom-call(s32[6]{0:T(128)S(1)} %stack.39.place, bf16[32,12288]{1,0:T(8,128)(2,1)S(1)} %get-tuple-element.41.mine, bf16[32,12288]{1,0:T(8,128)(2,1)S(1)} %collective-permute-done.2.theirs), custom_call_target="tpu_custom_call" | custom-call | flops 1024 | bytes 1024 | tf_op jit(solution)/shard_map/pallas_call | solution.py:111
  10.3 2.6 %collective-permute-start.4 = (f32[32,3072]{1,0:T(8,128)}, f32[32,3072]{1,0:T(8,128)}, u32[]{:S(2)}, u32[]{:S(2)}) collective-permute-start(f32[32,3072]{1,0:T(8,128)} %get-tuple-element.45), channel_id=1, source_target_pairs={{0,128},{4,132},{8,136},{12,140},{16,144},{20,148},{24,152},{28,15... | collective-permute-start | bytes 1179656 | tf_op jit(solution)/shard_map/ppermute | solution.py:99
  15.6 6.5 %collective-permute-done.3.b = f32[32,3072]{1,0:T(8,128)} collective-permute-done((f32[32,3072]{1,0:T(8,128)}, f32[32,3072]{1,0:T(8,128)}, u32[]{:S(2)}, u32[]{:S(2)}) %collective-permute-start.3) | collective-permute-done | bytes 393248 | tf_op jit(solution)/shard_map/ppermute | solution.py:99
  22.1 8.7 %collective-permute-done.4.c = f32[32,3072]{1,0:T(8,128)} collective-permute-done((f32[32,3072]{1,0:T(8,128)}, f32[32,3072]{1,0:T(8,128)}, u32[]{:S(2)}, u32[]{:S(2)}) %collective-permute-start.4) | collective-permute-done | bytes 393248 | tf_op jit(solution)/shard_map/ppermute | solution.py:99
  30.9 1.4 %collective-permute-done.5.d = f32[32,3072]{1,0:T(8,128)} collective-permute-done((f32[32,3072]{1,0:T(8,128)}, f32[32,3072]{1,0:T(8,128)}, u32[]{:S(2)}, u32[]{:S(2)}) %collective-permute-start.5) | collective-permute-done | bytes 393248 | tf_op jit(solution)/shard_map/ppermute | solution.py:99
  33.6 2.0 %collective-permute-start.6 = (f32[32,1536]{1,0:T(8,128)S(1)}, f32[32,1536]{1,0:T(8,128)S(1)}, u32[]{:S(2)}, u32[]{:S(2)}) collective-permute-start(f32[32,1536]{1,0:T(8,128)S(1)} %get-tuple-element.48), channel_id=1, source_target_pairs={{0,8},{4,12},{8,0},{12,4},{16,24},{20,28},{24,16},{28,20},{32,40},... | collective-permute-start | bytes 589832 | tf_op jit(solution)/shard_map/ppermute | solution.py:103
  36.5 2.8 %collective-permute-done.6.b = f32[32,1536]{1,0:T(8,128)S(1)} collective-permute-done((f32[32,1536]{1,0:T(8,128)S(1)}, f32[32,1536]{1,0:T(8,128)S(1)}, u32[]{:S(2)}, u32[]{:S(2)}) %collective-permute-start.6) | collective-permute-done | bytes 196640 | tf_op jit(solution)/shard_map/ppermute | solution.py:103
  39.9 3.4 %collective-permute-start.7 = (f32[32,384]{1,0:T(8,128)S(1)}, f32[32,384]{1,0:T(8,128)S(1)}, u32[]{:S(2)}, u32[]{:S(2)}) collective-permute-start(f32[32,384]{1,0:T(8,128)S(1)} %get-tuple-element.50), channel_id=1, source_target_pairs={{0,16},{4,20},{8,24},{12,28},{16,0},{20,4},{24,8},{28,12},{32,48},... | collective-permute-start | bytes 147464 | tf_op jit(solution)/shard_map/ppermute | solution.py:99
  43.3 5.4 %collective-permute-start.8 = (f32[32,384]{1,0:T(8,128)S(1)}, f32[32,384]{1,0:T(8,128)S(1)}, u32[]{:S(2)}, u32[]{:S(2)}) collective-permute-start(f32[32,384]{1,0:T(8,128)S(1)} %get-tuple-element.51), channel_id=1, source_target_pairs={{0,32},{4,36},{8,40},{12,44},{16,48},{20,52},{24,56},{28,60},{32,0... | collective-permute-start | bytes 147464 | tf_op jit(solution)/shard_map/ppermute | solution.py:99
  48.8 3.4 %collective-permute-done.8.c = f32[32,384]{1,0:T(8,128)S(1)} collective-permute-done((f32[32,384]{1,0:T(8,128)S(1)}, f32[32,384]{1,0:T(8,128)S(1)}, u32[]{:S(2)}, u32[]{:S(2)}) %collective-permute-start.8) | collective-permute-done | bytes 49184 | tf_op jit(solution)/shard_map/ppermute | solution.py:99
  52.2 2.7 %collective-permute-done.9.d = f32[32,384]{1,0:T(8,128)S(1)} collective-permute-done((f32[32,384]{1,0:T(8,128)S(1)}, f32[32,384]{1,0:T(8,128)S(1)}, u32[]{:S(2)}, u32[]{:S(2)}) %collective-permute-start.9) | collective-permute-done | bytes 49184 | tf_op jit(solution)/shard_map/ppermute | solution.py:99
  56.5 4.1 %collective-permute-start.12 = (bf16[32,384]{1,0:T(8,128)(2,1)S(1)}, bf16[32,384]{1,0:T(8,128)(2,1)S(1)}, u32[]{:S(2)}, u32[]{:S(2)}) collective-permute-start(bf16[32,384]{1,0:T(8,128)(2,1)S(1)} %get-tuple-element.54.refs_0_), channel_id=1, source_target_pairs={{0,32},{4,36},{8,40},{12,44},{16,48},{20,52},{24,56},{28,60},{32,0... | collective-permute-start | bytes 73736 | tf_op jit(solution)/shard_map/ppermute | solution.py:99
  60.6 1.5 %collective-permute-start.11 = (bf16[32,384]{1,0:T(8,128)(2,1)S(1)}, bf16[32,384]{1,0:T(8,128)(2,1)S(1)}, u32[]{:S(2)}, u32[]{:S(2)}) collective-permute-start(bf16[32,384]{1,0:T(8,128)(2,1)S(1)} %get-tuple-element.54.refs_0_), channel_id=1, source_target_pairs={{0,16},{4,20},{8,24},{12,28},{16,0},{20,4},{24,8},{28,12},{32,48},... | collective-permute-start | bytes 73736 | tf_op jit(solution)/shard_map/ppermute | solution.py:99
  62.1 2.1 %collective-permute-done.12.refs_2_ = bf16[32,384]{1,0:T(8,128)(2,1)S(1)} collective-permute-done((bf16[32,384]{1,0:T(8,128)(2,1)S(1)}, bf16[32,384]{1,0:T(8,128)(2,1)S(1)}, u32[]{:S(2)}, u32[]{:S(2)}) %collective-permute-start.12) | collective-permute-done | bytes 24608 | tf_op jit(solution)/shard_map/ppermute | solution.py:99
  66.0 6.0 %collective-permute-done.1.after = bf16[128,12288]{1,0:T(8,128)(2,1)S(1)} collective-permute-done((bf16[128,12288]{1,0:T(8,128)(2,1)}, bf16[128,12288]{1,0:T(8,128)(2,1)S(1)}, u32[]{:S(2)}, u32[]{:S(2)}) %collective-permute-start.1) | collective-permute-done | bytes 3145760 | tf_op jit(solution)/shard_map/ppermute | solution.py:33
  72.0 1.4 %collective-permute-done.before = bf16[128,12288]{1,0:T(8,128)(2,1)} collective-permute-done((bf16[128,12288]{1,0:T(8,128)(2,1)}, bf16[128,12288]{1,0:T(8,128)(2,1)}, u32[]{:S(2)}, u32[]{:S(2)}) %collective-permute-start) | collective-permute-done | bytes 3145760 | tf_op jit(solution)/shard_map/ppermute | solution.py:33
  74.6 1.5 %collective-permute-start.25 = (bf16[128,4608]{1,0:T(8,128)(2,1)S(1)}, bf16[128,4608]{1,0:T(8,128)(2,1)S(1)}, u32[]{:S(2)}, u32[]{:S(2)}) collective-permute-start(bf16[128,4608]{1,0:T(8,128)(2,1)S(1)} %get-tuple-element.75), channel_id=1, source_target_pairs={{0,3},{1,2},{2,1},{3,0},{4,7},{5,6},{6,5},{7,4},{8,11},{9,10},{10,... | collective-permute-start | bytes 3538952 | tf_op jit(solution)/shard_map/ppermute | solution.py:33
  76.1 1.9 %collective-permute-start.14 = (bf16[32,1536]{1,0:T(8,128)(2,1)S(1)}, bf16[32,1536]{1,0:T(8,128)(2,1)S(1)}, u32[]{:S(2)}, u32[]{:S(2)}) collective-permute-start(bf16[32,1536]{1,0:T(8,128)(2,1)S(1)} %shard_map.106.mine), channel_id=1, source_target_pairs={{0,8},{4,12},{8,0},{12,4},{16,24},{20,28},{24,16},{28,20},{32,40},... | collective-permute-start | bytes 294920 | tf_op jit(solution)/shard_map/ppermute | solution.py:103
  78.0 2.7 %collective-permute-done.14.other = bf16[32,1536]{1,0:T(8,128)(2,1)S(1)} collective-permute-done((bf16[32,1536]{1,0:T(8,128)(2,1)S(1)}, bf16[32,1536]{1,0:T(8,128)(2,1)S(1)}, u32[]{:S(2)}, u32[]{:S(2)}) %collective-permute-start.14) | collective-permute-done | bytes 98336 | tf_op jit(solution)/shard_map/ppermute | solution.py:103
  81.3 1.7 %collective-permute-start.17 = (bf16[32,3072]{1,0:T(8,128)(2,1)S(1)}, bf16[32,3072]{1,0:T(8,128)(2,1)S(1)}, u32[]{:S(2)}, u32[]{:S(2)}) collective-permute-start(bf16[32,3072]{1,0:T(8,128)(2,1)S(1)} %shard_map.108.refs_0_), channel_id=1, source_target_pairs={{0,192},{4,196},{8,200},{12,204},{16,208},{20,212},{24,216},{28,22... | collective-permute-start | bytes 589832 | tf_op jit(solution)/shard_map/ppermute | solution.py:99
  83.9 1.6 %collective-permute-start.15 = (bf16[32,3072]{1,0:T(8,128)(2,1)S(1)}, bf16[32,3072]{1,0:T(8,128)(2,1)S(1)}, u32[]{:S(2)}, u32[]{:S(2)}) collective-permute-start(bf16[32,3072]{1,0:T(8,128)(2,1)S(1)} %shard_map.108.refs_0_), channel_id=1, source_target_pairs={{0,64},{4,68},{8,72},{12,76},{16,80},{20,84},{24,88},{28,92},{32,9... | collective-permute-start | bytes 589832 | tf_op jit(solution)/shard_map/ppermute | solution.py:99
  86.5 2.8 %collective-permute-done.17.refs_3_ = bf16[32,3072]{1,0:T(8,128)(2,1)S(1)} collective-permute-done((bf16[32,3072]{1,0:T(8,128)(2,1)S(1)}, bf16[32,3072]{1,0:T(8,128)(2,1)S(1)}, u32[]{:S(2)}, u32[]{:S(2)}) %collective-permute-start.17) | collective-permute-done | bytes 196640 | tf_op jit(solution)/shard_map/ppermute | solution.py:99
  89.3 1.5 %collective-permute-done.16.refs_2_ = bf16[32,3072]{1,0:T(8,128)(2,1)S(1)} collective-permute-done((bf16[32,3072]{1,0:T(8,128)(2,1)S(1)}, bf16[32,3072]{1,0:T(8,128)(2,1)S(1)}, u32[]{:S(2)}, u32[]{:S(2)}) %collective-permute-start.16) | collective-permute-done | bytes 196640 | tf_op jit(solution)/shard_map/ppermute | solution.py:99
  94.2 1.5 %collective-permute-start.23 = (bf16[128,1536]{1,0:T(8,128)(2,1)S(1)}, bf16[128,1536]{1,0:T(8,128)(2,1)S(1)}, u32[]{:S(2)}, u32[]{:S(2)}) collective-permute-start(bf16[128,1536]{1,0:T(8,128)(2,1)S(1)} %get-tuple-element.73), channel_id=1, source_target_pairs={{0,3},{1,2},{2,1},{3,0},{4,7},{5,6},{6,5},{7,4},{8,11},{9,10},{10,... | collective-permute-start | bytes 1179656 | tf_op jit(solution)/shard_map/ppermute | solution.py:33
  95.7 1.4 %collective-permute-start.24 = (bf16[128,1536]{1,0:T(8,128)(2,1)S(1)}, bf16[128,1536]{1,0:T(8,128)(2,1)S(1)}, u32[]{:S(2)}, u32[]{:S(2)}) collective-permute-start(bf16[128,1536]{1,0:T(8,128)(2,1)S(1)} %get-tuple-element.74), channel_id=1, source_target_pairs={{0,1},{1,0},{2,3},{3,2},{4,5},{5,4},{6,7},{7,6},{8,9},{9,8},{10,11... | collective-permute-start | bytes 1179656 | tf_op jit(solution)/shard_map/ppermute | solution.py:33
  98.0 1.8 %shard_map.110 = bf16[64,12288]{1,0:T(8,128)(2,1)} custom-call(s32[6]{0:T(128)S(1)} %stack.39.place, bf16[32,3072]{1,0:T(8,128)(2,1)S(1)} %shard_map.108.refs_0_, bf16[32,3072]{1,0:T(8,128)(2,1)S(1)} %collective-permute-done.15.refs_1_, bf16[32,3072]{1,0:T(8,128)(2,1)S(1)} %collective-permute-done.16.refs_2_, ...), custom_call_target="tpu_custom_call" | custom-call | flops 1024 | bytes 1024 | tf_op jit(solution)/shard_map/pallas_call | solution.py:111
  99.7 5.1 %collective-permute-done.25.first = bf16[128,4608]{1,0:T(8,128)(2,1)S(1)} collective-permute-done((bf16[128,4608]{1,0:T(8,128)(2,1)S(1)}, bf16[128,4608]{1,0:T(8,128)(2,1)S(1)}, u32[]{:S(2)}, u32[]{:S(2)}) %collective-permute-start.25) | collective-permute-done | bytes 1179680 | tf_op jit(solution)/shard_map/ppermute | solution.py:33
  105.0 6.3 %shard_map.112.rest_0_ = bf16[1,256,12288]{2,1,0:T(8,128)(2,1)} custom-call(bf16[256,512]{1,0:T(8,128)(2,1)S(1)} %shard_map.111.lhs, bf16[128,12288]{1,0:T(8,128)(2,1)S(1)} %copy-done, bf16[128,12288]{1,0:T(8,128)(2,1)S(1)} %collective-permute-done.1.after, bf16[128,12288]{1,0:T(8,128)(2,1)} %collective-permute-done.before, ...), custom_call_target="tpu_custom_call" | custom-call | flops 2415919104 | bytes 14155776 | tf_op jit(solution)/shard_map/pallas_call | solution.py:78
  111.4 3.1 %shard_map.113 = bf16[1,256,12288]{2,1,0:T(8,128)(2,1)} custom-call(bf16[256,512]{1,0:T(8,128)(2,1)S(1)} %shard_map.111.lhs, bf16[128,12288]{1,0:T(8,128)(2,1)S(1)} %copy-done, bf16[128,12288]{1,0:T(8,128)(2,1)S(1)} %collective-permute-done.1.after, bf16[128,12288]{1,0:T(8,128)(2,1)} %collective-permute-done.before, ...), custom_call_target="tpu_custom_call", output_to_operand_aliasing={{}: (6, {})} | custom-call | flops 805306368 | bytes 4718592 | tf_op jit(solution)/shard_map/pallas_call | solution.py:78
  (53 shorter events, 18.5 us)
Async XLA Ops:
  0.6 71.3 %collective-permute-start.1 = (bf16[128,12288]{1,0:T(8,128)(2,1)}, bf16[128,12288]{1,0:T(8,128)(2,1)S(1)}, u32[]{:S(2)}, u32[]{:S(2)}) collective-permute-start(bf16[128,12288]{1,0:T(8,128)(2,1)} %own.3), channel_id=1, source_target_pairs={{0,3},{1,2},{2,1},{3,0},{4,7},{5,6},{6,5},{7,4},{8,11},{9,10},{10,... | collective-permute-start | bytes 9437192 | tf_op jit(solution)/shard_map/ppermute | solution.py:33
  3.5 69.9 %collective-permute-start = (bf16[128,12288]{1,0:T(8,128)(2,1)}, bf16[128,12288]{1,0:T(8,128)(2,1)}, u32[]{:S(2)}, u32[]{:S(2)}) collective-permute-start(bf16[128,12288]{1,0:T(8,128)(2,1)} %own.3), channel_id=1, source_target_pairs={{0,1},{1,0},{2,3},{3,2},{4,5},{5,4},{6,7},{7,6},{8,9},{9,8},{10,11... | collective-permute-start | bytes 9437192 | tf_op jit(solution)/shard_map/ppermute | solution.py:33
  3.8 1.4 %copy-start.1 = (bf16[1,64,12288]{2,1,0:T(8,128)(2,1)S(1)}, bf16[1,64,12288]{2,1,0:T(8,128)(2,1)}, u32[]{:S(2)}) copy-start(bf16[1,64,12288]{2,1,0:T(8,128)(2,1)} %grads.1) | copy-start | bytes 4718596
  5.9 2.4 %collective-permute-start.2 = (bf16[32,12288]{1,0:T(8,128)(2,1)S(1)}, bf16[32,12288]{1,0:T(8,128)(2,1)S(1)}, u32[]{:S(2)}, u32[]{:S(2)}) collective-permute-start(bf16[32,12288]{1,0:T(8,128)(2,1)S(1)} %get-tuple-element.42), channel_id=1, source_target_pairs={{0,4},{4,0},{8,12},{12,8},{16,20},{20,16},{24,28},{28,24},{32,36},... | collective-permute-start | bytes 2359304 | tf_op jit(solution)/shard_map/ppermute | solution.py:29
  9.9 12.3 %collective-permute-start.3 = (f32[32,3072]{1,0:T(8,128)}, f32[32,3072]{1,0:T(8,128)}, u32[]{:S(2)}, u32[]{:S(2)}) collective-permute-start(f32[32,3072]{1,0:T(8,128)} %get-tuple-element.44), channel_id=1, source_target_pairs={{0,64},{4,68},{8,72},{12,76},{16,80},{20,84},{24,88},{28,92},{32,9... | collective-permute-start | bytes 1179656 | tf_op jit(solution)/shard_map/ppermute | solution.py:99
  10.3 20.6 %collective-permute-start.4 = (f32[32,3072]{1,0:T(8,128)}, f32[32,3072]{1,0:T(8,128)}, u32[]{:S(2)}, u32[]{:S(2)}) collective-permute-start(f32[32,3072]{1,0:T(8,128)} %get-tuple-element.45), channel_id=1, source_target_pairs={{0,128},{4,132},{8,136},{12,140},{16,144},{20,148},{24,152},{28,15... | collective-permute-start | bytes 1179656 | tf_op jit(solution)/shard_map/ppermute | solution.py:99
  12.9 19.3 %collective-permute-start.5 = (f32[32,3072]{1,0:T(8,128)}, f32[32,3072]{1,0:T(8,128)}, u32[]{:S(2)}, u32[]{:S(2)}) collective-permute-start(f32[32,3072]{1,0:T(8,128)} %get-tuple-element.46), channel_id=1, source_target_pairs={{0,192},{4,196},{8,200},{12,204},{16,208},{20,212},{24,216},{28,22... | collective-permute-start | bytes 1179656 | tf_op jit(solution)/shard_map/ppermute | solution.py:99
  14.3 0.7 copy-start.3
  22.1 13.4 %collective-permute-start.10 = (f32[3,32,192]{2,1,0:T(8,128)}, f32[3,32,192]{2,1,0:T(8,128)}, u32[]{:S(2)}, u32[]{:S(2)}) collective-permute-start(f32[3,32,192]{2,1,0:T(8,128)} %constant_dynamic-slice_fusion), channel_id=1, source_target_pairs={{0,4},{4,0},{8,12},{12,8},{16,20},{20,16},{24,28},{28,24},{32,36},... | collective-permute-start | bytes 221192 | tf_op jit(solution)/shard_map/ppermute | solution.py:29
  22.1 13.4 %copy-start.4 = (f32[3,64,192]{2,1,0:T(8,128)S(1)}, f32[3,64,192]{2,1,0:T(8,128)}, u32[]{:S(2)}) copy-start(f32[3,64,192]{2,1,0:T(8,128)} %copy-done.3) | copy-start | bytes 442372
  33.6 5.8 %collective-permute-start.6 = (f32[32,1536]{1,0:T(8,128)S(1)}, f32[32,1536]{1,0:T(8,128)S(1)}, u32[]{:S(2)}, u32[]{:S(2)}) collective-permute-start(f32[32,1536]{1,0:T(8,128)S(1)} %get-tuple-element.48), channel_id=1, source_target_pairs={{0,8},{4,12},{8,0},{12,4},{16,24},{20,28},{24,16},{28,20},{32,40},... | collective-permute-start | bytes 589832 | tf_op jit(solution)/shard_map/ppermute | solution.py:103
  39.9 8.8 %collective-permute-start.7 = (f32[32,384]{1,0:T(8,128)S(1)}, f32[32,384]{1,0:T(8,128)S(1)}, u32[]{:S(2)}, u32[]{:S(2)}) collective-permute-start(f32[32,384]{1,0:T(8,128)S(1)} %get-tuple-element.50), channel_id=1, source_target_pairs={{0,16},{4,20},{8,24},{12,28},{16,0},{20,4},{24,8},{28,12},{32,48},... | collective-permute-start | bytes 147464 | tf_op jit(solution)/shard_map/ppermute | solution.py:99
  43.3 8.9 %collective-permute-start.8 = (f32[32,384]{1,0:T(8,128)S(1)}, f32[32,384]{1,0:T(8,128)S(1)}, u32[]{:S(2)}, u32[]{:S(2)}) collective-permute-start(f32[32,384]{1,0:T(8,128)S(1)} %get-tuple-element.51), channel_id=1, source_target_pairs={{0,32},{4,36},{8,40},{12,44},{16,48},{20,52},{24,56},{28,60},{32,0... | collective-permute-start | bytes 147464 | tf_op jit(solution)/shard_map/ppermute | solution.py:99
  48.6 6.3 %collective-permute-start.9 = (f32[32,384]{1,0:T(8,128)S(1)}, f32[32,384]{1,0:T(8,128)S(1)}, u32[]{:S(2)}, u32[]{:S(2)}) collective-permute-start(f32[32,384]{1,0:T(8,128)S(1)} %get-tuple-element.52), channel_id=1, source_target_pairs={{0,48},{4,52},{8,56},{12,60},{16,32},{20,36},{24,40},{28,44},{32,1... | collective-permute-start | bytes 147464 | tf_op jit(solution)/shard_map/ppermute | solution.py:99
  55.5 6.6 %collective-permute-start.13 = (bf16[32,384]{1,0:T(8,128)(2,1)S(1)}, bf16[32,384]{1,0:T(8,128)(2,1)S(1)}, u32[]{:S(2)}, u32[]{:S(2)}) collective-permute-start(bf16[32,384]{1,0:T(8,128)(2,1)S(1)} %get-tuple-element.54.refs_0_), channel_id=1, source_target_pairs={{0,48},{4,52},{8,56},{12,60},{16,32},{20,36},{24,40},{28,44},{32,1... | collective-permute-start | bytes 73736 | tf_op jit(solution)/shard_map/ppermute | solution.py:99
  56.5 7.7 %collective-permute-start.12 = (bf16[32,384]{1,0:T(8,128)(2,1)S(1)}, bf16[32,384]{1,0:T(8,128)(2,1)S(1)}, u32[]{:S(2)}, u32[]{:S(2)}) collective-permute-start(bf16[32,384]{1,0:T(8,128)(2,1)S(1)} %get-tuple-element.54.refs_0_), channel_id=1, source_target_pairs={{0,32},{4,36},{8,40},{12,44},{16,48},{20,52},{24,56},{28,60},{32,0... | collective-permute-start | bytes 73736 | tf_op jit(solution)/shard_map/ppermute | solution.py:99
  60.6 4.8 %collective-permute-start.11 = (bf16[32,384]{1,0:T(8,128)(2,1)S(1)}, bf16[32,384]{1,0:T(8,128)(2,1)S(1)}, u32[]{:S(2)}, u32[]{:S(2)}) collective-permute-start(bf16[32,384]{1,0:T(8,128)(2,1)S(1)} %get-tuple-element.54.refs_0_), channel_id=1, source_target_pairs={{0,16},{4,20},{8,24},{12,28},{16,0},{20,4},{24,8},{28,12},{32,48},... | collective-permute-start | bytes 73736 | tf_op jit(solution)/shard_map/ppermute | solution.py:99
  74.6 30.2 %collective-permute-start.25 = (bf16[128,4608]{1,0:T(8,128)(2,1)S(1)}, bf16[128,4608]{1,0:T(8,128)(2,1)S(1)}, u32[]{:S(2)}, u32[]{:S(2)}) collective-permute-start(bf16[128,4608]{1,0:T(8,128)(2,1)S(1)} %get-tuple-element.75), channel_id=1, source_target_pairs={{0,3},{1,2},{2,1},{3,0},{4,7},{5,6},{6,5},{7,4},{8,11},{9,10},{10,... | collective-permute-start | bytes 3538952 | tf_op jit(solution)/shard_map/ppermute | solution.py:33
  76.1 28.9 %collective-permute-start.26 = (bf16[128,4608]{1,0:T(8,128)(2,1)S(1)}, bf16[128,4608]{1,0:T(8,128)(2,1)S(1)}, u32[]{:S(2)}, u32[]{:S(2)}) collective-permute-start(bf16[128,4608]{1,0:T(8,128)(2,1)S(1)} %get-tuple-element.76), channel_id=1, source_target_pairs={{0,1},{1,0},{2,3},{3,2},{4,5},{5,4},{6,7},{7,6},{8,9},{9,8},{10,11... | collective-permute-start | bytes 3538952 | tf_op jit(solution)/shard_map/ppermute | solution.py:33
  76.1 4.6 %collective-permute-start.14 = (bf16[32,1536]{1,0:T(8,128)(2,1)S(1)}, bf16[32,1536]{1,0:T(8,128)(2,1)S(1)}, u32[]{:S(2)}, u32[]{:S(2)}) collective-permute-start(bf16[32,1536]{1,0:T(8,128)(2,1)S(1)} %shard_map.106.mine), channel_id=1, source_target_pairs={{0,8},{4,12},{8,0},{12,4},{16,24},{20,28},{24,16},{28,20},{32,40},... | collective-permute-start | bytes 294920 | tf_op jit(solution)/shard_map/ppermute | solution.py:103
  81.3 11.4 %copy-start.2 = (bf16[512,256]{1,0:T(8,128)(2,1)S(1)}, bf16[512,256]{1,0:T(8,128)(2,1)}, u32[]{:S(2)}) copy-start(bf16[512,256]{1,0:T(8,128)(2,1)} %out_grads.1) | copy-start | bytes 786436
  81.3 8.0 %collective-permute-start.17 = (bf16[32,3072]{1,0:T(8,128)(2,1)S(1)}, bf16[32,3072]{1,0:T(8,128)(2,1)S(1)}, u32[]{:S(2)}, u32[]{:S(2)}) collective-permute-start(bf16[32,3072]{1,0:T(8,128)(2,1)S(1)} %shard_map.108.refs_0_), channel_id=1, source_target_pairs={{0,192},{4,196},{8,200},{12,204},{16,208},{20,212},{24,216},{28,22... | collective-permute-start | bytes 589832 | tf_op jit(solution)/shard_map/ppermute | solution.py:99
  83.0 7.9 %collective-permute-start.16 = (bf16[32,3072]{1,0:T(8,128)(2,1)S(1)}, bf16[32,3072]{1,0:T(8,128)(2,1)S(1)}, u32[]{:S(2)}, u32[]{:S(2)}) collective-permute-start(bf16[32,3072]{1,0:T(8,128)(2,1)S(1)} %shard_map.108.refs_0_), channel_id=1, source_target_pairs={{0,128},{4,132},{8,136},{12,140},{16,144},{20,148},{24,152},{28,15... | collective-permute-start | bytes 589832 | tf_op jit(solution)/shard_map/ppermute | solution.py:99
  83.9 8.1 %collective-permute-start.15 = (bf16[32,3072]{1,0:T(8,128)(2,1)S(1)}, bf16[32,3072]{1,0:T(8,128)(2,1)S(1)}, u32[]{:S(2)}, u32[]{:S(2)}) collective-permute-start(bf16[32,3072]{1,0:T(8,128)(2,1)S(1)} %shard_map.108.refs_0_), channel_id=1, source_target_pairs={{0,64},{4,68},{8,72},{12,76},{16,80},{20,84},{24,88},{28,92},{32,9... | collective-permute-start | bytes 589832 | tf_op jit(solution)/shard_map/ppermute | solution.py:99
  89.3 3.3 %collective-permute-start.18 = (bf16[32,3072]{1,0:T(8,128)(2,1)S(1)}, bf16[32,3072]{1,0:T(8,128)(2,1)S(1)}, u32[]{:S(2)}, u32[]{:S(2)}) collective-permute-start(bf16[32,3072]{1,0:T(8,128)(2,1)S(1)} %shard_map.108.refs_0_), channel_id=1, source_target_pairs={{0,4},{4,0},{8,12},{12,8},{16,20},{20,16},{24,28},{28,24},{32,36},... | collective-permute-start | bytes 589832 | tf_op jit(solution)/shard_map/ppermute | solution.py:29
  92.0 2.2 %collective-permute-start.19 = (bf16[32,3072]{1,0:T(8,128)(2,1)S(1)}, bf16[32,3072]{1,0:T(8,128)(2,1)S(1)}, u32[]{:S(2)}, u32[]{:S(2)}) collective-permute-start(bf16[32,3072]{1,0:T(8,128)(2,1)S(1)} %collective-permute-done.15.refs_1_), channel_id=1, source_target_pairs={{0,4},{4,0},{8,12},{12,8},{16,20},{20,16},{24,28},{28,24},{32,36},... | collective-permute-start | bytes 589832 | tf_op jit(solution)/shard_map/ppermute | solution.py:29
  92.0 3.7 %collective-permute-start.20 = (bf16[32,3072]{1,0:T(8,128)(2,1)S(1)}, bf16[32,3072]{1,0:T(8,128)(2,1)S(1)}, u32[]{:S(2)}, u32[]{:S(2)}) collective-permute-start(bf16[32,3072]{1,0:T(8,128)(2,1)S(1)} %collective-permute-done.16.refs_2_), channel_id=1, source_target_pairs={{0,4},{4,0},{8,12},{12,8},{16,20},{20,16},{24,28},{28,24},{32,36},... | collective-permute-start | bytes 589832 | tf_op jit(solution)/shard_map/ppermute | solution.py:29
  92.6 1.4 %collective-permute-start.22 = (f32[3,32,192]{2,1,0:T(8,128)S(1)}, f32[3,32,192]{2,1,0:T(8,128)S(1)}, u32[]{:S(2)}, u32[]{:S(2)}) collective-permute-start(f32[3,32,192]{2,1,0:T(8,128)S(1)} %slice_select_fusion), channel_id=1, source_target_pairs={{0,4},{4,0},{8,12},{12,8},{16,20},{20,16},{24,28},{28,24},{32,36},... | collective-permute-start | bytes 221192 | tf_op jit(solution)/shard_map/ppermute | solution.py:29
  94.0 3.9 %collective-permute-start.21 = (bf16[32,3072]{1,0:T(8,128)(2,1)S(1)}, bf16[32,3072]{1,0:T(8,128)(2,1)S(1)}, u32[]{:S(2)}, u32[]{:S(2)}) collective-permute-start(bf16[32,3072]{1,0:T(8,128)(2,1)S(1)} %collective-permute-done.17.refs_3_), channel_id=1, source_target_pairs={{0,4},{4,0},{8,12},{12,8},{16,20},{20,16},{24,28},{28,24},{32,36},... | collective-permute-start | bytes 589832 | tf_op jit(solution)/shard_map/ppermute | solution.py:29
  94.2 17.2 %collective-permute-start.23 = (bf16[128,1536]{1,0:T(8,128)(2,1)S(1)}, bf16[128,1536]{1,0:T(8,128)(2,1)S(1)}, u32[]{:S(2)}, u32[]{:S(2)}) collective-permute-start(bf16[128,1536]{1,0:T(8,128)(2,1)S(1)} %get-tuple-element.73), channel_id=1, source_target_pairs={{0,3},{1,2},{2,1},{3,0},{4,7},{5,6},{6,5},{7,4},{8,11},{9,10},{10,... | collective-permute-start | bytes 1179656 | tf_op jit(solution)/shard_map/ppermute | solution.py:33
  95.7 15.6 %collective-permute-start.24 = (bf16[128,1536]{1,0:T(8,128)(2,1)S(1)}, bf16[128,1536]{1,0:T(8,128)(2,1)S(1)}, u32[]{:S(2)}, u32[]{:S(2)}) collective-permute-start(bf16[128,1536]{1,0:T(8,128)(2,1)S(1)} %get-tuple-element.74), channel_id=1, source_target_pairs={{0,1},{1,0},{2,3},{3,2},{4,5},{5,4},{6,7},{7,6},{8,9},{9,8},{10,11... | collective-permute-start | bytes 1179656 | tf_op jit(solution)/shard_map/ppermute | solution.py:33
  98.0 7.1 %copy-start = (bf16[128,12288]{1,0:T(8,128)(2,1)S(1)}, bf16[128,12288]{1,0:T(8,128)(2,1)}, u32[]{:S(2)}) copy-start(bf16[128,12288]{1,0:T(8,128)(2,1)} %own.3) | copy-start | bytes 9437188

commit v4 on v3

--- a/solution.py
+++ b/solution.py
@@ -42,7 +42,7 @@
     step, half_way = pl.program_id(0), pl.num_programs(0) // 2
 
     def columns_of(opposite):
-        tokens = jnp.concatenate([own[...], before[...], opposite[...], after[...]], axis=0)
+        tokens = jnp.concatenate([own[...], before[...], after[...], opposite[...]], axis=0)
         out[0] = jnp.dot(lhs[...], tokens, preferred_element_type=jnp.float32).astype(jnp.bfloat16)
 
     @pl.when(step < half_way)
@@ -87,6 +87,62 @@
     )(*operands)
 
 
+def near_kernel(lhs, own, after, before, out, done):
+    tokens = jnp.concatenate([own[...], before[...], after[...]], axis=0)
+    out[...] = jnp.dot(lhs[:, :384], tokens, preferred_element_type=jnp.float32)
+    done[...] = jnp.zeros_like(done)
+
+
+def near_product(piece, lhs, own, after, before):
+    start, width = piece
+    whole = pl.BlockSpec((128, width), lambda i: (0, start // width + i))
+    return pl.pallas_call(
+        near_kernel,
+        grid=(2,),
+        in_specs=[pl.BlockSpec((256, 512), lambda i: (0, 0)), whole, whole, whole],
+        out_specs=[pl.BlockSpec((256, width), lambda i: (0, i)), pl.BlockSpec((8, 128), lambda i: (0, 0))],
+        out_shape=[jax.ShapeDtypeStruct((256, 2 * width), jnp.float32), jax.ShapeDtypeStruct((8, 128), jnp.float32)],
+        compiler_params=pltpu.CompilerParams(vmem_limit_bytes=VMEM_LIMIT),
+    )(lhs, own, after, before)
+
+
+def far_kernel(lhs, summed, first, second, carry, out):
+    step = pl.program_id(0)
+
+    def columns_of(opposite):
+        far = jnp.dot(lhs[:, 384:], opposite[...], preferred_element_type=jnp.float32)
+        out[0] = (summed[...] + far).astype(jnp.bfloat16)
+
+    @pl.when(step == 0)
+    def _():
+        columns_of(first)
+
+    @pl.when(step == 1)
+    def _():
+        columns_of(second)
+
+
+def far_product(piece, lhs, summed, first, second, carry):
+    start, width = piece
+    alone = pl.BlockSpec((128, width), lambda i: (0, 0))
+    return pl.pallas_call(
+        far_kernel,
+        grid=(2,),
+        in_specs=[
+            pl.BlockSpec((256, 512), lambda i: (0, 0)),
+            pl.BlockSpec((256, width), lambda i: (0, i)),
+            alone,
+            alone,
+            pl.BlockSpec(memory_space=pl.ANY),
+        ],
+        out_specs=pl.BlockSpec((1, 256, width), lambda i: (0, 0, start // width + i)),
+        out_shape=jax.ShapeDtypeStruct((1, 256, D), jnp.bfloat16),
+        input_output_aliases={4: 0},
+        cost_estimate=pl.CostEstimate(flops=512 * 256 * width, bytes_accessed=2048 * width, transcendentals=0),
+        compiler_params=pltpu.CompilerParams(vmem_limit_bytes=VMEM_LIMIT),
+    )(lhs, summed, first, second, carry)
+
+
 def sign(*arrays):
     return jnp.concatenate([array[:16, :128] for array in arrays])
 
@@ -155,7 +211,7 @@
 
 def turn(place, out_grads, out):
     for step in range(NX):
-        owner = place[5] ^ step
+        owner = place[5] ^ (0, 1, 3, 2)[step]
         rows = pl.ds(pl.multiple_of(owner * 128, 128), 128)
         out[:, step * 128 : (step + 1) * 128] = out_grads[rows, :].T
 
@@ -287,7 +343,8 @@
     got = exchange([own] * 3, [(k, 0, 0) for k in (1, 2, 3)])
 
     near = cut(PIECES[1:], before, after)
-    *near, got0, got1, got2 = lax.optimization_barrier((*near, *got))
+    summed, there = near_product(PIECES[1], lhs, inputs, after, before)
+    *near, got0, got1, got2, there = lax.optimization_barrier((*near, *got, there))
     opposites += [swap_x(near[0], 3), swap_x(near[1], 1)]
     parts = [own, got0, got1, got2]
     others = [to_core(part) for part in parts]
@@ -299,9 +356,9 @@
     state = jnp.concatenate([jnp.where(first, kept, got), jnp.where(first, got, kept)], axis=1)
     state = [state[0], state[1], state[2]]
 
-    weights, state[0], state[1], state[2], lhs = lax.optimization_barrier((weights, *state, lhs))
-    carry = product(PIECES[0][0], 2304, lhs, inputs, after, before, *opposites[:2], None)
-    carry = product(PIECES[1][0], 1536, lhs, inputs, after, before, *opposites[2:], carry)
+    weights, state[0], state[1], state[2], there = lax.optimization_barrier((weights, *state, there))
+    carry = product(PIECES[0][0], 2304, lhs, inputs, after, before, *opposites[:2], None, there)
+    carry = far_product(PIECES[1], lhs, summed, *opposites[2:], carry)
 
     return (weights, state[0], state[1], state[2], carry)
 

time: 115 us -> 114 us (level)
  waiting for transfers between devices: 52.7 us -> 49.5 us
  Pallas kernels: 20.1 us -> 21.4 us
    pallas_call x0 -> x2, Pallas kernels: none -> 4.22 us  [the longest x1 2.37 us: near_product(): pl.pallas_call(near_kernel, grid=(2,), in_specs=[pl.BlockSpec((256, 512),...]
    ppermute x12, waiting for transfers between devices: 31.6 us -> 28 us  [exchange(): lax.ppermute(array, 'dp', dp_swap(*move))]
    pallas_call x2 -> x1, Pallas kernels: 9.48 us -> 6.27 us  [product(): pl.pallas_call(product_kernel, grid=(2 * steps,), in_specs=specs, out_spe...]
    unnamed x10 -> x8, local copies, waits for them, and re-layouts: 2.09 us -> 2.88 us
  transfers between devices with their start and end apart: 27 -> 27, of which waited for: 18 -> 17; matrix products, arithmetic and copies ran while one was open for 3% -> 3% of each run, Pallas kernels for 14% -> 16%
where the time goes in v4:
time: 114 us
  waiting for transfers between devices  49.5 us (43%)
  starting transfers between devices  35.7 us (31%)
  Pallas kernels  21.4 us (19%)
  local copies, waits for them, and re-layouts  3.6 us (3%)
  other arithmetic  2.82 us (2%)
    ppermute x12, waiting for transfers between devices, exchange(): lax.ppermute(array, 'dp', dp_swap(*move))  28 us
    ppermute x12, starting transfers between devices, exchange(): lax.ppermute(array, 'dp', dp_swap(*move))  22.4 us
    ppermute x6, waiting for transfers between devices, swap_x(): return lax.ppermute(array, 'mp', [(i, i ^ bits) for i in range(NX)])  12.4 us
    ppermute x6, starting transfers between devices, swap_x(): return lax.ppermute(array, 'mp', [(i, i ^ bits) for i in range(NX)])  8.45 us
    pallas_call x8, Pallas kernels, local(): pl.pallas_call(body, in_specs=[SMEM] + [VMEM] * len(operands), out_specs=...  7.67 us
    pallas_call x1, Pallas kernels, product(): pl.pallas_call(product_kernel, grid=(2 * steps,), in_specs=specs, out_spe...  6.27 us
    ppermute x2, waiting for transfers between devices, swap_z(): return lax.ppermute(array, 'dp', dp_swap(0, 1, 0))  5.49 us
    ppermute x2, starting transfers between devices, swap_z(): return lax.ppermute(array, 'dp', dp_swap(0, 1, 0))  3.92 us
  transfers between devices with their start and end apart: 27, of which 17 were waited for; matrix products, arithmetic and copies ran while one was open for 3% of the time, Pallas kernels for 16%

profile of v4, /device:TPU:8, one launch (start us, length us, event | category | flops | bytes accessed | tf_op | source)
XLA Modules:
  0.0 113.9 jit_solution(1510243276324105539)
XLA Ops:
  0.6 1.6 %collective-permute-start = (bf16[128,12288]{1,0:T(8,128)(2,1)}, bf16[128,12288]{1,0:T(8,128)(2,1)S(1)}, u32[]{:S(2)}, u32[]{:S(2)}) collective-permute-start(bf16[128,12288]{1,0:T(8,128)(2,1)} %own.3), channel_id=1, source_target_pairs={{0,1},{1,0},{2,3},{3,2},{4,5},{5,4},{6,7},{7,6},{8,9},{9,8},{10,11... | collective-permute-start | bytes 9437192 | tf_op jit(solution)/shard_map/ppermute | solution.py:33
  2.2 2.1 %collective-permute-start.1 = (bf16[128,12288]{1,0:T(8,128)(2,1)}, bf16[128,12288]{1,0:T(8,128)(2,1)}, u32[]{:S(2)}, u32[]{:S(2)}) collective-permute-start(bf16[128,12288]{1,0:T(8,128)(2,1)} %own.3), channel_id=1, source_target_pairs={{0,3},{1,2},{2,1},{3,0},{4,7},{5,6},{6,5},{7,4},{8,11},{9,10},{10,... | collective-permute-start | bytes 9437192 | tf_op jit(solution)/shard_map/ppermute | solution.py:33
  4.4 1.4 %copy-done.1 = bf16[1,64,12288]{2,1,0:T(8,128)(2,1)S(1)} copy-done((bf16[1,64,12288]{2,1,0:T(8,128)(2,1)S(1)}, bf16[1,64,12288]{2,1,0:T(8,128)(2,1)}, u32[]{:S(2)}) %copy-start.1) | copy-done | bytes 1572888
  6.6 2.3 %collective-permute-done.2.theirs = bf16[32,12288]{1,0:T(8,128)(2,1)S(1)} collective-permute-done((bf16[32,12288]{1,0:T(8,128)(2,1)S(1)}, bf16[32,12288]{1,0:T(8,128)(2,1)S(1)}, u32[]{:S(2)}, u32[]{:S(2)}) %collective-permute-start.2) | collective-permute-done | bytes 786464 | tf_op jit(solution)/shard_map/ppermute | solution.py:29
  8.9 1.6 %shard_map.102 = (f32[32,3072]{1,0:T(8,128)S(1)}, f32[32,3072]{1,0:T(8,128)}, f32[32,3072]{1,0:T(8,128)}, f32[32,3072]{1,0:T(8,128)}) custom-call(s32[6]{0:T(128)S(1)} %stack.39.place, bf16[32,12288]{1,0:T(8,128)(2,1)S(1)} %get-tuple-element.44.mine, bf16[32,12288]{1,0:T(8,128)(2,1)S(1)} %collective-permute-done.2.theirs), custom_call_target="tpu_custom_call" | custom-call | flops 1024 | bytes 1024 | tf_op jit(solution)/shard_map/pallas_call | solution.py:167
  10.9 2.6 %collective-permute-start.4 = (f32[32,3072]{1,0:T(8,128)}, f32[32,3072]{1,0:T(8,128)}, u32[]{:S(2)}, u32[]{:S(2)}) collective-permute-start(f32[32,3072]{1,0:T(8,128)} %get-tuple-element.48), channel_id=1, source_target_pairs={{0,128},{4,132},{8,136},{12,140},{16,144},{20,148},{24,152},{28,15... | collective-permute-start | bytes 1179656 | tf_op jit(solution)/shard_map/ppermute | solution.py:155
  16.2 6.5 %collective-permute-done.3.b = f32[32,3072]{1,0:T(8,128)} collective-permute-done((f32[32,3072]{1,0:T(8,128)}, f32[32,3072]{1,0:T(8,128)}, u32[]{:S(2)}, u32[]{:S(2)}) %collective-permute-start.3) | collective-permute-done | bytes 393248 | tf_op jit(solution)/shard_map/ppermute | solution.py:155
  22.7 8.7 %collective-permute-done.4.c = f32[32,3072]{1,0:T(8,128)} collective-permute-done((f32[32,3072]{1,0:T(8,128)}, f32[32,3072]{1,0:T(8,128)}, u32[]{:S(2)}, u32[]{:S(2)}) %collective-permute-start.4) | collective-permute-done | bytes 393248 | tf_op jit(solution)/shard_map/ppermute | solution.py:155
  31.5 1.4 %collective-permute-done.5.d = f32[32,3072]{1,0:T(8,128)} collective-permute-done((f32[32,3072]{1,0:T(8,128)}, f32[32,3072]{1,0:T(8,128)}, u32[]{:S(2)}, u32[]{:S(2)}) %collective-permute-start.5) | collective-permute-done | bytes 393248 | tf_op jit(solution)/shard_map/ppermute | solution.py:155
  34.2 2.0 %collective-permute-start.6 = (f32[32,1536]{1,0:T(8,128)S(1)}, f32[32,1536]{1,0:T(8,128)S(1)}, u32[]{:S(2)}, u32[]{:S(2)}) collective-permute-start(f32[32,1536]{1,0:T(8,128)S(1)} %get-tuple-element.51), channel_id=1, source_target_pairs={{0,8},{4,12},{8,0},{12,4},{16,24},{20,28},{24,16},{28,20},{32,40},... | collective-permute-start | bytes 589832 | tf_op jit(solution)/shard_map/ppermute | solution.py:159
  37.1 2.8 %collective-permute-done.6.b = f32[32,1536]{1,0:T(8,128)S(1)} collective-permute-done((f32[32,1536]{1,0:T(8,128)S(1)}, f32[32,1536]{1,0:T(8,128)S(1)}, u32[]{:S(2)}, u32[]{:S(2)}) %collective-permute-start.6) | collective-permute-done | bytes 196640 | tf_op jit(solution)/shard_map/ppermute | solution.py:159
  40.5 3.4 %collective-permute-start.7 = (f32[32,384]{1,0:T(8,128)S(1)}, f32[32,384]{1,0:T(8,128)S(1)}, u32[]{:S(2)}, u32[]{:S(2)}) collective-permute-start(f32[32,384]{1,0:T(8,128)S(1)} %get-tuple-element.53), channel_id=1, source_target_pairs={{0,16},{4,20},{8,24},{12,28},{16,0},{20,4},{24,8},{28,12},{32,48},... | collective-permute-start | bytes 147464 | tf_op jit(solution)/shard_map/ppermute | solution.py:155
  43.9 5.4 %collective-permute-start.8 = (f32[32,384]{1,0:T(8,128)S(1)}, f32[32,384]{1,0:T(8,128)S(1)}, u32[]{:S(2)}, u32[]{:S(2)}) collective-permute-start(f32[32,384]{1,0:T(8,128)S(1)} %get-tuple-element.54), channel_id=1, source_target_pairs={{0,32},{4,36},{8,40},{12,44},{16,48},{20,52},{24,56},{28,60},{32,0... | collective-permute-start | bytes 147464 | tf_op jit(solution)/shard_map/ppermute | solution.py:155
  49.4 3.4 %collective-permute-done.8.c = f32[32,384]{1,0:T(8,128)S(1)} collective-permute-done((f32[32,384]{1,0:T(8,128)S(1)}, f32[32,384]{1,0:T(8,128)S(1)}, u32[]{:S(2)}, u32[]{:S(2)}) %collective-permute-start.8) | collective-permute-done | bytes 49184 | tf_op jit(solution)/shard_map/ppermute | solution.py:155
  52.8 2.7 %collective-permute-done.9.d = f32[32,384]{1,0:T(8,128)S(1)} collective-permute-done((f32[32,384]{1,0:T(8,128)S(1)}, f32[32,384]{1,0:T(8,128)S(1)}, u32[]{:S(2)}, u32[]{:S(2)}) %collective-permute-start.9) | collective-permute-done | bytes 49184 | tf_op jit(solution)/shard_map/ppermute | solution.py:155
  56.1 1.5 %collective-permute-start.11 = (bf16[32,384]{1,0:T(8,128)(2,1)S(1)}, bf16[32,384]{1,0:T(8,128)(2,1)S(1)}, u32[]{:S(2)}, u32[]{:S(2)}) collective-permute-start(bf16[32,384]{1,0:T(8,128)(2,1)S(1)} %get-tuple-element.57.refs_0_), channel_id=1, source_target_pairs={{0,16},{4,20},{8,24},{12,28},{16,0},{20,4},{24,8},{28,12},{32,48},... | collective-permute-start | bytes 73736 | tf_op jit(solution)/shard_map/ppermute | solution.py:155
  57.6 1.8 %collective-permute-start.12 = (bf16[32,384]{1,0:T(8,128)(2,1)S(1)}, bf16[32,384]{1,0:T(8,128)(2,1)S(1)}, u32[]{:S(2)}, u32[]{:S(2)}) collective-permute-start(bf16[32,384]{1,0:T(8,128)(2,1)S(1)} %get-tuple-element.57.refs_0_), channel_id=1, source_target_pairs={{0,32},{4,36},{8,40},{12,44},{16,48},{20,52},{24,56},{28,60},{32,0... | collective-permute-start | bytes 73736 | tf_op jit(solution)/shard_map/ppermute | solution.py:155
  59.4 3.3 %collective-permute-start.13 = (bf16[32,384]{1,0:T(8,128)(2,1)S(1)}, bf16[32,384]{1,0:T(8,128)(2,1)S(1)}, u32[]{:S(2)}, u32[]{:S(2)}) collective-permute-start(bf16[32,384]{1,0:T(8,128)(2,1)S(1)} %get-tuple-element.57.refs_0_), channel_id=1, source_target_pairs={{0,48},{4,52},{8,56},{12,60},{16,32},{20,36},{24,40},{28,44},{32,1... | collective-permute-start | bytes 73736 | tf_op jit(solution)/shard_map/ppermute | solution.py:155
  62.7 2.8 %collective-permute-done.12.refs_2_ = bf16[32,384]{1,0:T(8,128)(2,1)S(1)} collective-permute-done((bf16[32,384]{1,0:T(8,128)(2,1)S(1)}, bf16[32,384]{1,0:T(8,128)(2,1)S(1)}, u32[]{:S(2)}, u32[]{:S(2)}) %collective-permute-start.12) | collective-permute-done | bytes 24608 | tf_op jit(solution)/shard_map/ppermute | solution.py:155
  66.3 4.5 %collective-permute-done.before = bf16[128,12288]{1,0:T(8,128)(2,1)S(1)} collective-permute-done((bf16[128,12288]{1,0:T(8,128)(2,1)}, bf16[128,12288]{1,0:T(8,128)(2,1)S(1)}, u32[]{:S(2)}, u32[]{:S(2)}) %collective-permute-start) | collective-permute-done | bytes 3145760 | tf_op jit(solution)/shard_map/ppermute | solution.py:33
  70.8 2.5 %collective-permute-done.1.after = bf16[128,12288]{1,0:T(8,128)(2,1)} collective-permute-done((bf16[128,12288]{1,0:T(8,128)(2,1)}, bf16[128,12288]{1,0:T(8,128)(2,1)}, u32[]{:S(2)}, u32[]{:S(2)}) %collective-permute-start.1) | collective-permute-done | bytes 3145760 | tf_op jit(solution)/shard_map/ppermute | solution.py:33
  73.3 1.4 %shard_map.107 = (bf16[128,4608]{1,0:T(8,128)(2,1)S(1)}, bf16[128,4608]{1,0:T(8,128)(2,1)S(1)}) custom-call(bf16[128,12288]{1,0:T(8,128)(2,1)S(1)} %collective-permute-done.before, bf16[128,12288]{1,0:T(8,128)(2,1)} %collective-permute-done.1.after), custom_call_target="tpu_custom_call" | custom-call | flops 1024 | bytes 1024 | tf_op jit(solution)/shard_map/pallas_call | solution.py:201
  74.7 2.2 %collective-permute-start.25 = (bf16[128,4608]{1,0:T(8,128)(2,1)S(1)}, bf16[128,4608]{1,0:T(8,128)(2,1)S(1)}, u32[]{:S(2)}, u32[]{:S(2)}) collective-permute-start(bf16[128,4608]{1,0:T(8,128)(2,1)S(1)} %get-tuple-element.80), channel_id=1, source_target_pairs={{0,3},{1,2},{2,1},{3,0},{4,7},{5,6},{6,5},{7,4},{8,11},{9,10},{10,... | collective-permute-start | bytes 3538952 | tf_op jit(solution)/shard_map/ppermute | solution.py:33
  76.9 1.9 %collective-permute-start.14 = (bf16[32,1536]{1,0:T(8,128)(2,1)S(1)}, bf16[32,1536]{1,0:T(8,128)(2,1)S(1)}, u32[]{:S(2)}, u32[]{:S(2)}) collective-permute-start(bf16[32,1536]{1,0:T(8,128)(2,1)S(1)} %shard_map.106.mine), channel_id=1, source_target_pairs={{0,8},{4,12},{8,0},{12,4},{16,24},{20,28},{24,16},{28,20},{32,40},... | collective-permute-start | bytes 294920 | tf_op jit(solution)/shard_map/ppermute | solution.py:159
  78.8 2.7 %collective-permute-done.14.other = bf16[32,1536]{1,0:T(8,128)(2,1)S(1)} collective-permute-done((bf16[32,1536]{1,0:T(8,128)(2,1)S(1)}, bf16[32,1536]{1,0:T(8,128)(2,1)S(1)}, u32[]{:S(2)}, u32[]{:S(2)}) %collective-permute-start.14) | collective-permute-done | bytes 98336 | tf_op jit(solution)/shard_map/ppermute | solution.py:159
  82.6 2.6 %collective-permute-start.16 = (bf16[32,3072]{1,0:T(8,128)(2,1)S(1)}, bf16[32,3072]{1,0:T(8,128)(2,1)S(1)}, u32[]{:S(2)}, u32[]{:S(2)}) collective-permute-start(bf16[32,3072]{1,0:T(8,128)(2,1)S(1)} %shard_map.108.refs_0_), channel_id=1, source_target_pairs={{0,128},{4,132},{8,136},{12,140},{16,144},{20,148},{24,152},{28,15... | collective-permute-start | bytes 589832 | tf_op jit(solution)/shard_map/ppermute | solution.py:155
  88.3 2.4 %shard_map.111 = (f32[256,3072]{1,0:T(8,128)S(1)}, f32[8,128]{1,0:T(8,128)S(1)}) custom-call(bf16[256,512]{1,0:T(8,128)(2,1)S(1)} %shard_map.110.lhs, bf16[128,12288]{1,0:T(8,128)(2,1)S(1)} %copy-done, bf16[128,12288]{1,0:T(8,128)(2,1)} %collective-permute-done.1.after, bf16[128,12288]{1,0:T(8,128)(2,1)S(1)} %collective-permute-done.before), custom_call_target="tpu_custom_call" | custom-call | tf_op jit(solution)/shard_map/pallas_call | solution.py:99
  96.4 1.4 %collective-permute-start.24 = (bf16[128,1536]{1,0:T(8,128)(2,1)S(1)}, bf16[128,1536]{1,0:T(8,128)(2,1)S(1)}, u32[]{:S(2)}, u32[]{:S(2)}) collective-permute-start(bf16[128,1536]{1,0:T(8,128)(2,1)S(1)} %get-tuple-element.79), channel_id=1, source_target_pairs={{0,1},{1,0},{2,3},{3,2},{4,5},{5,4},{6,7},{7,6},{8,9},{9,8},{10,11... | collective-permute-start | bytes 1179656 | tf_op jit(solution)/shard_map/ppermute | solution.py:33
  98.6 1.8 %shard_map.112 = bf16[64,12288]{1,0:T(8,128)(2,1)} custom-call(s32[6]{0:T(128)S(1)} %stack.39.place, bf16[32,3072]{1,0:T(8,128)(2,1)S(1)} %shard_map.108.refs_0_, bf16[32,3072]{1,0:T(8,128)(2,1)S(1)} %collective-permute-done.15.refs_1_, bf16[32,3072]{1,0:T(8,128)(2,1)S(1)} %collective-permute-done.16.refs_2_, ...), custom_call_target="tpu_custom_call" | custom-call | flops 1024 | bytes 1024 | tf_op jit(solution)/shard_map/pallas_call | solution.py:167
  100.4 4.5 %collective-permute-done.25.first = bf16[128,4608]{1,0:T(8,128)(2,1)S(1)} collective-permute-done((bf16[128,4608]{1,0:T(8,128)(2,1)S(1)}, bf16[128,4608]{1,0:T(8,128)(2,1)S(1)}, u32[]{:S(2)}, u32[]{:S(2)}) %collective-permute-start.25) | collective-permute-done | bytes 1179680 | tf_op jit(solution)/shard_map/ppermute | solution.py:33
  105.8 6.3 %shard_map.113.carry = bf16[1,256,12288]{2,1,0:T(8,128)(2,1)} custom-call(bf16[256,512]{1,0:T(8,128)(2,1)S(1)} %shard_map.110.lhs, bf16[128,12288]{1,0:T(8,128)(2,1)S(1)} %copy-done, bf16[128,12288]{1,0:T(8,128)(2,1)} %collective-permute-done.1.after, bf16[128,12288]{1,0:T(8,128)(2,1)S(1)} %collective-permute-done.before, ...), custom_call_target="tpu_custom_call" | custom-call | flops 2415919104 | bytes 14155776 | tf_op jit(solution)/shard_map/pallas_call | solution.py:78
  112.0 1.9 %shard_map.114 = bf16[1,256,12288]{2,1,0:T(8,128)(2,1)} custom-call(bf16[256,512]{1,0:T(8,128)(2,1)S(1)} %shard_map.110.lhs, f32[256,3072]{1,0:T(8,128)S(1)} %get-tuple-element.77.summed, bf16[128,1536]{1,0:T(8,128)(2,1)S(1)} %collective-permute-done.23.first, bf16[128,1536]{1,0:T(8,128)(2,1)S(1)} %collective-permute-done.24.second, ...), custom_call_target="tpu_custom_call", output_to_operand_aliasing={{}: (4, {})} | custom-call | flops 201326592 | bytes 3145728 | tf_op jit(solution)/shard_map/pallas_call | solution.py:128
  (52 shorter events, 19.8 us)
Async XLA Ops:
  0.6 70.1 %collective-permute-start = (bf16[128,12288]{1,0:T(8,128)(2,1)}, bf16[128,12288]{1,0:T(8,128)(2,1)S(1)}, u32[]{:S(2)}, u32[]{:S(2)}) collective-permute-start(bf16[128,12288]{1,0:T(8,128)(2,1)} %own.3), channel_id=1, source_target_pairs={{0,1},{1,0},{2,3},{3,2},{4,5},{5,4},{6,7},{7,6},{8,9},{9,8},{10,11... | collective-permute-start | bytes 9437192 | tf_op jit(solution)/shard_map/ppermute | solution.py:33
  2.2 71.1 %collective-permute-start.1 = (bf16[128,12288]{1,0:T(8,128)(2,1)}, bf16[128,12288]{1,0:T(8,128)(2,1)}, u32[]{:S(2)}, u32[]{:S(2)}) collective-permute-start(bf16[128,12288]{1,0:T(8,128)(2,1)} %own.3), channel_id=1, source_target_pairs={{0,3},{1,2},{2,1},{3,0},{4,7},{5,6},{6,5},{7,4},{8,11},{9,10},{10,... | collective-permute-start | bytes 9437192 | tf_op jit(solution)/shard_map/ppermute | solution.py:33
  4.4 1.4 %copy-start.1 = (bf16[1,64,12288]{2,1,0:T(8,128)(2,1)S(1)}, bf16[1,64,12288]{2,1,0:T(8,128)(2,1)}, u32[]{:S(2)}) copy-start(bf16[1,64,12288]{2,1,0:T(8,128)(2,1)} %grads.1) | copy-start | bytes 4718596
  6.5 2.4 %collective-permute-start.2 = (bf16[32,12288]{1,0:T(8,128)(2,1)S(1)}, bf16[32,12288]{1,0:T(8,128)(2,1)S(1)}, u32[]{:S(2)}, u32[]{:S(2)}) collective-permute-start(bf16[32,12288]{1,0:T(8,128)(2,1)S(1)} %get-tuple-element.45), channel_id=1, source_target_pairs={{0,4},{4,0},{8,12},{12,8},{16,20},{20,16},{24,28},{28,24},{32,36},... | collective-permute-start | bytes 2359304 | tf_op jit(solution)/shard_map/ppermute | solution.py:29
  10.5 12.3 %collective-permute-start.3 = (f32[32,3072]{1,0:T(8,128)}, f32[32,3072]{1,0:T(8,128)}, u32[]{:S(2)}, u32[]{:S(2)}) collective-permute-start(f32[32,3072]{1,0:T(8,128)} %get-tuple-element.47), channel_id=1, source_target_pairs={{0,64},{4,68},{8,72},{12,76},{16,80},{20,84},{24,88},{28,92},{32,9... | collective-permute-start | bytes 1179656 | tf_op jit(solution)/shard_map/ppermute | solution.py:155
  10.9 20.6 %collective-permute-start.4 = (f32[32,3072]{1,0:T(8,128)}, f32[32,3072]{1,0:T(8,128)}, u32[]{:S(2)}, u32[]{:S(2)}) collective-permute-start(f32[32,3072]{1,0:T(8,128)} %get-tuple-element.48), channel_id=1, source_target_pairs={{0,128},{4,132},{8,136},{12,140},{16,144},{20,148},{24,152},{28,15... | collective-permute-start | bytes 1179656 | tf_op jit(solution)/shard_map/ppermute | solution.py:155
  13.5 19.3 %collective-permute-start.5 = (f32[32,3072]{1,0:T(8,128)}, f32[32,3072]{1,0:T(8,128)}, u32[]{:S(2)}, u32[]{:S(2)}) collective-permute-start(f32[32,3072]{1,0:T(8,128)} %get-tuple-element.49), channel_id=1, source_target_pairs={{0,192},{4,196},{8,200},{12,204},{16,208},{20,212},{24,216},{28,22... | collective-permute-start | bytes 1179656 | tf_op jit(solution)/shard_map/ppermute | solution.py:155
  14.9 0.7 copy-start.3
  22.7 13.4 %collective-permute-start.10 = (f32[3,32,192]{2,1,0:T(8,128)}, f32[3,32,192]{2,1,0:T(8,128)}, u32[]{:S(2)}, u32[]{:S(2)}) collective-permute-start(f32[3,32,192]{2,1,0:T(8,128)} %constant_dynamic-slice_fusion), channel_id=1, source_target_pairs={{0,4},{4,0},{8,12},{12,8},{16,20},{20,16},{24,28},{28,24},{32,36},... | collective-permute-start | bytes 221192 | tf_op jit(solution)/shard_map/ppermute | solution.py:29
  34.2 5.8 %collective-permute-start.6 = (f32[32,1536]{1,0:T(8,128)S(1)}, f32[32,1536]{1,0:T(8,128)S(1)}, u32[]{:S(2)}, u32[]{:S(2)}) collective-permute-start(f32[32,1536]{1,0:T(8,128)S(1)} %get-tuple-element.51), channel_id=1, source_target_pairs={{0,8},{4,12},{8,0},{12,4},{16,24},{20,28},{24,16},{28,20},{32,40},... | collective-permute-start | bytes 589832 | tf_op jit(solution)/shard_map/ppermute | solution.py:159
  40.5 8.8 %collective-permute-start.7 = (f32[32,384]{1,0:T(8,128)S(1)}, f32[32,384]{1,0:T(8,128)S(1)}, u32[]{:S(2)}, u32[]{:S(2)}) collective-permute-start(f32[32,384]{1,0:T(8,128)S(1)} %get-tuple-element.53), channel_id=1, source_target_pairs={{0,16},{4,20},{8,24},{12,28},{16,0},{20,4},{24,8},{28,12},{32,48},... | collective-permute-start | bytes 147464 | tf_op jit(solution)/shard_map/ppermute | solution.py:155
  43.9 8.9 %collective-permute-start.8 = (f32[32,384]{1,0:T(8,128)S(1)}, f32[32,384]{1,0:T(8,128)S(1)}, u32[]{:S(2)}, u32[]{:S(2)}) collective-permute-start(f32[32,384]{1,0:T(8,128)S(1)} %get-tuple-element.54), channel_id=1, source_target_pairs={{0,32},{4,36},{8,40},{12,44},{16,48},{20,52},{24,56},{28,60},{32,0... | collective-permute-start | bytes 147464 | tf_op jit(solution)/shard_map/ppermute | solution.py:155
  49.3 6.3 %collective-permute-start.9 = (f32[32,384]{1,0:T(8,128)S(1)}, f32[32,384]{1,0:T(8,128)S(1)}, u32[]{:S(2)}, u32[]{:S(2)}) collective-permute-start(f32[32,384]{1,0:T(8,128)S(1)} %get-tuple-element.55), channel_id=1, source_target_pairs={{0,48},{4,52},{8,56},{12,60},{16,32},{20,36},{24,40},{28,44},{32,1... | collective-permute-start | bytes 147464 | tf_op jit(solution)/shard_map/ppermute | solution.py:155
  56.1 6.6 %collective-permute-start.11 = (bf16[32,384]{1,0:T(8,128)(2,1)S(1)}, bf16[32,384]{1,0:T(8,128)(2,1)S(1)}, u32[]{:S(2)}, u32[]{:S(2)}) collective-permute-start(bf16[32,384]{1,0:T(8,128)(2,1)S(1)} %get-tuple-element.57.refs_0_), channel_id=1, source_target_pairs={{0,16},{4,20},{8,24},{12,28},{16,0},{20,4},{24,8},{28,12},{32,48},... | collective-permute-start | bytes 73736 | tf_op jit(solution)/shard_map/ppermute | solution.py:155
  57.6 7.9 %collective-permute-start.12 = (bf16[32,384]{1,0:T(8,128)(2,1)S(1)}, bf16[32,384]{1,0:T(8,128)(2,1)S(1)}, u32[]{:S(2)}, u32[]{:S(2)}) collective-permute-start(bf16[32,384]{1,0:T(8,128)(2,1)S(1)} %get-tuple-element.57.refs_0_), channel_id=1, source_target_pairs={{0,32},{4,36},{8,40},{12,44},{16,48},{20,52},{24,56},{28,60},{32,0... | collective-permute-start | bytes 73736 | tf_op jit(solution)/shard_map/ppermute | solution.py:155
  59.4 6.2 %collective-permute-start.13 = (bf16[32,384]{1,0:T(8,128)(2,1)S(1)}, bf16[32,384]{1,0:T(8,128)(2,1)S(1)}, u32[]{:S(2)}, u32[]{:S(2)}) collective-permute-start(bf16[32,384]{1,0:T(8,128)(2,1)S(1)} %get-tuple-element.57.refs_0_), channel_id=1, source_target_pairs={{0,48},{4,52},{8,56},{12,60},{16,32},{20,36},{24,40},{28,44},{32,1... | collective-permute-start | bytes 73736 | tf_op jit(solution)/shard_map/ppermute | solution.py:155
  66.3 19.4 %copy-start.2 = (bf16[512,256]{1,0:T(8,128)(2,1)S(1)}, bf16[512,256]{1,0:T(8,128)(2,1)}, u32[]{:S(2)}) copy-start(bf16[512,256]{1,0:T(8,128)(2,1)} %out_grads.1) | copy-start | bytes 786436
  74.7 30.2 %collective-permute-start.25 = (bf16[128,4608]{1,0:T(8,128)(2,1)S(1)}, bf16[128,4608]{1,0:T(8,128)(2,1)S(1)}, u32[]{:S(2)}, u32[]{:S(2)}) collective-permute-start(bf16[128,4608]{1,0:T(8,128)(2,1)S(1)} %get-tuple-element.80), channel_id=1, source_target_pairs={{0,3},{1,2},{2,1},{3,0},{4,7},{5,6},{6,5},{7,4},{8,11},{9,10},{10,... | collective-permute-start | bytes 3538952 | tf_op jit(solution)/shard_map/ppermute | solution.py:33
  76.9 28.9 %collective-permute-start.26 = (bf16[128,4608]{1,0:T(8,128)(2,1)S(1)}, bf16[128,4608]{1,0:T(8,128)(2,1)S(1)}, u32[]{:S(2)}, u32[]{:S(2)}) collective-permute-start(bf16[128,4608]{1,0:T(8,128)(2,1)S(1)} %get-tuple-element.81), channel_id=1, source_target_pairs={{0,1},{1,0},{2,3},{3,2},{4,5},{5,4},{6,7},{7,6},{8,9},{9,8},{10,11... | collective-permute-start | bytes 3538952 | tf_op jit(solution)/shard_map/ppermute | solution.py:33
  76.9 4.6 %collective-permute-start.14 = (bf16[32,1536]{1,0:T(8,128)(2,1)S(1)}, bf16[32,1536]{1,0:T(8,128)(2,1)S(1)}, u32[]{:S(2)}, u32[]{:S(2)}) collective-permute-start(bf16[32,1536]{1,0:T(8,128)(2,1)S(1)} %shard_map.106.mine), channel_id=1, source_target_pairs={{0,8},{4,12},{8,0},{12,4},{16,24},{20,28},{24,16},{28,20},{32,40},... | collective-permute-start | bytes 294920 | tf_op jit(solution)/shard_map/ppermute | solution.py:159
  82.1 8.6 %collective-permute-start.15 = (bf16[32,3072]{1,0:T(8,128)(2,1)S(1)}, bf16[32,3072]{1,0:T(8,128)(2,1)S(1)}, u32[]{:S(2)}, u32[]{:S(2)}) collective-permute-start(bf16[32,3072]{1,0:T(8,128)(2,1)S(1)} %shard_map.108.refs_0_), channel_id=1, source_target_pairs={{0,64},{4,68},{8,72},{12,76},{16,80},{20,84},{24,88},{28,92},{32,9... | collective-permute-start | bytes 589832 | tf_op jit(solution)/shard_map/ppermute | solution.py:155
  82.6 9.1 %collective-permute-start.16 = (bf16[32,3072]{1,0:T(8,128)(2,1)S(1)}, bf16[32,3072]{1,0:T(8,128)(2,1)S(1)}, u32[]{:S(2)}, u32[]{:S(2)}) collective-permute-start(bf16[32,3072]{1,0:T(8,128)(2,1)S(1)} %shard_map.108.refs_0_), channel_id=1, source_target_pairs={{0,128},{4,132},{8,136},{12,140},{16,144},{20,148},{24,152},{28,15... | collective-permute-start | bytes 589832 | tf_op jit(solution)/shard_map/ppermute | solution.py:155
  85.2 7.9 %collective-permute-start.17 = (bf16[32,3072]{1,0:T(8,128)(2,1)S(1)}, bf16[32,3072]{1,0:T(8,128)(2,1)S(1)}, u32[]{:S(2)}, u32[]{:S(2)}) collective-permute-start(bf16[32,3072]{1,0:T(8,128)(2,1)S(1)} %shard_map.108.refs_0_), channel_id=1, source_target_pairs={{0,192},{4,196},{8,200},{12,204},{16,208},{20,212},{24,216},{28,22... | collective-permute-start | bytes 589832 | tf_op jit(solution)/shard_map/ppermute | solution.py:155
  86.3 2.0 %copy-start = (bf16[128,12288]{1,0:T(8,128)(2,1)S(1)}, bf16[128,12288]{1,0:T(8,128)(2,1)}, u32[]{:S(2)}) copy-start(bf16[128,12288]{1,0:T(8,128)(2,1)} %own.3) | copy-start | bytes 9437188
  90.7 2.9 %collective-permute-start.18 = (bf16[32,3072]{1,0:T(8,128)(2,1)S(1)}, bf16[32,3072]{1,0:T(8,128)(2,1)S(1)}, u32[]{:S(2)}, u32[]{:S(2)}) collective-permute-start(bf16[32,3072]{1,0:T(8,128)(2,1)S(1)} %shard_map.108.refs_0_), channel_id=1, source_target_pairs={{0,4},{4,0},{8,12},{12,8},{16,20},{20,16},{24,28},{28,24},{32,36},... | collective-permute-start | bytes 589832 | tf_op jit(solution)/shard_map/ppermute | solution.py:29
  93.0 2.2 %collective-permute-start.19 = (bf16[32,3072]{1,0:T(8,128)(2,1)S(1)}, bf16[32,3072]{1,0:T(8,128)(2,1)S(1)}, u32[]{:S(2)}, u32[]{:S(2)}) collective-permute-start(bf16[32,3072]{1,0:T(8,128)(2,1)S(1)} %collective-permute-done.15.refs_1_), channel_id=1, source_target_pairs={{0,4},{4,0},{8,12},{12,8},{16,20},{20,16},{24,28},{28,24},{32,36},... | collective-permute-start | bytes 589832 | tf_op jit(solution)/shard_map/ppermute | solution.py:29
  93.0 3.3 %collective-permute-start.20 = (bf16[32,3072]{1,0:T(8,128)(2,1)S(1)}, bf16[32,3072]{1,0:T(8,128)(2,1)S(1)}, u32[]{:S(2)}, u32[]{:S(2)}) collective-permute-start(bf16[32,3072]{1,0:T(8,128)(2,1)S(1)} %collective-permute-done.16.refs_2_), channel_id=1, source_target_pairs={{0,4},{4,0},{8,12},{12,8},{16,20},{20,16},{24,28},{28,24},{32,36},... | collective-permute-start | bytes 589832 | tf_op jit(solution)/shard_map/ppermute | solution.py:29
  93.7 1.4 %collective-permute-start.22 = (f32[3,32,192]{2,1,0:T(8,128)S(1)}, f32[3,32,192]{2,1,0:T(8,128)S(1)}, u32[]{:S(2)}, u32[]{:S(2)}) collective-permute-start(f32[3,32,192]{2,1,0:T(8,128)S(1)} %slice_select_fusion), channel_id=1, source_target_pairs={{0,4},{4,0},{8,12},{12,8},{16,20},{20,16},{24,28},{28,24},{32,36},... | collective-permute-start | bytes 221192 | tf_op jit(solution)/shard_map/ppermute | solution.py:29
  95.0 3.5 %collective-permute-start.21 = (bf16[32,3072]{1,0:T(8,128)(2,1)S(1)}, bf16[32,3072]{1,0:T(8,128)(2,1)S(1)}, u32[]{:S(2)}, u32[]{:S(2)}) collective-permute-start(bf16[32,3072]{1,0:T(8,128)(2,1)S(1)} %collective-permute-done.17.refs_3_), channel_id=1, source_target_pairs={{0,4},{4,0},{8,12},{12,8},{16,20},{20,16},{24,28},{28,24},{32,36},... | collective-permute-start | bytes 589832 | tf_op jit(solution)/shard_map/ppermute | solution.py:29
  95.2 16.8 %collective-permute-start.23 = (bf16[128,1536]{1,0:T(8,128)(2,1)S(1)}, bf16[128,1536]{1,0:T(8,128)(2,1)S(1)}, u32[]{:S(2)}, u32[]{:S(2)}) collective-permute-start(bf16[128,1536]{1,0:T(8,128)(2,1)S(1)} %get-tuple-element.78), channel_id=1, source_target_pairs={{0,3},{1,2},{2,1},{3,0},{4,7},{5,6},{6,5},{7,4},{8,11},{9,10},{10,... | collective-permute-start | bytes 1179656 | tf_op jit(solution)/shard_map/ppermute | solution.py:33
  96.4 15.7 %collective-permute-start.24 = (bf16[128,1536]{1,0:T(8,128)(2,1)S(1)}, bf16[128,1536]{1,0:T(8,128)(2,1)S(1)}, u32[]{:S(2)}, u32[]{:S(2)}) collective-permute-start(bf16[128,1536]{1,0:T(8,128)(2,1)S(1)} %get-tuple-element.79), channel_id=1, source_target_pairs={{0,1},{1,0},{2,3},{3,2},{4,5},{5,4},{6,7},{7,6},{8,9},{9,8},{10,11... | collective-permute-start | bytes 1179656 | tf_op jit(solution)/shard_map/ppermute | solution.py:33

commit v5 on v4

--- a/solution.py
+++ b/solution.py
@@ -83,7 +83,7 @@
         out_shape=jax.ShapeDtypeStruct((1, 256, D), jnp.bfloat16),
         input_output_aliases=aliases,
         cost_estimate=pl.CostEstimate(flops=2 * 256 * 512 * width, bytes_accessed=1536 * width, transcendentals=0),
-        compiler_params=pltpu.CompilerParams(vmem_limit_bytes=VMEM_LIMIT),
+        compiler_params=pltpu.CompilerParams(vmem_limit_bytes=32 * 1024 * 1024),
     )(*operands)
 
 
@@ -357,7 +357,7 @@
     state = [state[0], state[1], state[2]]
 
     weights, state[0], state[1], state[2], there = lax.optimization_barrier((weights, *state, there))
-    carry = product(PIECES[0][0], 2304, lhs, inputs, after, before, *opposites[:2], None, there)
+    carry = product(PIECES[0][0], 4608, lhs, inputs, after, before, *opposites[:2], None, there)
     carry = far_product(PIECES[1], lhs, summed, *opposites[2:], carry)
 
     return (weights, state[0], state[1], state[2], carry)

time: 114 us -> 114 us (level)
  transfers between devices with their start and end apart: 27 -> 27, of which waited for: 17 -> 18; matrix products, arithmetic and copies ran while one was open for 3% -> 3% of each run, Pallas kernels for 16% -> 15%
where the time goes in v5:
time: 114 us; the launch traced here: 113 us
  waiting for transfers between devices  49.7 us (44%)
  starting transfers between devices  35.7 us (31%)
  Pallas kernels  20.7 us (18%)
  local copies, waits for them, and re-layouts  3.6 us (3%)
  other arithmetic  2.82 us (2%)
    ppermute x12, waiting for transfers between devices, exchange(): lax.ppermute(array, 'dp', dp_swap(*move))  28 us
    ppermute x12, starting transfers between devices, exchange(): lax.ppermute(array, 'dp', dp_swap(*move))  22.4 us
    ppermute x6, waiting for transfers between devices, swap_x(): return lax.ppermute(array, 'mp', [(i, i ^ bits) for i in range(NX)])  12.6 us
    ppermute x6, starting transfers between devices, swap_x(): return lax.ppermute(array, 'mp', [(i, i ^ bits) for i in range(NX)])  8.45 us
    pallas_call x8, Pallas kernels, local(): pl.pallas_call(body, in_specs=[SMEM] + [VMEM] * len(operands), out_specs=...  7.67 us
    pallas_call x1, Pallas kernels, product(): pl.pallas_call(product_kernel, grid=(2 * steps,), in_specs=specs, out_spe...  5.61 us
    ppermute x2, waiting for transfers between devices, swap_z(): return lax.ppermute(array, 'dp', dp_swap(0, 1, 0))  5.49 us
    ppermute x2, starting transfers between devices, swap_z(): return lax.ppermute(array, 'dp', dp_swap(0, 1, 0))  3.92 us
  transfers between devices with their start and end apart: 27, of which 18 were waited for; matrix products, arithmetic and copies ran while one was open for 3% of the time, Pallas kernels for 15%

profile of v5, /device:TPU:8, one launch (start us, length us, event | category | flops | bytes accessed | tf_op | source)
XLA Modules:
  0.0 113.4 jit_solution(4305104965506786656)
XLA Ops:
  0.6 1.6 %collective-permute-start = (bf16[128,12288]{1,0:T(8,128)(2,1)}, bf16[128,12288]{1,0:T(8,128)(2,1)S(1)}, u32[]{:S(2)}, u32[]{:S(2)}) collective-permute-start(bf16[128,12288]{1,0:T(8,128)(2,1)} %own.3), channel_id=1, source_target_pairs={{0,1},{1,0},{2,3},{3,2},{4,5},{5,4},{6,7},{7,6},{8,9},{9,8},{10,11... | collective-permute-start | bytes 9437192 | tf_op jit(solution)/shard_map/ppermute | solution.py:33
  2.2 2.1 %collective-permute-start.1 = (bf16[128,12288]{1,0:T(8,128)(2,1)}, bf16[128,12288]{1,0:T(8,128)(2,1)}, u32[]{:S(2)}, u32[]{:S(2)}) collective-permute-start(bf16[128,12288]{1,0:T(8,128)(2,1)} %own.3), channel_id=1, source_target_pairs={{0,3},{1,2},{2,1},{3,0},{4,7},{5,6},{6,5},{7,4},{8,11},{9,10},{10,... | collective-permute-start | bytes 9437192 | tf_op jit(solution)/shard_map/ppermute | solution.py:33
  4.4 1.4 %copy-done.1 = bf16[1,64,12288]{2,1,0:T(8,128)(2,1)S(1)} copy-done((bf16[1,64,12288]{2,1,0:T(8,128)(2,1)S(1)}, bf16[1,64,12288]{2,1,0:T(8,128)(2,1)}, u32[]{:S(2)}) %copy-start.1) | copy-done | bytes 1572888
  6.6 2.3 %collective-permute-done.2.theirs = bf16[32,12288]{1,0:T(8,128)(2,1)S(1)} collective-permute-done((bf16[32,12288]{1,0:T(8,128)(2,1)S(1)}, bf16[32,12288]{1,0:T(8,128)(2,1)S(1)}, u32[]{:S(2)}, u32[]{:S(2)}) %collective-permute-start.2) | collective-permute-done | bytes 786464 | tf_op jit(solution)/shard_map/ppermute | solution.py:29
  8.9 1.6 %shard_map.102 = (f32[32,3072]{1,0:T(8,128)S(1)}, f32[32,3072]{1,0:T(8,128)}, f32[32,3072]{1,0:T(8,128)}, f32[32,3072]{1,0:T(8,128)}) custom-call(s32[6]{0:T(128)S(1)} %stack.39.place, bf16[32,12288]{1,0:T(8,128)(2,1)S(1)} %get-tuple-element.44.mine, bf16[32,12288]{1,0:T(8,128)(2,1)S(1)} %collective-permute-done.2.theirs), custom_call_target="tpu_custom_call" | custom-call | flops 1024 | bytes 1024 | tf_op jit(solution)/shard_map/pallas_call | solution.py:167
  10.9 2.6 %collective-permute-start.4 = (f32[32,3072]{1,0:T(8,128)}, f32[32,3072]{1,0:T(8,128)}, u32[]{:S(2)}, u32[]{:S(2)}) collective-permute-start(f32[32,3072]{1,0:T(8,128)} %get-tuple-element.48), channel_id=1, source_target_pairs={{0,128},{4,132},{8,136},{12,140},{16,144},{20,148},{24,152},{28,15... | collective-permute-start | bytes 1179656 | tf_op jit(solution)/shard_map/ppermute | solution.py:155
  16.2 6.5 %collective-permute-done.3.b = f32[32,3072]{1,0:T(8,128)} collective-permute-done((f32[32,3072]{1,0:T(8,128)}, f32[32,3072]{1,0:T(8,128)}, u32[]{:S(2)}, u32[]{:S(2)}) %collective-permute-start.3) | collective-permute-done | bytes 393248 | tf_op jit(solution)/shard_map/ppermute | solution.py:155
  22.7 8.7 %collective-permute-done.4.c = f32[32,3072]{1,0:T(8,128)} collective-permute-done((f32[32,3072]{1,0:T(8,128)}, f32[32,3072]{1,0:T(8,128)}, u32[]{:S(2)}, u32[]{:S(2)}) %collective-permute-start.4) | collective-permute-done | bytes 393248 | tf_op jit(solution)/shard_map/ppermute | solution.py:155
  31.5 1.4 %collective-permute-done.5.d = f32[32,3072]{1,0:T(8,128)} collective-permute-done((f32[32,3072]{1,0:T(8,128)}, f32[32,3072]{1,0:T(8,128)}, u32[]{:S(2)}, u32[]{:S(2)}) %collective-permute-start.5) | collective-permute-done | bytes 393248 | tf_op jit(solution)/shard_map/ppermute | solution.py:155
  34.2 2.0 %collective-permute-start.6 = (f32[32,1536]{1,0:T(8,128)S(1)}, f32[32,1536]{1,0:T(8,128)S(1)}, u32[]{:S(2)}, u32[]{:S(2)}) collective-permute-start(f32[32,1536]{1,0:T(8,128)S(1)} %get-tuple-element.51), channel_id=1, source_target_pairs={{0,8},{4,12},{8,0},{12,4},{16,24},{20,28},{24,16},{28,20},{32,40},... | collective-permute-start | bytes 589832 | tf_op jit(solution)/shard_map/ppermute | solution.py:159
  37.1 2.8 %collective-permute-done.6.b = f32[32,1536]{1,0:T(8,128)S(1)} collective-permute-done((f32[32,1536]{1,0:T(8,128)S(1)}, f32[32,1536]{1,0:T(8,128)S(1)}, u32[]{:S(2)}, u32[]{:S(2)}) %collective-permute-start.6) | collective-permute-done | bytes 196640 | tf_op jit(solution)/shard_map/ppermute | solution.py:159
  40.5 3.4 %collective-permute-start.7 = (f32[32,384]{1,0:T(8,128)S(1)}, f32[32,384]{1,0:T(8,128)S(1)}, u32[]{:S(2)}, u32[]{:S(2)}) collective-permute-start(f32[32,384]{1,0:T(8,128)S(1)} %get-tuple-element.53), channel_id=1, source_target_pairs={{0,16},{4,20},{8,24},{12,28},{16,0},{20,4},{24,8},{28,12},{32,48},... | collective-permute-start | bytes 147464 | tf_op jit(solution)/shard_map/ppermute | solution.py:155
  43.9 5.4 %collective-permute-start.8 = (f32[32,384]{1,0:T(8,128)S(1)}, f32[32,384]{1,0:T(8,128)S(1)}, u32[]{:S(2)}, u32[]{:S(2)}) collective-permute-start(f32[32,384]{1,0:T(8,128)S(1)} %get-tuple-element.54), channel_id=1, source_target_pairs={{0,32},{4,36},{8,40},{12,44},{16,48},{20,52},{24,56},{28,60},{32,0... | collective-permute-start | bytes 147464 | tf_op jit(solution)/shard_map/ppermute | solution.py:155
  49.4 3.4 %collective-permute-done.8.c = f32[32,384]{1,0:T(8,128)S(1)} collective-permute-done((f32[32,384]{1,0:T(8,128)S(1)}, f32[32,384]{1,0:T(8,128)S(1)}, u32[]{:S(2)}, u32[]{:S(2)}) %collective-permute-start.8) | collective-permute-done | bytes 49184 | tf_op jit(solution)/shard_map/ppermute | solution.py:155
  52.8 2.7 %collective-permute-done.9.d = f32[32,384]{1,0:T(8,128)S(1)} collective-permute-done((f32[32,384]{1,0:T(8,128)S(1)}, f32[32,384]{1,0:T(8,128)S(1)}, u32[]{:S(2)}, u32[]{:S(2)}) %collective-permute-start.9) | collective-permute-done | bytes 49184 | tf_op jit(solution)/shard_map/ppermute | solution.py:155
  56.1 1.5 %collective-permute-start.11 = (bf16[32,384]{1,0:T(8,128)(2,1)S(1)}, bf16[32,384]{1,0:T(8,128)(2,1)S(1)}, u32[]{:S(2)}, u32[]{:S(2)}) collective-permute-start(bf16[32,384]{1,0:T(8,128)(2,1)S(1)} %get-tuple-element.57.refs_0_), channel_id=1, source_target_pairs={{0,16},{4,20},{8,24},{12,28},{16,0},{20,4},{24,8},{28,12},{32,48},... | collective-permute-start | bytes 73736 | tf_op jit(solution)/shard_map/ppermute | solution.py:155
  57.6 1.8 %collective-permute-start.12 = (bf16[32,384]{1,0:T(8,128)(2,1)S(1)}, bf16[32,384]{1,0:T(8,128)(2,1)S(1)}, u32[]{:S(2)}, u32[]{:S(2)}) collective-permute-start(bf16[32,384]{1,0:T(8,128)(2,1)S(1)} %get-tuple-element.57.refs_0_), channel_id=1, source_target_pairs={{0,32},{4,36},{8,40},{12,44},{16,48},{20,52},{24,56},{28,60},{32,0... | collective-permute-start | bytes 73736 | tf_op jit(solution)/shard_map/ppermute | solution.py:155
  59.4 3.3 %collective-permute-start.13 = (bf16[32,384]{1,0:T(8,128)(2,1)S(1)}, bf16[32,384]{1,0:T(8,128)(2,1)S(1)}, u32[]{:S(2)}, u32[]{:S(2)}) collective-permute-start(bf16[32,384]{1,0:T(8,128)(2,1)S(1)} %get-tuple-element.57.refs_0_), channel_id=1, source_target_pairs={{0,48},{4,52},{8,56},{12,60},{16,32},{20,36},{24,40},{28,44},{32,1... | collective-permute-start | bytes 73736 | tf_op jit(solution)/shard_map/ppermute | solution.py:155
  62.7 2.8 %collective-permute-done.12.refs_2_ = bf16[32,384]{1,0:T(8,128)(2,1)S(1)} collective-permute-done((bf16[32,384]{1,0:T(8,128)(2,1)S(1)}, bf16[32,384]{1,0:T(8,128)(2,1)S(1)}, u32[]{:S(2)}, u32[]{:S(2)}) %collective-permute-start.12) | collective-permute-done | bytes 24608 | tf_op jit(solution)/shard_map/ppermute | solution.py:155
  66.3 4.5 %collective-permute-done.before = bf16[128,12288]{1,0:T(8,128)(2,1)S(1)} collective-permute-done((bf16[128,12288]{1,0:T(8,128)(2,1)}, bf16[128,12288]{1,0:T(8,128)(2,1)S(1)}, u32[]{:S(2)}, u32[]{:S(2)}) %collective-permute-start) | collective-permute-done | bytes 3145760 | tf_op jit(solution)/shard_map/ppermute | solution.py:33
  70.8 2.5 %collective-permute-done.1.after = bf16[128,12288]{1,0:T(8,128)(2,1)} collective-permute-done((bf16[128,12288]{1,0:T(8,128)(2,1)}, bf16[128,12288]{1,0:T(8,128)(2,1)}, u32[]{:S(2)}, u32[]{:S(2)}) %collective-permute-start.1) | collective-permute-done | bytes 3145760 | tf_op jit(solution)/shard_map/ppermute | solution.py:33
  73.3 1.4 %shard_map.107 = (bf16[128,4608]{1,0:T(8,128)(2,1)S(1)}, bf16[128,4608]{1,0:T(8,128)(2,1)S(1)}) custom-call(bf16[128,12288]{1,0:T(8,128)(2,1)S(1)} %collective-permute-done.before, bf16[128,12288]{1,0:T(8,128)(2,1)} %collective-permute-done.1.after), custom_call_target="tpu_custom_call" | custom-call | flops 1024 | bytes 1024 | tf_op jit(solution)/shard_map/pallas_call | solution.py:201
  74.7 2.2 %collective-permute-start.25 = (bf16[128,4608]{1,0:T(8,128)(2,1)S(1)}, bf16[128,4608]{1,0:T(8,128)(2,1)S(1)}, u32[]{:S(2)}, u32[]{:S(2)}) collective-permute-start(bf16[128,4608]{1,0:T(8,128)(2,1)S(1)} %get-tuple-element.80), channel_id=1, source_target_pairs={{0,3},{1,2},{2,1},{3,0},{4,7},{5,6},{6,5},{7,4},{8,11},{9,10},{10,... | collective-permute-start | bytes 3538952 | tf_op jit(solution)/shard_map/ppermute | solution.py:33
  76.9 1.9 %collective-permute-start.14 = (bf16[32,1536]{1,0:T(8,128)(2,1)S(1)}, bf16[32,1536]{1,0:T(8,128)(2,1)S(1)}, u32[]{:S(2)}, u32[]{:S(2)}) collective-permute-start(bf16[32,1536]{1,0:T(8,128)(2,1)S(1)} %shard_map.106.mine), channel_id=1, source_target_pairs={{0,8},{4,12},{8,0},{12,4},{16,24},{20,28},{24,16},{28,20},{32,40},... | collective-permute-start | bytes 294920 | tf_op jit(solution)/shard_map/ppermute | solution.py:159
  78.8 2.7 %collective-permute-done.14.other = bf16[32,1536]{1,0:T(8,128)(2,1)S(1)} collective-permute-done((bf16[32,1536]{1,0:T(8,128)(2,1)S(1)}, bf16[32,1536]{1,0:T(8,128)(2,1)S(1)}, u32[]{:S(2)}, u32[]{:S(2)}) %collective-permute-start.14) | collective-permute-done | bytes 98336 | tf_op jit(solution)/shard_map/ppermute | solution.py:159
  82.6 2.6 %collective-permute-start.16 = (bf16[32,3072]{1,0:T(8,128)(2,1)S(1)}, bf16[32,3072]{1,0:T(8,128)(2,1)S(1)}, u32[]{:S(2)}, u32[]{:S(2)}) collective-permute-start(bf16[32,3072]{1,0:T(8,128)(2,1)S(1)} %shard_map.108.refs_0_), channel_id=1, source_target_pairs={{0,128},{4,132},{8,136},{12,140},{16,144},{20,148},{24,152},{28,15... | collective-permute-start | bytes 589832 | tf_op jit(solution)/shard_map/ppermute | solution.py:155
  88.3 2.4 %shard_map.111 = (f32[256,3072]{1,0:T(8,128)S(1)}, f32[8,128]{1,0:T(8,128)S(1)}) custom-call(bf16[256,512]{1,0:T(8,128)(2,1)S(1)} %shard_map.110.lhs, bf16[128,12288]{1,0:T(8,128)(2,1)S(1)} %copy-done, bf16[128,12288]{1,0:T(8,128)(2,1)} %collective-permute-done.1.after, bf16[128,12288]{1,0:T(8,128)(2,1)S(1)} %collective-permute-done.before), custom_call_target="tpu_custom_call" | custom-call | tf_op jit(solution)/shard_map/pallas_call | solution.py:99
  96.4 1.4 %collective-permute-start.24 = (bf16[128,1536]{1,0:T(8,128)(2,1)S(1)}, bf16[128,1536]{1,0:T(8,128)(2,1)S(1)}, u32[]{:S(2)}, u32[]{:S(2)}) collective-permute-start(bf16[128,1536]{1,0:T(8,128)(2,1)S(1)} %get-tuple-element.79), channel_id=1, source_target_pairs={{0,1},{1,0},{2,3},{3,2},{4,5},{5,4},{6,7},{7,6},{8,9},{9,8},{10,11... | collective-permute-start | bytes 1179656 | tf_op jit(solution)/shard_map/ppermute | solution.py:33
  98.6 1.8 %shard_map.112 = bf16[64,12288]{1,0:T(8,128)(2,1)} custom-call(s32[6]{0:T(128)S(1)} %stack.39.place, bf16[32,3072]{1,0:T(8,128)(2,1)S(1)} %shard_map.108.refs_0_, bf16[32,3072]{1,0:T(8,128)(2,1)S(1)} %collective-permute-done.15.refs_1_, bf16[32,3072]{1,0:T(8,128)(2,1)S(1)} %collective-permute-done.16.refs_2_, ...), custom_call_target="tpu_custom_call" | custom-call | flops 1024 | bytes 1024 | tf_op jit(solution)/shard_map/pallas_call | solution.py:167
  100.4 4.5 %collective-permute-done.25.first = bf16[128,4608]{1,0:T(8,128)(2,1)S(1)} collective-permute-done((bf16[128,4608]{1,0:T(8,128)(2,1)S(1)}, bf16[128,4608]{1,0:T(8,128)(2,1)S(1)}, u32[]{:S(2)}, u32[]{:S(2)}) %collective-permute-start.25) | collective-permute-done | bytes 1179680 | tf_op jit(solution)/shard_map/ppermute | solution.py:33
  105.8 5.6 %shard_map.113.carry = bf16[1,256,12288]{2,1,0:T(8,128)(2,1)} custom-call(bf16[256,512]{1,0:T(8,128)(2,1)S(1)} %shard_map.110.lhs, bf16[128,12288]{1,0:T(8,128)(2,1)S(1)} %copy-done, bf16[128,12288]{1,0:T(8,128)(2,1)} %collective-permute-done.1.after, bf16[128,12288]{1,0:T(8,128)(2,1)S(1)} %collective-permute-done.before, ...), custom_call_target="tpu_custom_call" | custom-call | flops 2415919104 | bytes 14155776 | tf_op jit(solution)/shard_map/pallas_call | solution.py:78
  111.5 1.8 %shard_map.114 = bf16[1,256,12288]{2,1,0:T(8,128)(2,1)} custom-call(bf16[256,512]{1,0:T(8,128)(2,1)S(1)} %shard_map.110.lhs, f32[256,3072]{1,0:T(8,128)S(1)} %get-tuple-element.77.summed, bf16[128,1536]{1,0:T(8,128)(2,1)S(1)} %collective-permute-done.23.first, bf16[128,1536]{1,0:T(8,128)(2,1)S(1)} %collective-permute-done.24.second, ...), custom_call_target="tpu_custom_call", output_to_operand_aliasing={{}: (4, {})} | custom-call | flops 201326592 | bytes 3145728 | tf_op jit(solution)/shard_map/pallas_call | solution.py:128
  (52 shorter events, 19.9 us)
Async XLA Ops:
  0.6 70.1 %collective-permute-start = (bf16[128,12288]{1,0:T(8,128)(2,1)}, bf16[128,12288]{1,0:T(8,128)(2,1)S(1)}, u32[]{:S(2)}, u32[]{:S(2)}) collective-permute-start(bf16[128,12288]{1,0:T(8,128)(2,1)} %own.3), channel_id=1, source_target_pairs={{0,1},{1,0},{2,3},{3,2},{4,5},{5,4},{6,7},{7,6},{8,9},{9,8},{10,11... | collective-permute-start | bytes 9437192 | tf_op jit(solution)/shard_map/ppermute | solution.py:33
  2.2 71.1 %collective-permute-start.1 = (bf16[128,12288]{1,0:T(8,128)(2,1)}, bf16[128,12288]{1,0:T(8,128)(2,1)}, u32[]{:S(2)}, u32[]{:S(2)}) collective-permute-start(bf16[128,12288]{1,0:T(8,128)(2,1)} %own.3), channel_id=1, source_target_pairs={{0,3},{1,2},{2,1},{3,0},{4,7},{5,6},{6,5},{7,4},{8,11},{9,10},{10,... | collective-permute-start | bytes 9437192 | tf_op jit(solution)/shard_map/ppermute | solution.py:33
  4.4 1.4 %copy-start.1 = (bf16[1,64,12288]{2,1,0:T(8,128)(2,1)S(1)}, bf16[1,64,12288]{2,1,0:T(8,128)(2,1)}, u32[]{:S(2)}) copy-start(bf16[1,64,12288]{2,1,0:T(8,128)(2,1)} %grads.1) | copy-start | bytes 4718596
  6.5 2.4 %collective-permute-start.2 = (bf16[32,12288]{1,0:T(8,128)(2,1)S(1)}, bf16[32,12288]{1,0:T(8,128)(2,1)S(1)}, u32[]{:S(2)}, u32[]{:S(2)}) collective-permute-start(bf16[32,12288]{1,0:T(8,128)(2,1)S(1)} %get-tuple-element.45), channel_id=1, source_target_pairs={{0,4},{4,0},{8,12},{12,8},{16,20},{20,16},{24,28},{28,24},{32,36},... | collective-permute-start | bytes 2359304 | tf_op jit(solution)/shard_map/ppermute | solution.py:29
  10.5 12.3 %collective-permute-start.3 = (f32[32,3072]{1,0:T(8,128)}, f32[32,3072]{1,0:T(8,128)}, u32[]{:S(2)}, u32[]{:S(2)}) collective-permute-start(f32[32,3072]{1,0:T(8,128)} %get-tuple-element.47), channel_id=1, source_target_pairs={{0,64},{4,68},{8,72},{12,76},{16,80},{20,84},{24,88},{28,92},{32,9... | collective-permute-start | bytes 1179656 | tf_op jit(solution)/shard_map/ppermute | solution.py:155
  10.9 20.6 %collective-permute-start.4 = (f32[32,3072]{1,0:T(8,128)}, f32[32,3072]{1,0:T(8,128)}, u32[]{:S(2)}, u32[]{:S(2)}) collective-permute-start(f32[32,3072]{1,0:T(8,128)} %get-tuple-element.48), channel_id=1, source_target_pairs={{0,128},{4,132},{8,136},{12,140},{16,144},{20,148},{24,152},{28,15... | collective-permute-start | bytes 1179656 | tf_op jit(solution)/shard_map/ppermute | solution.py:155
  13.5 19.3 %collective-permute-start.5 = (f32[32,3072]{1,0:T(8,128)}, f32[32,3072]{1,0:T(8,128)}, u32[]{:S(2)}, u32[]{:S(2)}) collective-permute-start(f32[32,3072]{1,0:T(8,128)} %get-tuple-element.49), channel_id=1, source_target_pairs={{0,192},{4,196},{8,200},{12,204},{16,208},{20,212},{24,216},{28,22... | collective-permute-start | bytes 1179656 | tf_op jit(solution)/shard_map/ppermute | solution.py:155
  14.9 0.7 copy-start.3
  22.7 13.4 %collective-permute-start.10 = (f32[3,32,192]{2,1,0:T(8,128)}, f32[3,32,192]{2,1,0:T(8,128)}, u32[]{:S(2)}, u32[]{:S(2)}) collective-permute-start(f32[3,32,192]{2,1,0:T(8,128)} %constant_dynamic-slice_fusion), channel_id=1, source_target_pairs={{0,4},{4,0},{8,12},{12,8},{16,20},{20,16},{24,28},{28,24},{32,36},... | collective-permute-start | bytes 221192 | tf_op jit(solution)/shard_map/ppermute | solution.py:29
  34.2 5.8 %collective-permute-start.6 = (f32[32,1536]{1,0:T(8,128)S(1)}, f32[32,1536]{1,0:T(8,128)S(1)}, u32[]{:S(2)}, u32[]{:S(2)}) collective-permute-start(f32[32,1536]{1,0:T(8,128)S(1)} %get-tuple-element.51), channel_id=1, source_target_pairs={{0,8},{4,12},{8,0},{12,4},{16,24},{20,28},{24,16},{28,20},{32,40},... | collective-permute-start | bytes 589832 | tf_op jit(solution)/shard_map/ppermute | solution.py:159
  40.5 8.8 %collective-permute-start.7 = (f32[32,384]{1,0:T(8,128)S(1)}, f32[32,384]{1,0:T(8,128)S(1)}, u32[]{:S(2)}, u32[]{:S(2)}) collective-permute-start(f32[32,384]{1,0:T(8,128)S(1)} %get-tuple-element.53), channel_id=1, source_target_pairs={{0,16},{4,20},{8,24},{12,28},{16,0},{20,4},{24,8},{28,12},{32,48},... | collective-permute-start | bytes 147464 | tf_op jit(solution)/shard_map/ppermute | solution.py:155
  43.9 8.9 %collective-permute-start.8 = (f32[32,384]{1,0:T(8,128)S(1)}, f32[32,384]{1,0:T(8,128)S(1)}, u32[]{:S(2)}, u32[]{:S(2)}) collective-permute-start(f32[32,384]{1,0:T(8,128)S(1)} %get-tuple-element.54), channel_id=1, source_target_pairs={{0,32},{4,36},{8,40},{12,44},{16,48},{20,52},{24,56},{28,60},{32,0... | collective-permute-start | bytes 147464 | tf_op jit(solution)/shard_map/ppermute | solution.py:155
  49.3 6.3 %collective-permute-start.9 = (f32[32,384]{1,0:T(8,128)S(1)}, f32[32,384]{1,0:T(8,128)S(1)}, u32[]{:S(2)}, u32[]{:S(2)}) collective-permute-start(f32[32,384]{1,0:T(8,128)S(1)} %get-tuple-element.55), channel_id=1, source_target_pairs={{0,48},{4,52},{8,56},{12,60},{16,32},{20,36},{24,40},{28,44},{32,1... | collective-permute-start | bytes 147464 | tf_op jit(solution)/shard_map/ppermute | solution.py:155
  56.1 6.6 %collective-permute-start.11 = (bf16[32,384]{1,0:T(8,128)(2,1)S(1)}, bf16[32,384]{1,0:T(8,128)(2,1)S(1)}, u32[]{:S(2)}, u32[]{:S(2)}) collective-permute-start(bf16[32,384]{1,0:T(8,128)(2,1)S(1)} %get-tuple-element.57.refs_0_), channel_id=1, source_target_pairs={{0,16},{4,20},{8,24},{12,28},{16,0},{20,4},{24,8},{28,12},{32,48},... | collective-permute-start | bytes 73736 | tf_op jit(solution)/shard_map/ppermute | solution.py:155
  57.6 7.9 %collective-permute-start.12 = (bf16[32,384]{1,0:T(8,128)(2,1)S(1)}, bf16[32,384]{1,0:T(8,128)(2,1)S(1)}, u32[]{:S(2)}, u32[]{:S(2)}) collective-permute-start(bf16[32,384]{1,0:T(8,128)(2,1)S(1)} %get-tuple-element.57.refs_0_), channel_id=1, source_target_pairs={{0,32},{4,36},{8,40},{12,44},{16,48},{20,52},{24,56},{28,60},{32,0... | collective-permute-start | bytes 73736 | tf_op jit(solution)/shard_map/ppermute | solution.py:155
  59.4 6.2 %collective-permute-start.13 = (bf16[32,384]{1,0:T(8,128)(2,1)S(1)}, bf16[32,384]{1,0:T(8,128)(2,1)S(1)}, u32[]{:S(2)}, u32[]{:S(2)}) collective-permute-start(bf16[32,384]{1,0:T(8,128)(2,1)S(1)} %get-tuple-element.57.refs_0_), channel_id=1, source_target_pairs={{0,48},{4,52},{8,56},{12,60},{16,32},{20,36},{24,40},{28,44},{32,1... | collective-permute-start | bytes 73736 | tf_op jit(solution)/shard_map/ppermute | solution.py:155
  66.3 19.4 %copy-start.2 = (bf16[512,256]{1,0:T(8,128)(2,1)S(1)}, bf16[512,256]{1,0:T(8,128)(2,1)}, u32[]{:S(2)}) copy-start(bf16[512,256]{1,0:T(8,128)(2,1)} %out_grads.1) | copy-start | bytes 786436
  74.7 30.2 %collective-permute-start.25 = (bf16[128,4608]{1,0:T(8,128)(2,1)S(1)}, bf16[128,4608]{1,0:T(8,128)(2,1)S(1)}, u32[]{:S(2)}, u32[]{:S(2)}) collective-permute-start(bf16[128,4608]{1,0:T(8,128)(2,1)S(1)} %get-tuple-element.80), channel_id=1, source_target_pairs={{0,3},{1,2},{2,1},{3,0},{4,7},{5,6},{6,5},{7,4},{8,11},{9,10},{10,... | collective-permute-start | bytes 3538952 | tf_op jit(solution)/shard_map/ppermute | solution.py:33
  76.9 28.9 %collective-permute-start.26 = (bf16[128,4608]{1,0:T(8,128)(2,1)S(1)}, bf16[128,4608]{1,0:T(8,128)(2,1)S(1)}, u32[]{:S(2)}, u32[]{:S(2)}) collective-permute-start(bf16[128,4608]{1,0:T(8,128)(2,1)S(1)} %get-tuple-element.81), channel_id=1, source_target_pairs={{0,1},{1,0},{2,3},{3,2},{4,5},{5,4},{6,7},{7,6},{8,9},{9,8},{10,11... | collective-permute-start | bytes 3538952 | tf_op jit(solution)/shard_map/ppermute | solution.py:33
  76.9 4.6 %collective-permute-start.14 = (bf16[32,1536]{1,0:T(8,128)(2,1)S(1)}, bf16[32,1536]{1,0:T(8,128)(2,1)S(1)}, u32[]{:S(2)}, u32[]{:S(2)}) collective-permute-start(bf16[32,1536]{1,0:T(8,128)(2,1)S(1)} %shard_map.106.mine), channel_id=1, source_target_pairs={{0,8},{4,12},{8,0},{12,4},{16,24},{20,28},{24,16},{28,20},{32,40},... | collective-permute-start | bytes 294920 | tf_op jit(solution)/shard_map/ppermute | solution.py:159
  82.1 8.6 %collective-permute-start.15 = (bf16[32,3072]{1,0:T(8,128)(2,1)S(1)}, bf16[32,3072]{1,0:T(8,128)(2,1)S(1)}, u32[]{:S(2)}, u32[]{:S(2)}) collective-permute-start(bf16[32,3072]{1,0:T(8,128)(2,1)S(1)} %shard_map.108.refs_0_), channel_id=1, source_target_pairs={{0,64},{4,68},{8,72},{12,76},{16,80},{20,84},{24,88},{28,92},{32,9... | collective-permute-start | bytes 589832 | tf_op jit(solution)/shard_map/ppermute | solution.py:155
  82.6 9.1 %collective-permute-start.16 = (bf16[32,3072]{1,0:T(8,128)(2,1)S(1)}, bf16[32,3072]{1,0:T(8,128)(2,1)S(1)}, u32[]{:S(2)}, u32[]{:S(2)}) collective-permute-start(bf16[32,3072]{1,0:T(8,128)(2,1)S(1)} %shard_map.108.refs_0_), channel_id=1, source_target_pairs={{0,128},{4,132},{8,136},{12,140},{16,144},{20,148},{24,152},{28,15... | collective-permute-start | bytes 589832 | tf_op jit(solution)/shard_map/ppermute | solution.py:155
  85.2 7.9 %collective-permute-start.17 = (bf16[32,3072]{1,0:T(8,128)(2,1)S(1)}, bf16[32,3072]{1,0:T(8,128)(2,1)S(1)}, u32[]{:S(2)}, u32[]{:S(2)}) collective-permute-start(bf16[32,3072]{1,0:T(8,128)(2,1)S(1)} %shard_map.108.refs_0_), channel_id=1, source_target_pairs={{0,192},{4,196},{8,200},{12,204},{16,208},{20,212},{24,216},{28,22... | collective-permute-start | bytes 589832 | tf_op jit(solution)/shard_map/ppermute | solution.py:155
  86.3 2.0 %copy-start = (bf16[128,12288]{1,0:T(8,128)(2,1)S(1)}, bf16[128,12288]{1,0:T(8,128)(2,1)}, u32[]{:S(2)}) copy-start(bf16[128,12288]{1,0:T(8,128)(2,1)} %own.3) | copy-start | bytes 9437188
  90.7 2.9 %collective-permute-start.18 = (bf16[32,3072]{1,0:T(8,128)(2,1)S(1)}, bf16[32,3072]{1,0:T(8,128)(2,1)S(1)}, u32[]{:S(2)}, u32[]{:S(2)}) collective-permute-start(bf16[32,3072]{1,0:T(8,128)(2,1)S(1)} %shard_map.108.refs_0_), channel_id=1, source_target_pairs={{0,4},{4,0},{8,12},{12,8},{16,20},{20,16},{24,28},{28,24},{32,36},... | collective-permute-start | bytes 589832 | tf_op jit(solution)/shard_map/ppermute | solution.py:29
  93.0 2.2 %collective-permute-start.19 = (bf16[32,3072]{1,0:T(8,128)(2,1)S(1)}, bf16[32,3072]{1,0:T(8,128)(2,1)S(1)}, u32[]{:S(2)}, u32[]{:S(2)}) collective-permute-start(bf16[32,3072]{1,0:T(8,128)(2,1)S(1)} %collective-permute-done.15.refs_1_), channel_id=1, source_target_pairs={{0,4},{4,0},{8,12},{12,8},{16,20},{20,16},{24,28},{28,24},{32,36},... | collective-permute-start | bytes 589832 | tf_op jit(solution)/shard_map/ppermute | solution.py:29
  93.0 3.3 %collective-permute-start.20 = (bf16[32,3072]{1,0:T(8,128)(2,1)S(1)}, bf16[32,3072]{1,0:T(8,128)(2,1)S(1)}, u32[]{:S(2)}, u32[]{:S(2)}) collective-permute-start(bf16[32,3072]{1,0:T(8,128)(2,1)S(1)} %collective-permute-done.16.refs_2_), channel_id=1, source_target_pairs={{0,4},{4,0},{8,12},{12,8},{16,20},{20,16},{24,28},{28,24},{32,36},... | collective-permute-start | bytes 589832 | tf_op jit(solution)/shard_map/ppermute | solution.py:29
  93.7 1.4 %collective-permute-start.22 = (f32[3,32,192]{2,1,0:T(8,128)S(1)}, f32[3,32,192]{2,1,0:T(8,128)S(1)}, u32[]{:S(2)}, u32[]{:S(2)}) collective-permute-start(f32[3,32,192]{2,1,0:T(8,128)S(1)} %slice_select_fusion), channel_id=1, source_target_pairs={{0,4},{4,0},{8,12},{12,8},{16,20},{20,16},{24,28},{28,24},{32,36},... | collective-permute-start | bytes 221192 | tf_op jit(solution)/shard_map/ppermute | solution.py:29
  95.0 3.5 %collective-permute-start.21 = (bf16[32,3072]{1,0:T(8,128)(2,1)S(1)}, bf16[32,3072]{1,0:T(8,128)(2,1)S(1)}, u32[]{:S(2)}, u32[]{:S(2)}) collective-permute-start(bf16[32,3072]{1,0:T(8,128)(2,1)S(1)} %collective-permute-done.17.refs_3_), channel_id=1, source_target_pairs={{0,4},{4,0},{8,12},{12,8},{16,20},{20,16},{24,28},{28,24},{32,36},... | collective-permute-start | bytes 589832 | tf_op jit(solution)/shard_map/ppermute | solution.py:29
  95.2 16.2 %collective-permute-start.23 = (bf16[128,1536]{1,0:T(8,128)(2,1)S(1)}, bf16[128,1536]{1,0:T(8,128)(2,1)S(1)}, u32[]{:S(2)}, u32[]{:S(2)}) collective-permute-start(bf16[128,1536]{1,0:T(8,128)(2,1)S(1)} %get-tuple-element.78), channel_id=1, source_target_pairs={{0,3},{1,2},{2,1},{3,0},{4,7},{5,6},{6,5},{7,4},{8,11},{9,10},{10,... | collective-permute-start | bytes 1179656 | tf_op jit(solution)/shard_map/ppermute | solution.py:33
  96.4 15.2 %collective-permute-start.24 = (bf16[128,1536]{1,0:T(8,128)(2,1)S(1)}, bf16[128,1536]{1,0:T(8,128)(2,1)S(1)}, u32[]{:S(2)}, u32[]{:S(2)}) collective-permute-start(bf16[128,1536]{1,0:T(8,128)(2,1)S(1)} %get-tuple-element.79), channel_id=1, source_target_pairs={{0,1},{1,0},{2,3},{3,2},{4,5},{5,4},{6,7},{7,6},{8,9},{9,8},{10,11... | collective-permute-start | bytes 1179656 | tf_op jit(solution)/shard_map/ppermute | solution.py:33
